TPU v7x, 256 devices: a whole 4x4x8 slice. The times are simulated.
256 devices in a mesh: slab: 8 (over y, core), row: 32 (over x, z).
Axes of the slice: x: 4, y: 4, z: 8, core: 2. Of those that a mesh axis runs over, the one named last changes fastest.
Arguments:
- a_blocks: bfloat16 [16384, 64, 448], P(('slab', 'row')), may hold values from -0.25 to 0.25
- p_blocks: bfloat16 [16384, 64, 256], P(('slab', 'row')), may hold values from -1.5 to 1.5
- a_cols: int32 [16384, 7], P(('slab', 'row')), may hold values from 0 to 95
- p_slots: int32 [16384, 4], P(('slab', 'row')), may hold values from 0 to 63, as said below
- touched: int32 [256, 32, 2], P(('slab', 'row')), may hold values from -1 to 3, as said below
- touch_cols: int32 [256, 32, 2, 8], P(('slab', 'row')), may hold values from -1 to 1023, as said below
- halo_rows: int32 [256, 4, 8], P(('slab', 'row')), may hold values from 0 to 63, as said below
Outputs:
- coarse_ops: float32 [1024, 64, 512], P(('slab', 'row'))
Inputs may be any that keep to these rules, and one draw needn't show every extreme that they name: touched[d, p, :] lists distinct row indices among the 4 coarse rows owned by device p of d's slab, used entries first, -1 in unused slots; in every slab two owners have all 2 slots used by every device of the slab. `p_slots`: each fine row names 4 distinct used slots of its own device's touched table. touch_cols[d, p, c, :] holds 8 distinct global coarse row ids, the same list on every device naming that coarse row; -1 in unused slots. halo_rows[d, j, :] holds 8 distinct local fine row indices of device d.
All inputs are finite; a program needn't handle non-finite values.
Results may differ from a plain program's by a relative error of at most 0.013.
Values may be sent and summed in bfloat16 or wider, within the bound.
A program may use at most 128 MiB of HBM per device.

v0:
```python
import math

import jax
import jax.numpy as jnp
from jax import lax
from jax.sharding import PartitionSpec as P

NC = 4


def with_halo(cells, sides, width):
    for axis, dim in sides:
        count = lax.axis_size(axis)
        ends = count - 1
        head = lax.slice_in_dim(cells, 0, width, axis=dim)
        tail = lax.slice_in_dim(cells, cells.shape[dim] - width, cells.shape[dim], axis=dim)
        cells = jnp.concatenate(
            [
                lax.ppermute(tail, axis, [(i, (i + 1) % count) for i in range(ends)]),
                cells,
                lax.ppermute(head, axis, [((i + 1) % count, i) for i in range(ends)]),
            ],
            axis=dim,
        )
    return cells


def per_device(a_blocks, p_blocks, a_cols, p_slots, touched, touch_cols, halo_rows):
    rows, width, span = a_blocks.shape
    kp = p_blocks.shape[2] // width
    ka = span // width
    nrow = lax.axis_size("row")
    slab_at = lax.axis_index("slab")
    owned = NC
    cap = touched.shape[2]
    slots = touched.shape[1] * cap
    table = touched.reshape(slots)
    patterns = touch_cols.reshape(slots, touch_cols.shape[3])
    kc = patterns.shape[1]
    local_ids = table[p_slots]
    coarse_ids = (slab_at * nrow + p_slots // cap) * owned + local_ids
    lists = halo_rows[0]
    depth = lists.shape[1]
    sent_blocks = p_blocks[lists]
    sent_ids = coarse_ids[lists]
    slab_in = (
        with_halo(jnp.concatenate([sent_blocks[0], sent_blocks[1]], 0), (("slab", 0),), depth),
        with_halo(jnp.concatenate([sent_ids[0], sent_ids[1]], 0), (("slab", 0),), depth),
    )
    row_in = (
        with_halo(jnp.concatenate([sent_blocks[2], sent_blocks[3]], 0), (("row", 0),), depth),
        with_halo(jnp.concatenate([sent_ids[2], sent_ids[3]], 0), (("row", 0),), depth),
    )
    ext_blocks = jnp.concatenate(
        [
            p_blocks,
            slab_in[0][:depth],
            slab_in[0][3 * depth :],
            row_in[0][:depth],
            row_in[0][3 * depth :],
        ],
        0,
    )
    ext_ids = jnp.concatenate(
        [
            coarse_ids,
            slab_in[1][:depth],
            slab_in[1][3 * depth :],
            row_in[1][:depth],
            row_in[1][3 * depth :],
        ],
        0,
    )
    step = math.gcd(rows, 16)
    count = rows // step
    slot_range = jnp.arange(slots, dtype=jnp.int32)

    def advance(total, index):
        start = index * step
        cols_part = lax.dynamic_slice_in_dim(a_cols, start, step, 0)
        matrix_part = lax.dynamic_slice_in_dim(a_blocks, start, step, 0).reshape(
            step, width, ka, width
        )
        interp_part = lax.dynamic_slice_in_dim(p_blocks, start, step, 0).reshape(
            step, width, kp, width
        )
        slot_part = lax.dynamic_slice_in_dim(p_slots, start, step, 0)
        picked = ext_blocks[cols_part]
        product = jnp.einsum(
            "irkc,ikcq->irkq", matrix_part, picked, preferred_element_type=jnp.float32
        )
        product = product.reshape(step, width, ka * kp, width)
        reached = ext_ids[cols_part].reshape(step, ka * kp)
        wanted = patterns[slot_part]
        match = (reached[:, None, :, None] == wanted[:, :, None, :]).astype(jnp.float32)
        merged = jnp.einsum(
            "irjc,imjs->imrsc",
            product,
            match,
            precision=lax.Precision.HIGH,
            preferred_element_type=jnp.float32,
        )
        merged = merged.astype(jnp.bfloat16).reshape(step, kp, width, kc * width)
        term = jnp.einsum(
            "irmc,imrx->imcx", interp_part, merged, preferred_element_type=jnp.float32
        )
        term = term.reshape(step * kp, width * kc * width)
        return (total.at[slot_part.reshape(step * kp)].add(term), None)

    total, unused = lax.scan(
        advance, jnp.zeros((slots, width * kc * width), jnp.float32), jnp.arange(count)
    )
    targets = jnp.where(table >= 0, slot_range // cap * owned + table, -1)
    pick = (
        targets[None, :] == jnp.arange(owned * lax.axis_size("row"), dtype=jnp.int32)[:, None]
    ).astype(jnp.float32)
    summed = lax.psum_scatter(
        jnp.dot(
            pick, total, precision=lax.Precision.HIGHEST, preferred_element_type=jnp.float32
        ).astype(jnp.bfloat16),
        "row",
        scatter_dimension=0,
        tiled=True,
    ).astype(jnp.float32)
    return summed.reshape(owned, width, kc * width)


def solution(mesh):
    in_specs = (
        P(("slab", "row"), None, None),
        P(("slab", "row"), None, None),
        P(("slab", "row"), None),
        P(("slab", "row"), None),
        P(("slab", "row"), None, None),
        P(("slab", "row"), None, None, None),
        P(("slab", "row"), None, None),
    )
    out_specs = P(("slab", "row"), None, None)
    return jax.shard_map(
        per_device, mesh=mesh, in_specs=in_specs, out_specs=out_specs, check_vma=False
    )
```

profile of v0, /device:TPU:16, one launch (start us, length us, event | category | flops | bytes accessed | tf_op | source)
XLA Modules:
  0.0 687.1 jit_solution(16639226979832962629)
XLA Ops:
  9.1 1.9 gather_fusion.3
  11.9 1.9 collective-permute-start
  13.8 3.6 collective-permute-start.1
  19.0 1.9 collective-permute-start.4
  20.9 3.6 collective-permute-start.5
  24.6 3.8 collective-permute-start.6
  28.9 1.5 constant_dynamic-update-slice_fusion.4
  30.5 3.8 collective-permute-start.2
  34.4 1.3 collective-permute-start.3
  35.8 1.3 collective-permute-start.7
  37.1 2.7 collective-permute-done.3
  42.4 3.4 collective-permute-done.7
  46.5 3.9 broadcast_in_dim.14
  50.4 398.0 %while.10 = (s32[]{:T(128)}, f32[64,32768]{1,0:T(8,128)}, s32[4]{0:T(128)S(1)}, s32[64,4]{0,1:T(4,128)S(1)}, bf16[64,64,256]{2,1,0:T(8,128)(2,1)}, /*index=5*/s3...) while((s32[]{:T(128)}, f32[64,32768]{1,0:T(8,128)}, ...), condition=%wide.region_2.3_spmd, body=%wide.region_0.2_spmd.sunk | while | flops 859849408 | bytes 129400336 | solution.py:110
  72.6 4.6 gather_fusion
  77.2 1.3 constant_dynamic-slice_fusion.11
  78.5 1.3 reshape.233
  79.8 3.1 convolution_bitcast_fusion.2
  82.9 8.8 %copy.90 = f32[16,64,7,256]{3,2,1,0:T(8,128)} copy(f32[16,64,7,256]{3,1,2,0:T(8,128)S(1)} %convolution_bitcast_fusion.2) | data formatting | bytes 14680064 | tf_op jit(solution)/shard_map/while/body/eval_jaxpr/irkc,ikcq->irkq/transpose | solution.py:89
  91.8 12.8 %reshape.234 = f32[16,64,28,64,1]{3,2,1,0,4:T(8,128)} reshape(f32[16,64,7,256]{3,2,1,0:T(8,128)} %copy.90) | data formatting | bytes 14680064 | tf_op jit(solution)/shard_map/while/body/eval_jaxpr/reshape | solution.py:92
  106.2 14.6 %convert_bitcast_fusion.2 = bf16[16,4,64,8,64]{4,3,2,1,0:T(8,128)(2,1)} fusion(f32[16,64,28,64,1]{3,2,1,0,4:T(8,128)} %reshape.234, s32[16,4,8]{2,1,0:T(4,128)S(1)} %bitcast.72, s32[16,28]{1,0:T(8,128)S(1)} %eq.58), kind=kOutput, calls=%fused_computation.9.clone.1 | convolution fusion | flops 354433024 | bytes 11538176 | tf_op jit(solution)/shard_map/while/body/eval_jaxpr/irjc,imjs->imrsc/dot_general | solution.py:96
  120.8 11.8 %reshape.236 = bf16[16,4,64,512]{3,2,1,0:T(8,128)(2,1)} reshape(bf16[16,4,64,8,64]{4,3,2,1,0:T(8,128)(2,1)} %convert_bitcast_fusion.2) | data formatting | bytes 8388608 | tf_op jit(solution)/shard_map/while/body/eval_jaxpr/reshape | solution.py:103
  132.5 1.1 constant_dynamic-slice_fusion.9
  134.1 3.4 fusion.40
  137.5 8.0 %copy.91 = f32[8,8,64,512]{3,1,2,0:T(8,128)} copy(f32[8,8,64,512]{3,2,1,0:T(8,128)S(1)} %bitcast.67) | data formatting | bytes 16777216 | tf_op jit(solution)/shard_map/while
  145.6 18.8 %scatter_fusion = f32[64,32768]{1,0:T(8,128)} fusion(f32[64,32768]{1,0:T(8,128)} %get-tuple-element.204, s32[64]{0:T(128)S(1)} %fusion.39, f32[64,32768]{1,0:T(8,128)} %bitcast.68), kind=kCustom, calls=%fused_computation.6.clone.1 | custom fusion | flops 2097152 | bytes 25166080 | tf_op jit(solution)/shard_map/while/body/eval_jaxpr/scatter-add | solution.py:108
  165.9 4.6 gather_fusion
  170.5 1.3 constant_dynamic-slice_fusion.11
  171.8 1.3 reshape.233
  173.1 3.1 convolution_bitcast_fusion.2
  176.3 8.8 %copy.90 = f32[16,64,7,256]{3,2,1,0:T(8,128)} copy(f32[16,64,7,256]{3,1,2,0:T(8,128)S(1)} %convolution_bitcast_fusion.2) | data formatting | bytes 14680064 | tf_op jit(solution)/shard_map/while/body/eval_jaxpr/irkc,ikcq->irkq/transpose | solution.py:89
  185.1 12.8 %reshape.234 = f32[16,64,28,64,1]{3,2,1,0,4:T(8,128)} reshape(f32[16,64,7,256]{3,2,1,0:T(8,128)} %copy.90) | data formatting | bytes 14680064 | tf_op jit(solution)/shard_map/while/body/eval_jaxpr/reshape | solution.py:92
  199.5 14.6 %convert_bitcast_fusion.2 = bf16[16,4,64,8,64]{4,3,2,1,0:T(8,128)(2,1)} fusion(f32[16,64,28,64,1]{3,2,1,0,4:T(8,128)} %reshape.234, s32[16,4,8]{2,1,0:T(4,128)S(1)} %bitcast.72, s32[16,28]{1,0:T(8,128)S(1)} %eq.58), kind=kOutput, calls=%fused_computation.9.clone.1 | convolution fusion | flops 354433024 | bytes 11538176 | tf_op jit(solution)/shard_map/while/body/eval_jaxpr/irjc,imjs->imrsc/dot_general | solution.py:96
  214.1 11.8 %reshape.236 = bf16[16,4,64,512]{3,2,1,0:T(8,128)(2,1)} reshape(bf16[16,4,64,8,64]{4,3,2,1,0:T(8,128)(2,1)} %convert_bitcast_fusion.2) | data formatting | bytes 8388608 | tf_op jit(solution)/shard_map/while/body/eval_jaxpr/reshape | solution.py:103
  225.9 1.1 constant_dynamic-slice_fusion.9
  227.4 3.4 fusion.40
  230.9 8.0 %copy.91 = f32[8,8,64,512]{3,1,2,0:T(8,128)} copy(f32[8,8,64,512]{3,2,1,0:T(8,128)S(1)} %bitcast.67) | data formatting | bytes 16777216 | tf_op jit(solution)/shard_map/while
  238.9 18.8 %scatter_fusion = f32[64,32768]{1,0:T(8,128)} fusion(f32[64,32768]{1,0:T(8,128)} %get-tuple-element.204, s32[64]{0:T(128)S(1)} %fusion.39, f32[64,32768]{1,0:T(8,128)} %bitcast.68), kind=kCustom, calls=%fused_computation.6.clone.1 | custom fusion | flops 2097152 | bytes 25166080 | tf_op jit(solution)/shard_map/while/body/eval_jaxpr/scatter-add | solution.py:108
  259.3 4.6 gather_fusion
  263.9 1.3 constant_dynamic-slice_fusion.11
  265.2 1.3 reshape.233
  266.5 3.1 convolution_bitcast_fusion.2
  269.6 8.8 %copy.90 = f32[16,64,7,256]{3,2,1,0:T(8,128)} copy(f32[16,64,7,256]{3,1,2,0:T(8,128)S(1)} %convolution_bitcast_fusion.2) | data formatting | bytes 14680064 | tf_op jit(solution)/shard_map/while/body/eval_jaxpr/irkc,ikcq->irkq/transpose | solution.py:89
  278.4 12.8 %reshape.234 = f32[16,64,28,64,1]{3,2,1,0,4:T(8,128)} reshape(f32[16,64,7,256]{3,2,1,0:T(8,128)} %copy.90) | data formatting | bytes 14680064 | tf_op jit(solution)/shard_map/while/body/eval_jaxpr/reshape | solution.py:92
  292.9 14.6 %convert_bitcast_fusion.2 = bf16[16,4,64,8,64]{4,3,2,1,0:T(8,128)(2,1)} fusion(f32[16,64,28,64,1]{3,2,1,0,4:T(8,128)} %reshape.234, s32[16,4,8]{2,1,0:T(4,128)S(1)} %bitcast.72, s32[16,28]{1,0:T(8,128)S(1)} %eq.58), kind=kOutput, calls=%fused_computation.9.clone.1 | convolution fusion | flops 354433024 | bytes 11538176 | tf_op jit(solution)/shard_map/while/body/eval_jaxpr/irjc,imjs->imrsc/dot_general | solution.py:96
  307.5 11.8 %reshape.236 = bf16[16,4,64,512]{3,2,1,0:T(8,128)(2,1)} reshape(bf16[16,4,64,8,64]{4,3,2,1,0:T(8,128)(2,1)} %convert_bitcast_fusion.2) | data formatting | bytes 8388608 | tf_op jit(solution)/shard_map/while/body/eval_jaxpr/reshape | solution.py:103
  319.2 1.1 constant_dynamic-slice_fusion.9
  320.8 3.4 fusion.40
  324.2 8.0 %copy.91 = f32[8,8,64,512]{3,1,2,0:T(8,128)} copy(f32[8,8,64,512]{3,2,1,0:T(8,128)S(1)} %bitcast.67) | data formatting | bytes 16777216 | tf_op jit(solution)/shard_map/while
  332.3 18.8 %scatter_fusion = f32[64,32768]{1,0:T(8,128)} fusion(f32[64,32768]{1,0:T(8,128)} %get-tuple-element.204, s32[64]{0:T(128)S(1)} %fusion.39, f32[64,32768]{1,0:T(8,128)} %bitcast.68), kind=kCustom, calls=%fused_computation.6.clone.1 | custom fusion | flops 2097152 | bytes 25166080 | tf_op jit(solution)/shard_map/while/body/eval_jaxpr/scatter-add | solution.py:108
  352.6 4.6 gather_fusion
  357.2 1.3 constant_dynamic-slice_fusion.11
  358.5 1.3 reshape.233
  359.8 3.1 convolution_bitcast_fusion.2
  363.0 8.8 %copy.90 = f32[16,64,7,256]{3,2,1,0:T(8,128)} copy(f32[16,64,7,256]{3,1,2,0:T(8,128)S(1)} %convolution_bitcast_fusion.2) | data formatting | bytes 14680064 | tf_op jit(solution)/shard_map/while/body/eval_jaxpr/irkc,ikcq->irkq/transpose | solution.py:89
  371.8 12.8 %reshape.234 = f32[16,64,28,64,1]{3,2,1,0,4:T(8,128)} reshape(f32[16,64,7,256]{3,2,1,0:T(8,128)} %copy.90) | data formatting | bytes 14680064 | tf_op jit(solution)/shard_map/while/body/eval_jaxpr/reshape | solution.py:92
  386.2 14.6 %convert_bitcast_fusion.2 = bf16[16,4,64,8,64]{4,3,2,1,0:T(8,128)(2,1)} fusion(f32[16,64,28,64,1]{3,2,1,0,4:T(8,128)} %reshape.234, s32[16,4,8]{2,1,0:T(4,128)S(1)} %bitcast.72, s32[16,28]{1,0:T(8,128)S(1)} %eq.58), kind=kOutput, calls=%fused_computation.9.clone.1 | convolution fusion | flops 354433024 | bytes 11538176 | tf_op jit(solution)/shard_map/while/body/eval_jaxpr/irjc,imjs->imrsc/dot_general | solution.py:96
  400.8 11.8 %reshape.236 = bf16[16,4,64,512]{3,2,1,0:T(8,128)(2,1)} reshape(bf16[16,4,64,8,64]{4,3,2,1,0:T(8,128)(2,1)} %convert_bitcast_fusion.2) | data formatting | bytes 8388608 | tf_op jit(solution)/shard_map/while/body/eval_jaxpr/reshape | solution.py:103
  414.1 3.4 fusion.40
  417.5 8.0 %copy.91 = f32[8,8,64,512]{3,1,2,0:T(8,128)} copy(f32[8,8,64,512]{3,2,1,0:T(8,128)S(1)} %bitcast.67) | data formatting | bytes 16777216 | tf_op jit(solution)/shard_map/while
  425.6 18.8 %scatter_fusion = f32[64,32768]{1,0:T(8,128)} fusion(f32[64,32768]{1,0:T(8,128)} %get-tuple-element.204, s32[64]{0:T(128)S(1)} %fusion.39, f32[64,32768]{1,0:T(8,128)} %bitcast.68), kind=kCustom, calls=%fused_computation.6.clone.1 | custom fusion | flops 2097152 | bytes 25166080 | tf_op jit(solution)/shard_map/while/body/eval_jaxpr/scatter-add | solution.py:108
  448.4 15.0 %convolution_convert_fusion = bf16[128,32768]{1,0:T(8,128)(2,1)} fusion(f32[64,32768]{1,0:T(8,128)} %get-tuple-element.57, s32[64]{0:T(128)S(1)} %copy-done.4), kind=kOutput, calls=%fused_computation.26 | convolution fusion | flops 3225427968 | bytes 16777472 | tf_op jit(solution)/shard_map/dot_general | solution.py:118
  465.4 212.6 %all-reduce.3.cloned.1.call-done = bf16[128,32768]{1,0:T(8,128)(2,1)} async-done(((bf16[128,32768]{1,0:T(8,128)(2,1)}), bf16[128,32768]{1,0:T(8,128)(2,1)}) %all-reduce.3.cloned.1.call-update) | async-done | bytes 8388624
  678.0 1.1 dynamic-slice_convert_fusion
  (120 shorter events, 24.2 us)
Async XLA Ops:
  6.5 671.4 %all-reduce.3.cloned.1.call-start = ((), (), s32[]{:S(2)}) async-start(), calls=%async_computation | async-start | bytes 16777216
  9.1 2.1 copy-start.2
  9.1 8.4 %copy-start = (bf16[64,64,256]{2,1,0:T(8,128)(2,1)S(1)}, bf16[64,64,256]{2,1,0:T(8,128)(2,1)}, u32[]{:S(2)}) copy-start(bf16[64,64,256]{2,1,0:T(8,128)(2,1)} %param.10) | copy-start | bytes 6291460
  11.9 18.6 %collective-permute-start = (s32[8,4]{1,0:T(8,128)S(1)}, s32[8,4]{1,0:T(8,128)S(1)}, u32[]{:S(2)}, u32[]{:S(2)}) collective-permute-start(s32[8,4]{1,0:T(8,128)S(1)} %get-tuple-element.125), channel_id=1, source_target_pairs={{0,32},{32,64},{64,96},{96,128},{128,160},{160,192},{192,224},{1,3... | collective-permute-start | bytes 392 | tf_op jit(solution)/shard_map/ppermute | solution.py:19
  13.8 16.6 %copy-start.3 = (s32[1,32,2,8]{1,3,2,0:T(8,128)S(1)}, s32[1,32,2,8]{1,3,2,0:T(8,128)}, u32[]{:S(2)}) copy-start(s32[1,32,2,8]{1,3,2,0:T(8,128)} %param.14) | copy-start | bytes 6148
  13.8 20.6 %collective-permute-start.1 = (s32[8,4]{1,0:T(8,128)S(1)}, s32[8,4]{1,0:T(8,128)S(1)}, u32[]{:S(2)}, u32[]{:S(2)}) collective-permute-start(s32[8,4]{1,0:T(8,128)S(1)} %get-tuple-element.124), channel_id=1, source_target_pairs={{32,0},{64,32},{96,64},{128,96},{160,128},{192,160},{224,192},{33,... | collective-permute-start | bytes 392 | tf_op jit(solution)/shard_map/ppermute | solution.py:21
  19.0 21.2 %collective-permute-start.4 = (bf16[8,64,256]{2,1,0:T(8,128)(2,1)}, bf16[8,64,256]{2,1,0:T(8,128)(2,1)S(1)}, u32[]{:S(2)}, u32[]{:S(2)}) collective-permute-start(bf16[8,64,256]{2,1,0:T(8,128)(2,1)} %get-tuple-element.121), channel_id=1, source_target_pairs={{0,32},{32,64},{64,96},{96,128},{128,160},{160,192},{192,224},{1,3... | collective-permute-start | bytes 786440 | tf_op jit(solution)/shard_map/ppermute | solution.py:19
  20.9 20.0 %collective-permute-start.5 = (bf16[8,64,256]{2,1,0:T(8,128)(2,1)}, bf16[8,64,256]{2,1,0:T(8,128)(2,1)S(1)}, u32[]{:S(2)}, u32[]{:S(2)}) collective-permute-start(bf16[8,64,256]{2,1,0:T(8,128)(2,1)} %get-tuple-element.120), channel_id=1, source_target_pairs={{32,0},{64,32},{96,64},{128,96},{160,128},{192,160},{224,192},{33,... | collective-permute-start | bytes 786440 | tf_op jit(solution)/shard_map/ppermute | solution.py:21
  24.6 17.1 %collective-permute-start.6 = (bf16[8,64,256]{2,1,0:T(8,128)(2,1)}, bf16[8,64,256]{2,1,0:T(8,128)(2,1)S(1)}, u32[]{:S(2)}, u32[]{:S(2)}) collective-permute-start(bf16[8,64,256]{2,1,0:T(8,128)(2,1)} %get-tuple-element.119), channel_id=1, source_target_pairs={{0,1},{1,2},{2,3},{3,4},{4,5},{5,6},{6,7},{7,8},{8,9},{9,10},{10,1... | collective-permute-start | bytes 786440 | tf_op jit(solution)/shard_map/ppermute | solution.py:19
  30.5 5.3 collective-permute-start.2
  34.4 5.5 collective-permute-start.3
  35.8 10.0 %collective-permute-start.7 = (bf16[8,64,256]{2,1,0:T(8,128)(2,1)S(1)}, bf16[8,64,256]{2,1,0:T(8,128)(2,1)S(1)}, u32[]{:S(2)}, u32[]{:S(2)}) collective-permute-start(bf16[8,64,256]{2,1,0:T(8,128)(2,1)S(1)} %get-tuple-element.118), channel_id=1, source_target_pairs={{1,0},{2,1},{3,2},{4,3},{5,4},{6,5},{7,6},{8,7},{9,8},{10,9},{11,1... | collective-permute-start | bytes 786440 | tf_op jit(solution)/shard_map/ppermute | solution.py:21
  46.5 3.9 copy-start.1
  50.4 398.0 %copy-start.4 = (s32[64]{0:T(128)S(1)}, s32[64]{0:T(128)}, u32[]{:S(2)}) copy-start(s32[64]{0:T(128)} %compare_select_fusion.4) | copy-start | bytes 772
  463.5 0.7 copy-start.5
Sparse Core Ops, SparseCore 0:
  463.6 214.2 all-reduce.2
where the time goes:
time: 694 us; the launch traced here: 687 us
  local copies, waits for them, and re-layouts  227 us (33%)
  waiting for transfers between devices  219 us (32%)
  matrix products  99.7 us (14%)
  other arithmetic  78.6 us (11%)
  loops' own time  27.6 us (4%)
  starting transfers between devices  21.3 us (3%)
  between operations  14.4 us (2%)
    unnamed x2, waiting for transfers between devices  213 us
    scatter-add x4, other arithmetic, advance(): return (total.at[slot_part.reshape(step * kp)].add(term), None)  75.4 us
    dot_general x4, matrix products, advance(): jnp.einsum('irjc,imjs->imrsc', product, match, precision=lax.Precision.HI...  58.4 us
    reshape x4, local copies, waits for them, and re-layouts, advance(): product = product.reshape(step, width, ka * kp, width)  51.4 us
    reshape x4, local copies, waits for them, and re-layouts, advance(): merged = merged.astype(jnp.bfloat16).reshape(step, kp, width, kc * width)  47 us
    transpose x4, local copies, waits for them, and re-layouts, advance(): jnp.einsum('irkc,ikcq->irkq', matrix_part, picked, preferred_element_type...  35.3 us
    while x4, local copies, waits for them, and re-layouts  31.8 us
    another operation x1, loops' own time, per_device(): lax.scan(advance, jnp.zeros((slots, width * kc * width), jnp.float32), jn...  27.6 us
  transfers between devices with their start and end apart: 9, of which 3 were waited for; matrix products, arithmetic and copies ran while one was open for 1% of the time, Pallas kernels for 0%

commit v1 on v0

v1 whole, which is shorter than its diff:
```python
import functools

import jax
import jax.numpy as jnp
from jax import lax
from jax.experimental import pallas as pl
from jax.experimental.pallas import tpu as pltpu
from jax.sharding import PartitionSpec as P

NC = 4
UNROLL = 8


def coarse_kernel(cols, slots, masks, places, a_hbm, p_hbm, halo_hbm, out_ref, a_v, ext_v, g_v, acc, items, sems):
    rows, width, span = a_v.shape
    ka = span // width
    kp = ext_v.shape[2] // width
    kq = ka * kp
    nslots, _, outspan = out_ref.shape
    kc = outspan // width
    pair = 2 * width
    copy_a = pltpu.make_async_copy(a_hbm, a_v, sems.at[0])
    copy_p = pltpu.make_async_copy(p_hbm, ext_v.at[pl.ds(0, rows)], sems.at[1])
    copy_h = pltpu.make_async_copy(halo_hbm, ext_v.at[pl.ds(rows, halo_hbm.shape[0])], sems.at[2])
    copy_a.start()
    copy_p.start()
    copy_h.start()

    def clear(t, unused):
        acc[pl.ds(t * kc, kc)] = jnp.zeros((kc, width, pair), jnp.float32)
        return unused

    lax.fori_loop(0, nslots, clear, 0)
    acc[pl.ds(nslots * kc, 1)] = jnp.zeros((1, width, pair), jnp.float32)

    def gather_items(im, count):
        slot = slots[im]
        head = im * 32

        def more(state):
            return state[0] != 0

        def take(state):
            mask, at = state
            bit = 31 - lax.clz(mask)
            items[at] = (head + bit) * 1024 + slot * kc + places[im * kq + bit]
            return (mask - lax.shift_left(1, bit), at + 1)

        return lax.while_loop(more, take, (masks[im], count))[1]

    count = lax.fori_loop(0, rows * kp, gather_items, 0)
    for u in range(UNROLL):
        items[count + u] = nslots * kc
    copy_a.wait()
    copy_p.wait()
    copy_h.wait()

    def products(i, unused):
        row = a_v[i]
        for k in range(ka):
            right = ext_v[cols[i * ka + k]]
            value = jnp.dot(row[:, k * width : (k + 1) * width], right, preferred_element_type=jnp.float32).astype(
                jnp.bfloat16
            )
            for h in range(kp // 2):
                g_v[(i * ka + k) * (kp // 2) + h] = value[:, h * pair : (h + 1) * pair]
        return unused

    lax.fori_loop(0, rows, products, 0)
    upper = lax.broadcasted_iota(jnp.int32, (width, pair), 1) // width

    def batch(b, unused):
        found = []
        for u in range(UNROLL):
            word = items[b * UNROLL + u]
            target = word % 1024
            bit = (word // 1024) % 32
            im = word // 32768
            i = im // kp
            m = im % kp
            k = bit // kp
            q = bit % kp
            g = g_v[(i * ka + k) * (kp // 2) + q // 2]
            g = jnp.where(upper == q % 2, g, jnp.zeros_like(g))
            p = ext_v[i, :, pl.ds(pl.multiple_of((m // 2) * pair, pair), pair)]
            z = lax.dot_general(p, g, (((0,), (0,)), ((), ())), preferred_element_type=jnp.float32)
            z = jnp.where(m % 2 == 1, z[width:], z[:width])
            found.append((target, z))
        for target, z in found:
            acc[target] = acc[target] + z
        return unused

    lax.fori_loop(0, (count + UNROLL - 1) // UNROLL, batch, 0)

    def finish(t, unused):
        for h in range(kc // 2):
            one = acc[t * kc + 2 * h]
            two = acc[t * kc + 2 * h + 1]
            one = one + pltpu.roll(one, width, 1)
            two = two + pltpu.roll(two, width, 1)
            out_ref[t, :, h * pair : (h + 1) * pair] = jnp.where(upper == 0, one, two).astype(jnp.bfloat16)
        return unused

    lax.fori_loop(0, nslots, finish, 0)


def coarse_partials(cols, slots, masks, places, a_blocks, p_blocks, halo, nslots, kc):
    rows, width, span = a_blocks.shape
    kp = p_blocks.shape[2] // width
    ka = span // width
    extended = rows + halo.shape[0]
    smem = pl.BlockSpec(memory_space=pltpu.SMEM)
    hbm = pl.BlockSpec(memory_space=pl.ANY)
    return pl.pallas_call(
        coarse_kernel,
        out_shape=jax.ShapeDtypeStruct((nslots, width, kc * width), jnp.bfloat16),
        in_specs=[smem, smem, smem, smem, hbm, hbm, hbm],
        out_specs=pl.BlockSpec(memory_space=pltpu.VMEM),
        scratch_shapes=[
            pltpu.VMEM((rows, width, span), jnp.bfloat16),
            pltpu.VMEM((extended, width, kp * width), jnp.bfloat16),
            pltpu.VMEM((rows * ka * (kp // 2), width, 2 * width), jnp.bfloat16),
            pltpu.VMEM((nslots * kc + 1, width, 2 * width), jnp.float32),
            pltpu.SMEM((rows * kp * ka * kp + UNROLL,), jnp.int32),
            pltpu.SemaphoreType.DMA((3,)),
        ],
        compiler_params=pltpu.CompilerParams(vmem_limit_bytes=56 * 2**20),
        name="coarse_partials",
    )(cols, slots, masks, places, a_blocks, p_blocks, halo)


def sum_kernel(ids, parts, out_ref):
    out_ref[...] = jnp.zeros_like(out_ref)

    def one(n, unused):
        row = ids[n]

        @pl.when(row >= 0)
        def _():
            out_ref[row] = out_ref[row] + parts[n].astype(jnp.float32)

        return unused

    lax.fori_loop(0, parts.shape[0], one, 0)


def sum_parts(ids, parts):
    return pl.pallas_call(
        sum_kernel,
        out_shape=jax.ShapeDtypeStruct((NC,) + parts.shape[1:], jnp.float32),
        in_specs=[pl.BlockSpec(memory_space=pltpu.SMEM), pl.BlockSpec(memory_space=pltpu.VMEM)],
        out_specs=pl.BlockSpec(memory_space=pltpu.VMEM),
        compiler_params=pltpu.CompilerParams(vmem_limit_bytes=32 * 2**20),
        name="sum_parts",
    )(ids, parts)


def lookup(table, index):
    hot = index[..., None] == jnp.arange(table.shape[0], dtype=jnp.int32)
    return jnp.sum(jnp.where(hot, table, 0), axis=-1)


def find_matches(ext_ids, a_cols, p_slots, patterns):
    rows = a_cols.shape[0]
    kp = p_slots.shape[1]
    reached = jnp.stack([lookup(ext_ids[:, q], a_cols) for q in range(kp)], -1).reshape(rows, -1)
    wanted = jnp.stack([lookup(patterns[:, j], p_slots) for j in range(patterns.shape[1])], 0)
    order = jnp.arange(1, patterns.shape[1] + 1, dtype=jnp.int32)[:, None, None, None]
    places = jnp.sum(jnp.where(reached[None, :, None, :] == wanted[..., None], order, 0), 0)
    bits = lax.shift_left(1, jnp.arange(reached.shape[1], dtype=jnp.int32))
    masks = jnp.sum(jnp.where(places > 0, bits, 0), -1)
    return places - 1, masks


def per_device(a_blocks, p_blocks, a_cols, p_slots, touched, touch_cols, halo_rows):
    nrow = lax.axis_size("row")
    nslab = lax.axis_size("slab")
    slab_at = lax.axis_index("slab")
    cap = touched.shape[2]
    slots = touched.shape[1] * cap
    table = touched.reshape(slots)
    patterns = touch_cols.reshape(slots, touch_cols.shape[3])
    kc = patterns.shape[1]
    coarse_ids = (slab_at * nrow + p_slots // cap) * NC + lookup(table, p_slots)
    lists = halo_rows[0]
    sent_blocks = p_blocks[lists]
    sent_ids = coarse_ids[lists]
    routes = (
        (1, "slab", [(i, i + 1) for i in range(nslab - 1)]),
        (0, "slab", [(i + 1, i) for i in range(nslab - 1)]),
        (3, "row", [(i, i + 1) for i in range(nrow - 1)]),
        (2, "row", [(i + 1, i) for i in range(nrow - 1)]),
    )
    halo_ids = jnp.concatenate([lax.ppermute(sent_ids[n], axis, way) for n, axis, way in routes], 0)
    halo = jnp.concatenate([lax.ppermute(sent_blocks[n], axis, way) for n, axis, way in routes], 0)
    ext_ids = jnp.concatenate([coarse_ids, halo_ids], 0)
    places, masks = find_matches(ext_ids, a_cols, p_slots, patterns)
    partial = coarse_partials(
        a_cols.reshape(-1), p_slots.reshape(-1), masks.reshape(-1), places.reshape(-1), a_blocks, p_blocks, halo, slots, kc
    )
    width = a_blocks.shape[1]
    parts = lax.all_to_all(partial.reshape(nrow, cap * width, kc * width), "row", 0, 0)
    ids = lax.all_to_all(touched[0], "row", 0, 0)
    return sum_parts(ids.reshape(-1), parts.reshape(slots, width, kc * width))


def solution(mesh):
    in_specs = (
        P(("slab", "row"), None, None),
        P(("slab", "row"), None, None),
        P(("slab", "row"), None),
        P(("slab", "row"), None),
        P(("slab", "row"), None, None),
        P(("slab", "row"), None, None, None),
        P(("slab", "row"), None, None),
    )
    out_specs = P(("slab", "row"), None, None)
    return jax.shard_map(per_device, mesh=mesh, in_specs=in_specs, out_specs=out_specs, check_vma=False)
```

time: 694 us -> 238 us (0.34)
  local copies, waits for them, and re-layouts: 227 us -> 10.2 us
  waiting for transfers between devices: 219 us -> 92 us
  matrix products: 99.7 us -> 0 us
  other arithmetic: 78.6 us -> 5.62 us
  Pallas kernels: 0 us -> 67.2 us
  starting transfers between devices: 21.3 us -> 60.4 us
  loops' own time: 27.6 us -> 0 us
  between operations: 14.4 us -> 0.23 us
    unnamed x2 -> x0, waiting for transfers between devices: 213 us -> none
    reshape x16 -> x4, local copies, waits for them, and re-layouts: 104 us -> 2.22 us  [the longest x1 0.72 us: per_device(): a_cols.reshape(-1)]
    dot_general x13 -> x0, matrix products: 99.7 us -> none  [the longest x4 58.4 us: advance(): jnp.einsum('irjc,imjs->imrsc', product, match, precision=lax.Precision.HI...]
    all_to_all x0 -> x2, waiting for transfers between devices: none -> 86.8 us  [the longest x1 86.8 us: per_device(): lax.all_to_all(partial.reshape(nrow, cap * width, kc * width), 'row', 0, 0)]
    scatter-add x4 -> x0, other arithmetic: 75.4 us -> none  [advance(): return (total.at[slot_part.reshape(step * kp)].add(term), None)]
    pallas_call x0 -> x2, Pallas kernels: none -> 67.2 us  [the longest x1 62.7 us: coarse_partials(): pl.pallas_call(coarse_kernel, out_shape=jax.ShapeDtypeStruct((nslots, wid...]
    all_to_all x0 -> x2, starting transfers between devices: none -> 39.7 us  [the longest x1 26.5 us: per_device(): lax.all_to_all(partial.reshape(nrow, cap * width, kc * width), 'row', 0, 0)]
    transpose x4 -> x0, local copies, waits for them, and re-layouts: 35.3 us -> none  [advance(): jnp.einsum('irkc,ikcq->irkq', matrix_part, picked, preferred_element_type...]
  transfers between devices with their start and end apart: 9 -> 10, of which waited for: 3 -> 3; matrix products, arithmetic and copies ran while one was open for 1% -> 4% of each run, Pallas kernels for 0% -> 27%
where the time goes in v1:
time: 238 us; the launch traced here: 236 us
  waiting for transfers between devices  92 us (39%)
  Pallas kernels  67.2 us (28%)
  starting transfers between devices  60.4 us (25%)
  local copies, waits for them, and re-layouts  10.2 us (4%)
  other arithmetic  5.62 us (2%)
    all_to_all x1, waiting for transfers between devices, per_device(): lax.all_to_all(partial.reshape(nrow, cap * width, kc * width), 'row', 0, 0)  86.8 us
    pallas_call x1, Pallas kernels, coarse_partials(): pl.pallas_call(coarse_kernel, out_shape=jax.ShapeDtypeStruct((nslots, wid...  62.7 us
    all_to_all x1, starting transfers between devices, per_device(): lax.all_to_all(partial.reshape(nrow, cap * width, kc * width), 'row', 0, 0)  26.5 us
    all_to_all x1, starting transfers between devices, per_device(): ids = lax.all_to_all(touched[0], 'row', 0, 0)  13.3 us
    ppermute x4, starting transfers between devices, per_device(): lax.ppermute(sent_ids[n], axis, way)  10.7 us
    ppermute x4, starting transfers between devices, per_device(): lax.ppermute(sent_blocks[n], axis, way)  9.98 us
    ppermute x4, waiting for transfers between devices, per_device(): lax.ppermute(sent_blocks[n], axis, way)  5.21 us
  transfers between devices with their start and end apart: 10, of which 3 were waited for; matrix products, arithmetic and copies ran while one was open for 4% of the time, Pallas kernels for 27%

profile of v1, /device:TPU:16, one launch (start us, length us, event | category | flops | bytes accessed | tf_op | source)
XLA Modules:
  0.0 235.6 jit_solution(16531322300536355880)
XLA Ops:
  0.0 0.0 copy-start.2
  0.0 0.0 copy-start
  0.0 0.0 copy-start.1
  0.0 0.8 copy.119
  0.8 0.3 slice_reduce_fusion
  1.2 0.8 copy.112
  1.9 0.1 reshape.71
  2.0 1.5 select_reduce_fusion.13
  3.5 0.7 fusion.3
  4.2 0.1 copy.113
  4.3 0.7 compare_select_fusion
  5.0 0.1 reshape.78
  5.1 0.6 gather_fusion
  5.7 1.9 collective-permute-start
  7.6 3.6 %collective-permute-start.1 = (s32[8,4]{1,0:T(8,128)S(1)}, s32[8,4]{1,0:T(8,128)S(1)}, u32[]{:S(2)}, u32[]{:S(2)}) collective-permute-start(s32[8,4]{1,0:T(8,128)S(1)} %get-tuple-element.34), channel_id=1, source_target_pairs={{32,0},{64,32},{96,64},{128,96},{160,128},{192,160},{224,192},{33,... | collective-permute-start | bytes 392 | tf_op jit(solution)/shard_map/ppermute | solution.py:194
  11.2 3.8 %collective-permute-start.2 = (s32[8,4]{1,0:T(8,128)S(1)}, s32[8,4]{1,0:T(8,128)S(1)}, u32[]{:S(2)}, u32[]{:S(2)}) collective-permute-start(s32[8,4]{1,0:T(8,128)S(1)} %get-tuple-element.33), channel_id=1, source_target_pairs={{0,1},{1,2},{2,3},{3,4},{4,5},{5,6},{6,7},{7,8},{8,9},{9,10},{10,1... | collective-permute-start | bytes 392 | tf_op jit(solution)/shard_map/ppermute | solution.py:194
  15.1 1.3 collective-permute-start.3
  16.4 2.2 gather_fusion.1
  18.6 0.1 fusion.5
  18.7 1.9 collective-permute-start.4
  20.6 0.0 copy-done.2
  20.6 0.7 copy.109
  21.3 13.3 %all-to-all-start = ((s32[32,1,2]{2,1,0:T(1,128)}), s32[32,1,2]{2,1,0:T(1,128)S(1)}, u32[]{:S(2)}, u32[]{:S(2)}) async-start(s32[32,1,2]{2,1,0:T(1,128)} %copy.109), calls=%async_computation | async-start | bytes 32768 | tf_op jit(solution)/shard_map/all_to_all | solution.py:203
  34.6 0.0 copy-done
  34.6 0.1 copy.111
  34.7 0.0 copy-done.1
  34.7 0.1 copy.110
  34.8 0.7 reshape.69.cols
  35.5 0.7 reshape.70.slots
  36.3 0.0 collective-permute-done
  36.3 3.4 %collective-permute-start.5 = (bf16[8,64,256]{2,1,0:T(8,128)(2,1)S(1)}, bf16[8,64,256]{2,1,0:T(8,128)(2,1)S(1)}, u32[]{:S(2)}, u32[]{:S(2)}) collective-permute-start(bf16[8,64,256]{2,1,0:T(8,128)(2,1)S(1)} %get-tuple-element.28), channel_id=1, source_target_pairs={{32,0},{64,32},{96,64},{128,96},{160,128},{192,160},{224,192},{33,... | collective-permute-start | bytes 786440 | tf_op jit(solution)/shard_map/ppermute | solution.py:195
  39.6 0.1 copy.114
  39.7 0.0 collective-permute-done.1
  39.7 3.4 %collective-permute-start.6 = (bf16[8,64,256]{2,1,0:T(8,128)(2,1)S(1)}, bf16[8,64,256]{2,1,0:T(8,128)(2,1)S(1)}, u32[]{:S(2)}, u32[]{:S(2)}) collective-permute-start(bf16[8,64,256]{2,1,0:T(8,128)(2,1)S(1)} %get-tuple-element.27), channel_id=1, source_target_pairs={{0,1},{1,2},{2,3},{3,4},{4,5},{5,6},{6,7},{7,8},{8,9},{9,10},{10,1... | collective-permute-start | bytes 786440 | tf_op jit(solution)/shard_map/ppermute | solution.py:195
  43.2 0.1 copy.115
  43.2 0.0 collective-permute-done.2
  43.2 1.3 collective-permute-start.7
  44.5 0.1 copy.116
  44.6 0.0 collective-permute-done.3
  44.6 0.1 copy.117
  44.7 0.1 concatenate.6
  44.8 0.7 select_reduce_fusion.4
  45.5 0.2 select_reduce_fusion
  45.7 0.1 broadcast_add_fusion
  45.8 0.1 copy.129
  45.9 0.8 sub.14.places
  46.7 0.1 copy.128
  46.8 0.7 reshape.73.masks
  47.5 0.0 collective-permute-done.4
  47.5 0.0 collective-permute-done.5
  47.5 1.0 collective-permute-done.6
  48.5 4.2 %collective-permute-done.7 = bf16[8,64,256]{2,1,0:T(8,128)(2,1)S(1)} collective-permute-done((bf16[8,64,256]{2,1,0:T(8,128)(2,1)S(1)}, bf16[8,64,256]{2,1,0:T(8,128)(2,1)S(1)}, u32[]{:S(2)}, u32[]{:S(2)}) %collective-permute-start.7) | collective-permute-done | bytes 262176 | tf_op jit(solution)/shard_map/ppermute | solution.py:195
  52.7 1.1 pad_maximum_fusion.halo_hbm
  53.8 62.7 %coarse_partials.1 = bf16[64,64,512]{2,1,0:T(8,128)(2,1)} custom-call(s32[448]{0:T(512)} %reshape.69.cols, s32[256]{0:T(256)} %reshape.70.slots, s32[256]{0:T(256)} %reshape.73.masks, s32[7168]{0:T(1024)} %sub.14.places, bf16[64,64,448]{2,1,0:T(8,128)(2,1)} %a_hbm.1, bf16[64,64,256]{2,1,0:T(8,128)(2,1)} %p_hbm.1, bf16[32,64,256]{2,1,0:T(8,128)(2,1)} %pad_maximum_fusion.halo_hbm), custom_call_target="tpu_custom_call" | custom-call | tf_op jit(solution)/shard_map/coarse_partials/pallas_call | solution.py:114
  116.5 0.0 all-to-all-done
  116.6 26.5 %all-to-all-start.1 = ((bf16[32,128,512]{2,1,0:T(8,128)(2,1)}), bf16[32,128,512]{2,1,0:T(8,128)(2,1)}, u32[]{:S(2)}, u32[]{:S(2)}) async-start(bf16[32,128,512]{2,1,0:T(8,128)(2,1)} %bitcast.46), calls=%async_computation.1 | async-start | bytes 8388608 | tf_op jit(solution)/shard_map/all_to_all | solution.py:202
  143.0 0.5 broadcast.79
  143.5 0.7 reduce.19
  144.2 0.1 reshape.68.ids
  144.3 86.8 %all-to-all-done.1 = bf16[32,128,512]{2,1,0:T(8,128)(2,1)} async-done(((bf16[32,128,512]{2,1,0:T(8,128)(2,1)}), bf16[32,128,512]{2,1,0:T(8,128)(2,1)}, u32[]{:S(2)}, u32[]{:S(2)}) %all-to-all-start.1) | async-done | bytes 4194336 | tf_op jit(solution)/shard_map/all_to_all | solution.py:202
  231.1 4.5 %sum_parts.1 = f32[4,64,512]{2,1,0:T(8,128)} custom-call(s32[64]{0:T(128)S(1)} %reshape.68.ids, bf16[64,64,512]{2,1,0:T(8,128)(2,1)} %bitcast.28.parts), custom_call_target="tpu_custom_call" | custom-call | tf_op jit(solution)/shard_map/sum_parts/pallas_call | solution.py:148
  (9 shorter events, 0.1 us)
Async XLA Ops:
  0.0 20.6 %copy-start.2 = (s32[1,32,2]{1,2,0:T(2,128)S(1)}, s32[1,32,2]{1,2,0:T(2,128)}, u32[]{:S(2)}) copy-start(s32[1,32,2]{1,2,0:T(2,128)} %param.11) | copy-start | bytes 772
  0.0 34.6 %copy-start = (s32[64,4]{0,1:T(4,128)S(1)}, s32[64,4]{0,1:T(4,128)}, u32[]{:S(2)}) copy-start(s32[64,4]{0,1:T(4,128)} %param.10) | copy-start | bytes 3076
  0.0 34.7 %copy-start.1 = (s32[64,7]{0,1:T(8,128)S(1)}, s32[64,7]{0,1:T(8,128)}, u32[]{:S(2)}) copy-start(s32[64,7]{0,1:T(8,128)} %param.9) | copy-start | bytes 5380
  5.7 30.6 %collective-permute-start = (s32[8,4]{1,0:T(8,128)S(1)}, s32[8,4]{1,0:T(8,128)S(1)}, u32[]{:S(2)}, u32[]{:S(2)}) collective-permute-start(s32[8,4]{1,0:T(8,128)S(1)} %get-tuple-element.35), channel_id=1, source_target_pairs={{0,32},{32,64},{64,96},{96,128},{128,160},{160,192},{192,224},{1,3... | collective-permute-start | bytes 392 | tf_op jit(solution)/shard_map/ppermute | solution.py:194
  7.6 32.1 %collective-permute-start.1 = (s32[8,4]{1,0:T(8,128)S(1)}, s32[8,4]{1,0:T(8,128)S(1)}, u32[]{:S(2)}, u32[]{:S(2)}) collective-permute-start(s32[8,4]{1,0:T(8,128)S(1)} %get-tuple-element.34), channel_id=1, source_target_pairs={{32,0},{64,32},{96,64},{128,96},{160,128},{192,160},{224,192},{33,... | collective-permute-start | bytes 392 | tf_op jit(solution)/shard_map/ppermute | solution.py:194
  11.2 32.0 %collective-permute-start.2 = (s32[8,4]{1,0:T(8,128)S(1)}, s32[8,4]{1,0:T(8,128)S(1)}, u32[]{:S(2)}, u32[]{:S(2)}) collective-permute-start(s32[8,4]{1,0:T(8,128)S(1)} %get-tuple-element.33), channel_id=1, source_target_pairs={{0,1},{1,2},{2,3},{3,4},{4,5},{5,6},{6,7},{7,8},{8,9},{9,10},{10,1... | collective-permute-start | bytes 392 | tf_op jit(solution)/shard_map/ppermute | solution.py:194
  15.1 29.5 %collective-permute-start.3 = (s32[8,4]{1,0:T(8,128)S(1)}, s32[8,4]{1,0:T(8,128)S(1)}, u32[]{:S(2)}, u32[]{:S(2)}) collective-permute-start(s32[8,4]{1,0:T(8,128)S(1)} %get-tuple-element.32), channel_id=1, source_target_pairs={{1,0},{2,1},{3,2},{4,3},{5,4},{6,5},{7,6},{8,7},{9,8},{10,9},{11,1... | collective-permute-start | bytes 392 | tf_op jit(solution)/shard_map/ppermute | solution.py:194
  18.7 28.8 %collective-permute-start.4 = (bf16[8,64,256]{2,1,0:T(8,128)(2,1)S(1)}, bf16[8,64,256]{2,1,0:T(8,128)(2,1)S(1)}, u32[]{:S(2)}, u32[]{:S(2)}) collective-permute-start(bf16[8,64,256]{2,1,0:T(8,128)(2,1)S(1)} %get-tuple-element.26), channel_id=1, source_target_pairs={{0,32},{32,64},{64,96},{96,128},{128,160},{160,192},{192,224},{1,3... | collective-permute-start | bytes 786440 | tf_op jit(solution)/shard_map/ppermute | solution.py:195
  21.3 95.2 %all-to-all-start = ((s32[32,1,2]{2,1,0:T(1,128)}), s32[32,1,2]{2,1,0:T(1,128)S(1)}, u32[]{:S(2)}, u32[]{:S(2)}) async-start(s32[32,1,2]{2,1,0:T(1,128)} %copy.109), calls=%async_computation | async-start | bytes 32768 | tf_op jit(solution)/shard_map/all_to_all | solution.py:203
  36.3 11.2 %collective-permute-start.5 = (bf16[8,64,256]{2,1,0:T(8,128)(2,1)S(1)}, bf16[8,64,256]{2,1,0:T(8,128)(2,1)S(1)}, u32[]{:S(2)}, u32[]{:S(2)}) collective-permute-start(bf16[8,64,256]{2,1,0:T(8,128)(2,1)S(1)} %get-tuple-element.28), channel_id=1, source_target_pairs={{32,0},{64,32},{96,64},{128,96},{160,128},{192,160},{224,192},{33,... | collective-permute-start | bytes 786440 | tf_op jit(solution)/shard_map/ppermute | solution.py:195
  39.7 8.8 %collective-permute-start.6 = (bf16[8,64,256]{2,1,0:T(8,128)(2,1)S(1)}, bf16[8,64,256]{2,1,0:T(8,128)(2,1)S(1)}, u32[]{:S(2)}, u32[]{:S(2)}) collective-permute-start(bf16[8,64,256]{2,1,0:T(8,128)(2,1)S(1)} %get-tuple-element.27), channel_id=1, source_target_pairs={{0,1},{1,2},{2,3},{3,4},{4,5},{5,6},{6,7},{7,8},{8,9},{9,10},{10,1... | collective-permute-start | bytes 786440 | tf_op jit(solution)/shard_map/ppermute | solution.py:195
  43.2 9.5 %collective-permute-start.7 = (bf16[8,64,256]{2,1,0:T(8,128)(2,1)S(1)}, bf16[8,64,256]{2,1,0:T(8,128)(2,1)S(1)}, u32[]{:S(2)}, u32[]{:S(2)}) collective-permute-start(bf16[8,64,256]{2,1,0:T(8,128)(2,1)S(1)} %get-tuple-element.29), channel_id=1, source_target_pairs={{1,0},{2,1},{3,2},{4,3},{5,4},{6,5},{7,6},{8,7},{9,8},{10,9},{11,1... | collective-permute-start | bytes 786440 | tf_op jit(solution)/shard_map/ppermute | solution.py:195
  116.6 114.5 %all-to-all-start.1 = ((bf16[32,128,512]{2,1,0:T(8,128)(2,1)}), bf16[32,128,512]{2,1,0:T(8,128)(2,1)}, u32[]{:S(2)}, u32[]{:S(2)}) async-start(bf16[32,128,512]{2,1,0:T(8,128)(2,1)} %bitcast.46), calls=%async_computation.1 | async-start | bytes 8388608 | tf_op jit(solution)/shard_map/all_to_all | solution.py:202

commit v2 on v1

--- a/solution.py
+++ b/solution.py
@@ -9,51 +9,24 @@
 
 NC = 4
 UNROLL = 8
-
-
-def coarse_kernel(cols, slots, masks, places, a_hbm, p_hbm, halo_hbm, out_ref, a_v, ext_v, g_v, acc, items, sems):
+BLOCKS = 144
+IDS = 256
+
+
+def load_operands(a_hbm, p_hbm, halo_hbm, a_v, ext_v, sems):
+    rows = p_hbm.shape[0]
+    return (
+        pltpu.make_async_copy(a_hbm, a_v, sems.at[0]),
+        pltpu.make_async_copy(p_hbm, ext_v.at[pl.ds(0, rows)], sems.at[1]),
+        pltpu.make_async_copy(halo_hbm, ext_v.at[pl.ds(rows, halo_hbm.shape[0])], sems.at[2]),
+    )
+
+
+def all_products(cols, a_v, ext_v, g_v):
     rows, width, span = a_v.shape
     ka = span // width
-    kp = ext_v.shape[2] // width
-    kq = ka * kp
-    nslots, _, outspan = out_ref.shape
-    kc = outspan // width
+    pairs = ext_v.shape[2] // (2 * width)
     pair = 2 * width
-    copy_a = pltpu.make_async_copy(a_hbm, a_v, sems.at[0])
-    copy_p = pltpu.make_async_copy(p_hbm, ext_v.at[pl.ds(0, rows)], sems.at[1])
-    copy_h = pltpu.make_async_copy(halo_hbm, ext_v.at[pl.ds(rows, halo_hbm.shape[0])], sems.at[2])
-    copy_a.start()
-    copy_p.start()
-    copy_h.start()
-
-    def clear(t, unused):
-        acc[pl.ds(t * kc, kc)] = jnp.zeros((kc, width, pair), jnp.float32)
-        return unused
-
-    lax.fori_loop(0, nslots, clear, 0)
-    acc[pl.ds(nslots * kc, 1)] = jnp.zeros((1, width, pair), jnp.float32)
-
-    def gather_items(im, count):
-        slot = slots[im]
-        head = im * 32
-
-        def more(state):
-            return state[0] != 0
-
-        def take(state):
-            mask, at = state
-            bit = 31 - lax.clz(mask)
-            items[at] = (head + bit) * 1024 + slot * kc + places[im * kq + bit]
-            return (mask - lax.shift_left(1, bit), at + 1)
-
-        return lax.while_loop(more, take, (masks[im], count))[1]
-
-    count = lax.fori_loop(0, rows * kp, gather_items, 0)
-    for u in range(UNROLL):
-        items[count + u] = nslots * kc
-    copy_a.wait()
-    copy_p.wait()
-    copy_h.wait()
 
     def products(i, unused):
         row = a_v[i]
@@ -62,11 +35,16 @@
             value = jnp.dot(row[:, k * width : (k + 1) * width], right, preferred_element_type=jnp.float32).astype(
                 jnp.bfloat16
             )
-            for h in range(kp // 2):
-                g_v[(i * ka + k) * (kp // 2) + h] = value[:, h * pair : (h + 1) * pair]
+            for h in range(pairs):
+                g_v[(i * ka + k) * pairs + h] = value[:, h * pair : (h + 1) * pair]
         return unused
 
     lax.fori_loop(0, rows, products, 0)
+
+
+def add_items(count, items, ext_v, g_v, acc, width, ka):
+    pair = 2 * width
+    kp = ext_v.shape[2] // width
     upper = lax.broadcasted_iota(jnp.int32, (width, pair), 1) // width
 
     def batch(b, unused):
@@ -85,20 +63,307 @@
             p = ext_v[i, :, pl.ds(pl.multiple_of((m // 2) * pair, pair), pair)]
             z = lax.dot_general(p, g, (((0,), (0,)), ((), ())), preferred_element_type=jnp.float32)
             z = jnp.where(m % 2 == 1, z[width:], z[:width])
-            found.append((target, z))
-        for target, z in found:
-            acc[target] = acc[target] + z
+            found.append((pl.ds(pl.multiple_of(target * width, width), width), z))
+        for where, z in found:
+            acc[where, :] = acc[where, :] + z
         return unused
 
     lax.fori_loop(0, (count + UNROLL - 1) // UNROLL, batch, 0)
+
+
+def clear_rows(acc, step):
+    def clear(n, unused):
+        acc[pl.ds(pl.multiple_of(n * step, step), step), :] = jnp.zeros((step, acc.shape[1]), jnp.float32)
+        return unused
+
+    lax.fori_loop(0, acc.shape[0] // step, clear, 0)
+
+
+def packed_kernel(
+    cols, slots, masks, places, bases, a_hbm, p_hbm, halo_hbm, out_ref, ids_ref, count_ref, a_v, ext_v, g_v, acc, items, index, sems
+):
+    rows, width, span = a_v.shape
+    ka = span // width
+    kp = ext_v.shape[2] // width
+    kq = ka * kp
+    pair = 2 * width
+    half = width // 2
+    kc = index.shape[0] // bases.shape[0]
+    copies = load_operands(a_hbm, p_hbm, halo_hbm, a_v, ext_v, sems)
+    for copy in copies:
+        copy.start()
+    clear_rows(acc, 16 * width)
+
+    def unset(n, unused):
+        for u in range(8):
+            index[n * 8 + u] = -1
+        return unused
+
+    lax.fori_loop(0, index.shape[0] // 8, unset, 0)
+
+    def no_id(n, unused):
+        for u in range(8):
+            ids_ref[0, n * 8 + u] = -1
+        return unused
+
+    lax.fori_loop(0, ids_ref.shape[1] // 8, no_id, 0)
+
+    def gather_items(im, state):
+        slot = slots[im]
+        base = bases[slot]
+        head = im * 32
+
+        def more(state):
+            return state[0] != 0
+
+        def take(state):
+            mask, at, blocks = state
+            bit = 31 - lax.clz(mask)
+            place = places[im * kq + bit]
+            old = index[slot * kc + place]
+            fresh = old < 0
+            block = jnp.where(fresh, blocks, old)
+            index[slot * kc + place] = block
+            kept = jnp.minimum(block, BLOCKS)
+            ids_ref[0, kept] = base + place
+            items[at] = (head + bit) * 1024 + kept
+            return (mask - lax.shift_left(1, bit), at + 1, blocks + fresh.astype(jnp.int32))
+
+        return lax.while_loop(more, take, (masks[im],) + state)[1:]
+
+    count, blocks = lax.fori_loop(0, rows * kp, gather_items, (0, 0))
+    for u in range(UNROLL):
+        items[count + u] = BLOCKS
+    count_ref[0] = blocks
+    for copy in copies:
+        copy.wait()
+    all_products(cols, a_v, ext_v, g_v)
+    add_items(count, items, ext_v, g_v, acc, width, ka)
+    lower = lax.broadcasted_iota(jnp.int32, (16, pair), 1) < width
+
+    def finish(n, unused):
+        for r in range(half):
+            one = acc[pl.ds(n * 16 * width + r, 16, stride=width), :]
+            two = acc[pl.ds(n * 16 * width + half + r, 16, stride=width), :]
+            one = one + pltpu.roll(one, width, 1)
+            two = two + pltpu.roll(two, width, 1)
+            out_ref[r, pl.ds(pl.multiple_of(n * 16, 16), 16), :] = jnp.where(lower, one, two).astype(jnp.bfloat16)
+        return unused
+
+    lax.fori_loop(0, BLOCKS // 16, finish, 0)
+
+
+def packed_partials(cols, slots, masks, places, bases, a_blocks, p_blocks, halo, kc):
+    rows, width, span = a_blocks.shape
+    kp = p_blocks.shape[2] // width
+    ka = span // width
+    extended = rows + halo.shape[0]
+    smem = pl.BlockSpec(memory_space=pltpu.SMEM)
+    vmem = pl.BlockSpec(memory_space=pltpu.VMEM)
+    hbm = pl.BlockSpec(memory_space=pl.ANY)
+    return pl.pallas_call(
+        packed_kernel,
+        out_shape=(
+            jax.ShapeDtypeStruct((width // 2, BLOCKS, 2 * width), jnp.bfloat16),
+            jax.ShapeDtypeStruct((1, IDS), jnp.int32),
+            jax.ShapeDtypeStruct((1,), jnp.int32),
+        ),
+        in_specs=[smem, smem, smem, smem, smem, hbm, hbm, hbm],
+        out_specs=(vmem, smem, smem),
+        scratch_shapes=[
+            pltpu.VMEM((rows, width, span), jnp.bfloat16),
+            pltpu.VMEM((extended, width, kp * width), jnp.bfloat16),
+            pltpu.VMEM((rows * ka * (kp // 2), width, 2 * width), jnp.bfloat16),
+            pltpu.VMEM(((BLOCKS + 16) * width, 2 * width), jnp.float32),
+            pltpu.SMEM((rows * kp * ka * kp + UNROLL,), jnp.int32),
+            pltpu.SMEM((bases.shape[0] * kc,), jnp.int32),
+            pltpu.SemaphoreType.DMA((3,)),
+        ],
+        compiler_params=pltpu.CompilerParams(vmem_limit_bytes=48 * 2**20),
+        name="packed_partials",
+    )(cols, slots, masks, places, bases, a_blocks, p_blocks, halo)
+
+
+def exchange_kernel(count, *refs):
+    sends, takes = refs[:count], refs[count : 2 * count]
+    here_sem, send_sem, take_sem = refs[2 * count :]
+    me = lax.axis_index("row")
+    n = lax.axis_size("row")
+    barrier = pltpu.get_barrier_semaphore()
+
+    def greet(o, unused):
+        pl.semaphore_signal(
+            barrier, inc=1, device_id={"row": lax.rem(me + o, n)}, device_id_type=pl.DeviceIdType.MESH
+        )
+        return unused
+
+    lax.fori_loop(1, n, greet, 0)
+    pl.semaphore_wait(barrier, n - 1)
+
+    def source(x, to):
+        return sends[x].at[to] if sends[x].shape[0] == n else sends[x].at[0]
+
+    def remote(x, o):
+        to = lax.rem(me + o, n)
+        return pltpu.make_async_remote_copy(
+            src_ref=source(x, to),
+            dst_ref=takes[x].at[me],
+            send_sem=send_sem.at[x, o],
+            recv_sem=take_sem.at[x, o],
+            device_id={"row": to},
+            device_id_type=pl.DeviceIdType.MESH,
+        )
+
+    def arriving(x, o):
+        came = lax.rem(me + n - o, n)
+        return pltpu.make_async_remote_copy(
+            src_ref=source(x, came),
+            dst_ref=takes[x].at[came],
+            send_sem=send_sem.at[x, o],
+            recv_sem=take_sem.at[x, o],
+            device_id={"row": came},
+            device_id_type=pl.DeviceIdType.MESH,
+        )
+
+    def begin(o, unused):
+        for x in range(count):
+            remote(x, o).start()
+        return unused
+
+    lax.fori_loop(1, n, begin, 0)
+    for x in range(count):
+        pltpu.make_async_copy(source(x, me), takes[x].at[me], here_sem.at[x]).start()
+
+    def end(o, unused):
+        for x in range(count):
+            remote(x, o).wait_send()
+            arriving(x, o).wait_recv()
+        return unused
+
+    lax.fori_loop(1, n, end, 0)
+    for x in range(count):
+        pltpu.make_async_copy(source(x, me), takes[x].at[me], here_sem.at[x]).wait()
+
+
+def exchange(arrays, n, collective_id):
+    hbm = pl.BlockSpec(memory_space=pl.ANY)
+    count = len(arrays)
+    return pl.pallas_call(
+        functools.partial(exchange_kernel, count),
+        out_shape=tuple(jax.ShapeDtypeStruct((n,) + x.shape[1:], x.dtype) for x in arrays),
+        in_specs=[hbm] * count,
+        out_specs=(hbm,) * count,
+        scratch_shapes=[
+            pltpu.SemaphoreType.DMA((count,)),
+            pltpu.SemaphoreType.DMA((count, n)),
+            pltpu.SemaphoreType.DMA((count, n)),
+        ],
+        compiler_params=pltpu.CompilerParams(collective_id=collective_id, has_side_effects=True),
+        name="exchange",
+    )(*arrays)
+
+
+def relay_kernel(ids_ref, parts_ref, out_ref, acc):
+    n, blocks, lanes = parts_ref.shape
+    targets = acc.shape[0]
+    acc[...] = jnp.zeros_like(acc)
+    order = lax.broadcasted_iota(jnp.int32, (targets, blocks), 0)
+
+    def one(d, unused):
+        hot = jnp.where(order == ids_ref[d, :, :blocks], 1.0, 0.0).astype(jnp.bfloat16)
+        acc[...] += jnp.dot(hot, parts_ref[d], preferred_element_type=jnp.float32)
+        return unused
+
+    lax.fori_loop(0, n, one, 0)
+    out_ref[...] = acc[...].astype(jnp.bfloat16)
+
+
+def relay_sums(ids, parts, targets):
+    vmem = pl.BlockSpec(memory_space=pltpu.VMEM)
+    return pl.pallas_call(
+        relay_kernel,
+        out_shape=jax.ShapeDtypeStruct((targets, parts.shape[2]), jnp.bfloat16),
+        in_specs=[vmem, vmem],
+        out_specs=vmem,
+        scratch_shapes=[pltpu.VMEM((targets, parts.shape[2]), jnp.float32)],
+        compiler_params=pltpu.CompilerParams(vmem_limit_bytes=32 * 2**20),
+        name="relay_sums",
+    )(ids, parts)
+
+
+def assemble_kernel(pieces_ref, out_ref, wide):
+    n, targets, pair = pieces_ref.shape
+    owned, width, outspan = out_ref.shape
+    half = width // 2
+    kc = targets // owned
+    lower = lax.broadcasted_iota(jnp.int32, (half, pair), 1) < half * 2
+    wide[...] = pieces_ref[...].reshape(n * targets, pair).astype(jnp.float32)
+    for g in range(owned):
+        for h in range(kc // 2):
+            one = wide[pl.ds(g * kc + 2 * h, n, stride=targets), :]
+            two = wide[pl.ds(g * kc + 2 * h + 1, n, stride=targets), :]
+            span = slice(h * pair, (h + 1) * pair)
+            out_ref[g, :half, span] = jnp.where(lower, one, pltpu.roll(two, width, 1))
+            out_ref[g, half:, span] = jnp.where(lower, pltpu.roll(one, width, 1), two)
+
+
+def assemble(pieces, width, kc):
+    vmem = pl.BlockSpec(memory_space=pltpu.VMEM)
+    n, targets, pair = pieces.shape
+    return pl.pallas_call(
+        assemble_kernel,
+        out_shape=jax.ShapeDtypeStruct((NC, width, kc * width), jnp.float32),
+        in_specs=[vmem],
+        out_specs=vmem,
+        scratch_shapes=[pltpu.VMEM((n * targets, pair), jnp.float32)],
+        name="assemble",
+    )(pieces)
+
+
+def coarse_kernel(cols, slots, masks, places, a_hbm, p_hbm, halo_hbm, out_ref, a_v, ext_v, g_v, acc, items, sems):
+    rows, width, span = a_v.shape
+    ka = span // width
+    kp = ext_v.shape[2] // width
+    kq = ka * kp
+    nslots, _, outspan = out_ref.shape
+    kc = outspan // width
+    pair = 2 * width
+    copies = load_operands(a_hbm, p_hbm, halo_hbm, a_v, ext_v, sems)
+    for copy in copies:
+        copy.start()
+    clear_rows(acc, width)
+
+    def gather_items(im, count):
+        slot = slots[im]
+        head = im * 32
+
+        def more(state):
+            return state[0] != 0
+
+        def take(state):
+            mask, at = state
+            bit = 31 - lax.clz(mask)
+            items[at] = (head + bit) * 1024 + slot * kc + places[im * kq + bit]
+            return (mask - lax.shift_left(1, bit), at + 1)
+
+        return lax.while_loop(more, take, (masks[im], count))[1]
+
+    count = lax.fori_loop(0, rows * kp, gather_items, 0)
+    for u in range(UNROLL):
+        items[count + u] = nslots * kc
+    for copy in copies:
+        copy.wait()
+    all_products(cols, a_v, ext_v, g_v)
+    add_items(count, items, ext_v, g_v, acc, width, ka)
+    lower = lax.broadcasted_iota(jnp.int32, (width, pair), 1) < width
 
     def finish(t, unused):
         for h in range(kc // 2):
-            one = acc[t * kc + 2 * h]
-            two = acc[t * kc + 2 * h + 1]
+            one = acc[pl.ds(pl.multiple_of((t * kc + 2 * h) * width, width), width), :]
+            two = acc[pl.ds(pl.multiple_of((t * kc + 2 * h + 1) * width, width), width), :]
             one = one + pltpu.roll(one, width, 1)
             two = two + pltpu.roll(two, width, 1)
-            out_ref[t, :, h * pair : (h + 1) * pair] = jnp.where(upper == 0, one, two).astype(jnp.bfloat16)
+            out_ref[t, :, h * pair : (h + 1) * pair] = jnp.where(lower, one, two).astype(jnp.bfloat16)
         return unused
 
     lax.fori_loop(0, nslots, finish, 0)
@@ -120,7 +385,7 @@
             pltpu.VMEM((rows, width, span), jnp.bfloat16),
             pltpu.VMEM((extended, width, kp * width), jnp.bfloat16),
             pltpu.VMEM((rows * ka * (kp // 2), width, 2 * width), jnp.bfloat16),
-            pltpu.VMEM((nslots * kc + 1, width, 2 * width), jnp.float32),
+            pltpu.VMEM(((nslots * kc + 1) * width, 2 * width), jnp.float32),
             pltpu.SMEM((rows * kp * ka * kp + UNROLL,), jnp.int32),
             pltpu.SemaphoreType.DMA((3,)),
         ],
@@ -195,13 +460,23 @@
     halo = jnp.concatenate([lax.ppermute(sent_blocks[n], axis, way) for n, axis, way in routes], 0)
     ext_ids = jnp.concatenate([coarse_ids, halo_ids], 0)
     places, masks = find_matches(ext_ids, a_cols, p_slots, patterns)
-    partial = coarse_partials(
-        a_cols.reshape(-1), p_slots.reshape(-1), masks.reshape(-1), places.reshape(-1), a_blocks, p_blocks, halo, slots, kc
-    )
     width = a_blocks.shape[1]
-    parts = lax.all_to_all(partial.reshape(nrow, cap * width, kc * width), "row", 0, 0)
-    ids = lax.all_to_all(touched[0], "row", 0, 0)
-    return sum_parts(ids.reshape(-1), parts.reshape(slots, width, kc * width))
+    lists_in = (a_cols.reshape(-1), p_slots.reshape(-1), masks.reshape(-1), places.reshape(-1))
+    bases = (jnp.arange(slots, dtype=jnp.int32) // cap * NC + table) * kc
+    packed, ids, blocks = packed_partials(*lists_in, bases, a_blocks, p_blocks, halo, kc)
+    most = lax.pmax(blocks[0], ("slab", "row"))
+    parts, part_ids = exchange((packed, ids.reshape(1, 1, IDS)), nrow, 0)
+    sums = relay_sums(part_ids, parts, nrow * NC * kc)
+    (pieces,) = exchange((sums.reshape(nrow, NC * kc, 2 * width),), nrow, 1)
+    result = assemble(pieces, width, kc)
+
+    def whole(unused):
+        partial = coarse_partials(*lists_in, a_blocks, p_blocks, halo, slots, kc)
+        parts = lax.all_to_all(partial.reshape(nrow, cap * width, kc * width), "row", 0, 0)
+        owners = lax.all_to_all(touched[0], "row", 0, 0)
+        return sum_parts(owners.reshape(-1), parts.reshape(slots, width, kc * width))
+
+    return lax.cond(most > BLOCKS, whole, lambda x: x, result)
 
 
 def solution(mesh):

time: 238 us -> 257 us (1.080)
  waiting for transfers between devices: 92 us -> 4.75 us
  blocking collectives: 0 us -> 78.5 us
  Pallas kernels: 67.2 us -> 129 us
  starting transfers between devices: 60.4 us -> 22.9 us
  local copies, waits for them, and re-layouts: 10.2 us -> 14.5 us
    all_to_all x2 -> x0, waiting for transfers between devices: 86.8 us -> none  [the longest x1 86.8 us: per_device(): lax.all_to_all(partial.reshape(nrow, cap * width, kc * width), 'row', 0, 0)]
    pmax x0 -> x1, blocking collectives: none -> 78.5 us  [per_device(): most = lax.pmax(blocks[0], ('slab', 'row'))]
    pallas_call x2 -> x5, Pallas kernels: 67.2 us -> 129 us  [the longest x2 68.9 us: exchange(): pl.pallas_call(functools.partial(exchange_kernel, count), out_shape=tuple...]
    all_to_all x2 -> x0, starting transfers between devices: 39.7 us -> none  [the longest x1 26.5 us: per_device(): lax.all_to_all(partial.reshape(nrow, cap * width, kc * width), 'row', 0, 0)]
    unnamed x10 -> x25, local copies, waits for them, and re-layouts: 1.78 us -> 7.99 us
  transfers between devices with their start and end apart: 10 -> 8, of which waited for: 3 -> 2; matrix products, arithmetic and copies ran while one was open for 4% -> 3% of each run, Pallas kernels for 27% -> 0%
where the time goes in v2:
time: 257 us; the launch traced here: 254 us
  Pallas kernels  129 us (50%)
  blocking collectives  78.5 us (31%)
  starting transfers between devices  22.9 us (9%)
  local copies, waits for them, and re-layouts  14.5 us (6%)
  waiting for transfers between devices  4.75 us (2%)
  other arithmetic  3.83 us (1%)
    pmax x1, blocking collectives, per_device(): most = lax.pmax(blocks[0], ('slab', 'row'))  78.5 us
    pallas_call x2, Pallas kernels, exchange(): pl.pallas_call(functools.partial(exchange_kernel, count), out_shape=tuple...  68.9 us
    pallas_call x1, Pallas kernels, packed_partials(): pl.pallas_call(packed_kernel, out_shape=(jax.ShapeDtypeStruct((width // 2...  48 us
    ppermute x4, starting transfers between devices, per_device(): lax.ppermute(sent_blocks[n], axis, way)  12.2 us
    ppermute x4, starting transfers between devices, per_device(): lax.ppermute(sent_ids[n], axis, way)  10.7 us
    pallas_call x1, Pallas kernels, relay_sums(): pl.pallas_call(relay_kernel, out_shape=jax.ShapeDtypeStruct((targets, par...  9.5 us
    unnamed x25, local copies, waits for them, and re-layouts  7.99 us
  transfers between devices with their start and end apart: 8, of which 2 were waited for; matrix products, arithmetic and copies ran while one was open for 3% of the time, Pallas kernels for 0%

profile of v2, /device:TPU:16, one launch (start us, length us, event | category | flops | bytes accessed | tf_op | source)
XLA Modules:
  0.0 253.9 jit_solution(12534671653423982294)
XLA Ops:
  0.0 0.8 copy.121
  0.8 0.3 slice_reduce_fusion
  1.1 0.8 copy.114
  1.9 0.1 reshape.76
  2.0 1.5 select_reduce_fusion.13
  3.5 0.7 fusion.3
  4.2 0.1 copy.115
  4.3 0.7 compare_select_fusion
  4.9 0.1 reshape.83
  5.0 0.6 gather_fusion
  5.6 1.9 collective-permute-start
  7.5 3.6 %collective-permute-start.1 = (s32[8,4]{1,0:T(8,128)S(1)}, s32[8,4]{1,0:T(8,128)S(1)}, u32[]{:S(2)}, u32[]{:S(2)}) collective-permute-start(s32[8,4]{1,0:T(8,128)S(1)} %get-tuple-element.73), channel_id=1, source_target_pairs={{32,0},{64,32},{96,64},{128,96},{160,128},{192,160},{224,192},{33,... | collective-permute-start | bytes 392 | tf_op jit(solution)/shard_map/ppermute | solution.py:459
  11.2 3.8 %collective-permute-start.2 = (s32[8,4]{1,0:T(8,128)S(1)}, s32[8,4]{1,0:T(8,128)S(1)}, u32[]{:S(2)}, u32[]{:S(2)}) collective-permute-start(s32[8,4]{1,0:T(8,128)S(1)} %get-tuple-element.72), channel_id=1, source_target_pairs={{0,1},{1,2},{2,3},{3,4},{4,5},{5,6},{6,7},{7,8},{8,9},{9,10},{10,1... | collective-permute-start | bytes 392 | tf_op jit(solution)/shard_map/ppermute | solution.py:459
  15.0 0.0 copy-start.6
  15.0 0.0 copy-start.7
  15.0 1.3 collective-permute-start.3
  16.3 2.2 gather_fusion.1
  18.6 0.9 fusion.8
  19.5 2.0 collective-permute-start.4
  21.5 0.0 copy-done.6
  21.5 0.1 copy.113
  21.6 0.1 copy.112
  21.7 0.1 reshape.74.cols
  21.9 0.1 reshape.75.slots
  22.0 0.0 collective-permute-done
  22.0 3.6 %collective-permute-start.5 = (bf16[8,64,256]{2,1,0:T(8,128)(2,1)}, bf16[8,64,256]{2,1,0:T(8,128)(2,1)}, u32[]{:S(2)}, u32[]{:S(2)}) collective-permute-start(bf16[8,64,256]{2,1,0:T(8,128)(2,1)} %get-tuple-element.67), channel_id=1, source_target_pairs={{32,0},{64,32},{96,64},{128,96},{160,128},{192,160},{224,192},{33,... | collective-permute-start | bytes 786440 | tf_op jit(solution)/shard_map/ppermute | solution.py:460
  25.7 0.1 copy.116
  25.8 0.0 collective-permute-done.1
  25.8 5.2 %collective-permute-start.6 = (bf16[8,64,256]{2,1,0:T(8,128)(2,1)}, bf16[8,64,256]{2,1,0:T(8,128)(2,1)}, u32[]{:S(2)}, u32[]{:S(2)}) collective-permute-start(bf16[8,64,256]{2,1,0:T(8,128)(2,1)} %get-tuple-element.66), channel_id=1, source_target_pairs={{0,1},{1,2},{2,3},{3,4},{4,5},{5,6},{6,7},{7,8},{8,9},{9,10},{10,1... | collective-permute-start | bytes 786440 | tf_op jit(solution)/shard_map/ppermute | solution.py:460
  31.0 0.1 copy.117
  31.1 0.0 collective-permute-done.2
  31.1 1.3 collective-permute-start.7
  32.4 0.1 copy.118
  32.5 0.0 collective-permute-done.3
  32.5 0.1 copy.119
  32.6 0.1 concatenate.6
  32.7 0.7 select_reduce_fusion.4
  33.4 0.2 select_reduce_fusion
  33.6 0.1 broadcast_add_fusion
  33.7 0.1 copy.131
  33.8 0.2 sub.20.places
  34.0 0.1 copy.130
  34.1 0.1 reshape.78.masks
  34.2 0.0 collective-permute-done.4
  34.2 0.0 collective-permute-done.5
  34.2 1.0 constant_dynamic-update-slice_fusion.2
  35.2 0.8 collective-permute-done.6
  36.0 1.0 constant_dynamic-update-slice_fusion.1
  37.0 3.9 %collective-permute-done.7 = bf16[8,64,256]{2,1,0:T(8,128)(2,1)} collective-permute-done((bf16[8,64,256]{2,1,0:T(8,128)(2,1)}, bf16[8,64,256]{2,1,0:T(8,128)(2,1)}, u32[]{:S(2)}, u32[]{:S(2)}) %collective-permute-start.7) | collective-permute-done | bytes 262176 | tf_op jit(solution)/shard_map/ppermute | solution.py:460
  40.9 1.0 constant_dynamic-update-slice_fusion.halo_hbm
  41.9 0.0 copy-done.5
  41.9 48.0 %packed_partials.1 = (bf16[32,144,128]{2,1,0:T(8,128)(2,1)S(1)}, s32[1,256]{1,0:T(1,128)S(1)}, s32[1]{0:T(128)}) custom-call(s32[448]{0:T(512)S(1)} %reshape.74.cols, s32[256]{0:T(256)S(1)} %reshape.75.slots, s32[256]{0:T(256)S(1)} %reshape.78.masks, s32[7168]{0:T(1024)S(1)} %sub.20.places, s32[64]{0:T(128)S(1)} %fusion.7.bases, bf16[64,64,448]{2,1,0:T(8,128)(2,1)} %a_hbm.1, ...), custom_call_target="tpu_custom_call" | custom-call | tf_op jit(solution)/shard_map/packed_partials/pallas_call | solution.py:164
  89.9 0.0 copy-start.1
  89.9 1.0 copy-done.1
  90.9 0.6 copy-done.4
  91.4 55.5 %exchange.2 = (bf16[32,144,128]{2,1,0:T(8,128)(2,1)}, s32[32,1,256]{2,1,0:T(1,128)}) custom-call(bf16[32,144,128]{2,1,0:T(8,128)(2,1)} %copy-done.1, s32[1,1,256]{2,1,0:T(1,128)} %bitcast.50), custom_call_target="tpu_custom_call" | custom-call | tf_op jit(solution)/shard_map/exchange/pallas_call | solution.py:251
  147.0 1.3 copy-done
  148.2 0.8 copy-done.3
  149.0 9.5 %relay_sums.1 = bf16[1024,128]{1,0:T(8,128)(2,1)S(1)} custom-call(s32[32,1,256]{2,1,0:T(1,128)S(1)} %copy-done.3, bf16[32,144,128]{2,1,0:T(8,128)(2,1)S(1)} %copy-done), custom_call_target="tpu_custom_call" | custom-call | tf_op jit(solution)/shard_map/relay_sums/pallas_call | solution.py:283
  158.5 0.0 copy-start.2
  158.5 0.7 copy-done.2
  159.2 13.3 %exchange.3.pieces_ref = bf16[32,32,128]{2,1,0:T(8,128)(2,1)} custom-call(bf16[32,32,128]{2,1,0:T(8,128)(2,1)} %bitcast.49), custom_call_target="tpu_custom_call" | custom-call | tf_op jit(solution)/shard_map/exchange/pallas_call | solution.py:251
  172.6 2.2 assemble.1
  174.7 78.5 %pmax.7 = s32[]{:T(128)} all-reduce(s32[]{:T(128)} %bitcast.29), channel_id=1, replica_groups=mesh['slab'=8,'row'=32] {'slab','row'}, use_global_device_ids=true, to_apply=%region_15.16 | all-reduce | flops 1 | bytes 8 | tf_op jit(solution)/shard_map/pmax | solution.py:467
  (19 shorter events, 0.1 us)
Async XLA Ops:
  5.6 16.4 %collective-permute-start = (s32[8,4]{1,0:T(8,128)S(1)}, s32[8,4]{1,0:T(8,128)S(1)}, u32[]{:S(2)}, u32[]{:S(2)}) collective-permute-start(s32[8,4]{1,0:T(8,128)S(1)} %get-tuple-element.74), channel_id=1, source_target_pairs={{0,32},{32,64},{64,96},{96,128},{128,160},{160,192},{192,224},{1,3... | collective-permute-start | bytes 392 | tf_op jit(solution)/shard_map/ppermute | solution.py:459
  7.5 18.2 %collective-permute-start.1 = (s32[8,4]{1,0:T(8,128)S(1)}, s32[8,4]{1,0:T(8,128)S(1)}, u32[]{:S(2)}, u32[]{:S(2)}) collective-permute-start(s32[8,4]{1,0:T(8,128)S(1)} %get-tuple-element.73), channel_id=1, source_target_pairs={{32,0},{64,32},{96,64},{128,96},{160,128},{192,160},{224,192},{33,... | collective-permute-start | bytes 392 | tf_op jit(solution)/shard_map/ppermute | solution.py:459
  11.2 19.9 %collective-permute-start.2 = (s32[8,4]{1,0:T(8,128)S(1)}, s32[8,4]{1,0:T(8,128)S(1)}, u32[]{:S(2)}, u32[]{:S(2)}) collective-permute-start(s32[8,4]{1,0:T(8,128)S(1)} %get-tuple-element.72), channel_id=1, source_target_pairs={{0,1},{1,2},{2,3},{3,4},{4,5},{5,6},{6,7},{7,8},{8,9},{9,10},{10,1... | collective-permute-start | bytes 392 | tf_op jit(solution)/shard_map/ppermute | solution.py:459
  15.0 6.5 %copy-start.6 = (s32[64,4]{0,1:T(4,128)S(1)}, s32[64,4]{0,1:T(4,128)}, u32[]{:S(2)}) copy-start(s32[64,4]{0,1:T(4,128)} %param.12) | copy-start | bytes 3076
  15.0 6.6 %copy-start.7 = (s32[64,7]{0,1:T(8,128)S(1)}, s32[64,7]{0,1:T(8,128)}, u32[]{:S(2)}) copy-start(s32[64,7]{0,1:T(8,128)} %param.11) | copy-start | bytes 5380
  15.0 17.4 %collective-permute-start.3 = (s32[8,4]{1,0:T(8,128)S(1)}, s32[8,4]{1,0:T(8,128)S(1)}, u32[]{:S(2)}, u32[]{:S(2)}) collective-permute-start(s32[8,4]{1,0:T(8,128)S(1)} %get-tuple-element.71), channel_id=1, source_target_pairs={{1,0},{2,1},{3,2},{4,3},{5,4},{6,5},{7,6},{8,7},{9,8},{10,9},{11,1... | collective-permute-start | bytes 392 | tf_op jit(solution)/shard_map/ppermute | solution.py:459
  19.4 22.4 %copy-start.5 = (bf16[64,64,256]{2,1,0:T(8,128)(2,1)S(1)}, bf16[64,64,256]{2,1,0:T(8,128)(2,1)}, u32[]{:S(2)}) copy-start(bf16[64,64,256]{2,1,0:T(8,128)(2,1)} %p_hbm.1) | copy-start | bytes 6291460
  19.5 14.7 %collective-permute-start.4 = (bf16[8,64,256]{2,1,0:T(8,128)(2,1)S(1)}, bf16[8,64,256]{2,1,0:T(8,128)(2,1)S(1)}, u32[]{:S(2)}, u32[]{:S(2)}) collective-permute-start(bf16[8,64,256]{2,1,0:T(8,128)(2,1)S(1)} %get-tuple-element.68), channel_id=1, source_target_pairs={{0,32},{32,64},{64,96},{96,128},{128,160},{160,192},{192,224},{1,3... | collective-permute-start | bytes 786440 | tf_op jit(solution)/shard_map/ppermute | solution.py:460
  22.0 12.2 %collective-permute-start.5 = (bf16[8,64,256]{2,1,0:T(8,128)(2,1)}, bf16[8,64,256]{2,1,0:T(8,128)(2,1)}, u32[]{:S(2)}, u32[]{:S(2)}) collective-permute-start(bf16[8,64,256]{2,1,0:T(8,128)(2,1)} %get-tuple-element.67), channel_id=1, source_target_pairs={{32,0},{64,32},{96,64},{128,96},{160,128},{192,160},{224,192},{33,... | collective-permute-start | bytes 786440 | tf_op jit(solution)/shard_map/ppermute | solution.py:460
  25.8 10.2 %collective-permute-start.6 = (bf16[8,64,256]{2,1,0:T(8,128)(2,1)}, bf16[8,64,256]{2,1,0:T(8,128)(2,1)}, u32[]{:S(2)}, u32[]{:S(2)}) collective-permute-start(bf16[8,64,256]{2,1,0:T(8,128)(2,1)} %get-tuple-element.66), channel_id=1, source_target_pairs={{0,1},{1,2},{2,3},{3,4},{4,5},{5,6},{6,7},{7,8},{8,9},{9,10},{10,1... | collective-permute-start | bytes 786440 | tf_op jit(solution)/shard_map/ppermute | solution.py:460
  31.1 9.8 %collective-permute-start.7 = (bf16[8,64,256]{2,1,0:T(8,128)(2,1)}, bf16[8,64,256]{2,1,0:T(8,128)(2,1)}, u32[]{:S(2)}, u32[]{:S(2)}) collective-permute-start(bf16[8,64,256]{2,1,0:T(8,128)(2,1)} %get-tuple-element.65), channel_id=1, source_target_pairs={{1,0},{2,1},{3,2},{4,3},{5,4},{6,5},{7,6},{8,7},{9,8},{10,9},{11,1... | collective-permute-start | bytes 786440 | tf_op jit(solution)/shard_map/ppermute | solution.py:460
  89.9 1.0 copy-start.1
  90.9 0.6 copy-start.4
  91.4 162.5 %copy-start.8 = (s32[1,32,2]{1,2,0:T(2,128)S(1)}, s32[1,32,2]{1,2,0:T(2,128)}, u32[]{:S(2)}) copy-start(s32[1,32,2]{1,2,0:T(2,128)} %param.13) | copy-start | bytes 772
  147.0 1.3 copy-start
  148.2 0.8 copy-start.3
  158.5 0.7 copy-start.2

commit v3 on v2

--- a/solution.py
+++ b/solution.py
@@ -8,7 +8,7 @@
 from jax.sharding import PartitionSpec as P
 
 NC = 4
-UNROLL = 8
+UNROLL = 16
 BLOCKS = 144
 IDS = 256
 
@@ -22,7 +22,7 @@
     )
 
 
-def all_products(cols, a_v, ext_v, g_v):
+def all_products(cols, a_v, ext_v, g_v, pt_v):
     rows, width, span = a_v.shape
     ka = span // width
     pairs = ext_v.shape[2] // (2 * width)
@@ -30,6 +30,9 @@
 
     def products(i, unused):
         row = a_v[i]
+        turned = ext_v[i].T
+        for m in range(2 * pairs):
+            pt_v[i * 2 * pairs + m] = turned[m * width : (m + 1) * width, :]
         for k in range(ka):
             right = ext_v[cols[i * ka + k]]
             value = jnp.dot(row[:, k * width : (k + 1) * width], right, preferred_element_type=jnp.float32).astype(
@@ -42,33 +45,26 @@
     lax.fori_loop(0, rows, products, 0)
 
 
-def add_items(count, items, ext_v, g_v, acc, width, ka):
+def add_items(count, items, pt_v, g_v, acc, width, ka, kp):
     pair = 2 * width
-    kp = ext_v.shape[2] // width
-    upper = lax.broadcasted_iota(jnp.int32, (width, pair), 1) // width
+    upper = (lax.broadcasted_iota(jnp.int32, (width, pair), 1) >= width).astype(jnp.int32)
 
     def batch(b, unused):
         found = []
         for u in range(UNROLL):
             word = items[b * UNROLL + u]
-            target = word % 1024
-            bit = (word // 1024) % 32
-            im = word // 32768
-            i = im // kp
-            m = im % kp
-            k = bit // kp
-            q = bit % kp
-            g = g_v[(i * ka + k) * (kp // 2) + q // 2]
-            g = jnp.where(upper == q % 2, g, jnp.zeros_like(g))
-            p = ext_v[i, :, pl.ds(pl.multiple_of((m // 2) * pair, pair), pair)]
-            z = lax.dot_general(p, g, (((0,), (0,)), ((), ())), preferred_element_type=jnp.float32)
-            z = jnp.where(m % 2 == 1, z[width:], z[:width])
+            target = word & 1023
+            bit = lax.shift_right_logical(word, 10) & 31
+            im = lax.shift_right_logical(word, 15)
+            g = g_v[lax.shift_right_logical(im, kp.bit_length() - 1) * (ka * kp // 2) + lax.shift_right_logical(bit, 1)]
+            g = jnp.where(upper == (bit & 1), g, jnp.zeros_like(g))
+            z = jnp.dot(pt_v[im], g, preferred_element_type=jnp.float32)
             found.append((pl.ds(pl.multiple_of(target * width, width), width), z))
         for where, z in found:
             acc[where, :] = acc[where, :] + z
         return unused
 
-    lax.fori_loop(0, (count + UNROLL - 1) // UNROLL, batch, 0)
+    lax.fori_loop(0, lax.div(count + UNROLL - 1, UNROLL), batch, 0)
 
 
 def clear_rows(acc, step):
@@ -80,7 +76,7 @@
 
 
 def packed_kernel(
-    cols, slots, masks, places, bases, a_hbm, p_hbm, halo_hbm, out_ref, ids_ref, count_ref, a_v, ext_v, g_v, acc, items, index, sems
+    cols, slots, masks, places, bases, a_hbm, p_hbm, halo_hbm, out_ref, ids_ref, a_v, ext_v, g_v, pt_v, acc, items, index, sems
 ):
     rows, width, span = a_v.shape
     ka = span // width
@@ -134,11 +130,11 @@
     count, blocks = lax.fori_loop(0, rows * kp, gather_items, (0, 0))
     for u in range(UNROLL):
         items[count + u] = BLOCKS
-    count_ref[0] = blocks
+    ids_ref[0, IDS - 1] = blocks
     for copy in copies:
         copy.wait()
-    all_products(cols, a_v, ext_v, g_v)
-    add_items(count, items, ext_v, g_v, acc, width, ka)
+    all_products(cols, a_v, ext_v, g_v, pt_v)
+    add_items(count, items, pt_v, g_v, acc, width, ka, kp)
     lower = lax.broadcasted_iota(jnp.int32, (16, pair), 1) < width
 
     def finish(n, unused):
@@ -166,14 +162,14 @@
         out_shape=(
             jax.ShapeDtypeStruct((width // 2, BLOCKS, 2 * width), jnp.bfloat16),
             jax.ShapeDtypeStruct((1, IDS), jnp.int32),
-            jax.ShapeDtypeStruct((1,), jnp.int32),
         ),
         in_specs=[smem, smem, smem, smem, smem, hbm, hbm, hbm],
-        out_specs=(vmem, smem, smem),
+        out_specs=(vmem, smem),
         scratch_shapes=[
             pltpu.VMEM((rows, width, span), jnp.bfloat16),
             pltpu.VMEM((extended, width, kp * width), jnp.bfloat16),
             pltpu.VMEM((rows * ka * (kp // 2), width, 2 * width), jnp.bfloat16),
+            pltpu.VMEM((rows * kp, width, width), jnp.bfloat16),
             pltpu.VMEM(((BLOCKS + 16) * width, 2 * width), jnp.float32),
             pltpu.SMEM((rows * kp * ka * kp + UNROLL,), jnp.int32),
             pltpu.SMEM((bases.shape[0] * kc,), jnp.int32),
@@ -184,86 +180,133 @@
     )(cols, slots, masks, places, bases, a_blocks, p_blocks, halo)
 
 
-def exchange_kernel(count, *refs):
+def exchange_kernel(axes, *refs):
+    count = len(axes)
     sends, takes = refs[:count], refs[count : 2 * count]
     here_sem, send_sem, take_sem = refs[2 * count :]
-    me = lax.axis_index("row")
-    n = lax.axis_size("row")
+    me = {axis: lax.axis_index(axis) for axis in axes}
+    size = {axis: lax.axis_size(axis) for axis in axes}
     barrier = pltpu.get_barrier_semaphore()
-
-    def greet(o, unused):
-        pl.semaphore_signal(
-            barrier, inc=1, device_id={"row": lax.rem(me + o, n)}, device_id_type=pl.DeviceIdType.MESH
-        )
-        return unused
-
-    lax.fori_loop(1, n, greet, 0)
-    pl.semaphore_wait(barrier, n - 1)
+    for axis in me:
+
+        def greet(o, unused, axis=axis):
+            to = lax.rem(me[axis] + o, size[axis])
+            pl.semaphore_signal(barrier, inc=1, device_id={axis: to}, device_id_type=pl.DeviceIdType.MESH)
+            return unused
+
+        lax.fori_loop(1, size[axis], greet, 0)
+    pl.semaphore_wait(barrier, sum(n - 1 for n in size.values()))
 
     def source(x, to):
-        return sends[x].at[to] if sends[x].shape[0] == n else sends[x].at[0]
+        return sends[x].at[to] if sends[x].shape[0] > 1 else sends[x].at[0]
 
     def remote(x, o):
-        to = lax.rem(me + o, n)
+        axis = axes[x]
+        to = lax.rem(me[axis] + o, size[axis])
         return pltpu.make_async_remote_copy(
             src_ref=source(x, to),
-            dst_ref=takes[x].at[me],
+            dst_ref=takes[x].at[me[axis]],
             send_sem=send_sem.at[x, o],
             recv_sem=take_sem.at[x, o],
-            device_id={"row": to},
+            device_id={axis: to},
             device_id_type=pl.DeviceIdType.MESH,
         )
 
     def arriving(x, o):
-        came = lax.rem(me + n - o, n)
+        axis = axes[x]
+        came = lax.rem(me[axis] + size[axis] - o, size[axis])
         return pltpu.make_async_remote_copy(
             src_ref=source(x, came),
             dst_ref=takes[x].at[came],
             send_sem=send_sem.at[x, o],
             recv_sem=take_sem.at[x, o],
-            device_id={"row": came},
+            device_id={axis: came},
             device_id_type=pl.DeviceIdType.MESH,
         )
 
-    def begin(o, unused):
-        for x in range(count):
+    def here(x):
+        at = me[axes[x]]
+        return pltpu.make_async_copy(source(x, at), takes[x].at[at], here_sem.at[x])
+
+    for x in range(count):
+
+        def begin(o, unused, x=x):
             remote(x, o).start()
-        return unused
-
-    lax.fori_loop(1, n, begin, 0)
+            return unused
+
+        lax.fori_loop(1, size[axes[x]], begin, 0)
+        here(x).start()
     for x in range(count):
-        pltpu.make_async_copy(source(x, me), takes[x].at[me], here_sem.at[x]).start()
-
-    def end(o, unused):
-        for x in range(count):
+
+        def end(o, unused, x=x):
             remote(x, o).wait_send()
             arriving(x, o).wait_recv()
-        return unused
-
-    lax.fori_loop(1, n, end, 0)
-    for x in range(count):
-        pltpu.make_async_copy(source(x, me), takes[x].at[me], here_sem.at[x]).wait()
-
-
-def exchange(arrays, n, collective_id):
+            return unused
+
+        lax.fori_loop(1, size[axes[x]], end, 0)
+        here(x).wait()
+
+
+def exchange(arrays, axes, collective_id):
     hbm = pl.BlockSpec(memory_space=pl.ANY)
     count = len(arrays)
-    return pl.pallas_call(
-        functools.partial(exchange_kernel, count),
-        out_shape=tuple(jax.ShapeDtypeStruct((n,) + x.shape[1:], x.dtype) for x in arrays),
+    most = max(lax.axis_size(axis) for axis in axes)
+    return pl.pallas_call(
+        functools.partial(exchange_kernel, axes),
+        out_shape=tuple(jax.ShapeDtypeStruct((lax.axis_size(a),) + x.shape[1:], x.dtype) for x, a in zip(arrays, axes)),
         in_specs=[hbm] * count,
         out_specs=(hbm,) * count,
         scratch_shapes=[
             pltpu.SemaphoreType.DMA((count,)),
-            pltpu.SemaphoreType.DMA((count, n)),
-            pltpu.SemaphoreType.DMA((count, n)),
+            pltpu.SemaphoreType.DMA((count, most)),
+            pltpu.SemaphoreType.DMA((count, most)),
         ],
         compiler_params=pltpu.CompilerParams(collective_id=collective_id, has_side_effects=True),
         name="exchange",
     )(*arrays)
 
 
-def relay_kernel(ids_ref, parts_ref, out_ref, acc):
+def halo_kernel(blocks, ids, out_blocks, out_ids, send_sem, take_sem):
+    barrier = pltpu.get_barrier_semaphore()
+    routes = []
+    for axis, way, chosen in (("slab", 1, 1), ("slab", -1, 0), ("row", 1, 3), ("row", -1, 2)):
+        n = lax.axis_size(axis)
+        routes.append(({axis: lax.rem(lax.axis_index(axis) + way + n, n)}, chosen))
+    for to, chosen in routes:
+        pl.semaphore_signal(barrier, inc=1, device_id=to, device_id_type=pl.DeviceIdType.MESH)
+    pl.semaphore_wait(barrier, len(routes))
+    copies = []
+    for x, (to, chosen) in enumerate(routes):
+        for y, (src, dst) in enumerate(((ids, out_ids), (blocks, out_blocks))):
+            copies.append(
+                pltpu.make_async_remote_copy(
+                    src_ref=src.at[chosen],
+                    dst_ref=dst.at[x],
+                    send_sem=send_sem.at[y, x],
+                    recv_sem=take_sem.at[y, x],
+                    device_id=to,
+                    device_id_type=pl.DeviceIdType.MESH,
+                )
+            )
+            copies[-1].start()
+    for copy in copies:
+        copy.wait()
+
+
+def exchange_halo(blocks, ids):
+    hbm = pl.BlockSpec(memory_space=pl.ANY)
+    return pl.pallas_call(
+        halo_kernel,
+        out_shape=(jax.ShapeDtypeStruct(blocks.shape, blocks.dtype), jax.ShapeDtypeStruct(ids.shape, ids.dtype)),
+        in_specs=[hbm, hbm],
+        out_specs=(hbm, hbm),
+        scratch_shapes=[pltpu.SemaphoreType.DMA((2, 4)), pltpu.SemaphoreType.DMA((2, 4))],
+        compiler_params=pltpu.CompilerParams(collective_id=2, has_side_effects=True),
+        name="exchange_halo",
+    )(blocks, ids)
+
+
+def relay_kernel(ids_ref, parts_ref, out_ref, most_ref, acc):
     n, blocks, lanes = parts_ref.shape
     targets = acc.shape[0]
     acc[...] = jnp.zeros_like(acc)
@@ -276,15 +319,21 @@
 
     lax.fori_loop(0, n, one, 0)
     out_ref[...] = acc[...].astype(jnp.bfloat16)
+    ids = ids_ref[...]
+    counts = jnp.where(lax.broadcasted_iota(jnp.int32, ids.shape, 2) == ids.shape[2] - 1, ids, 0)
+    most_ref[...] = jnp.full(most_ref.shape, jnp.max(counts), jnp.int32)
 
 
 def relay_sums(ids, parts, targets):
     vmem = pl.BlockSpec(memory_space=pltpu.VMEM)
     return pl.pallas_call(
         relay_kernel,
-        out_shape=jax.ShapeDtypeStruct((targets, parts.shape[2]), jnp.bfloat16),
+        out_shape=(
+            jax.ShapeDtypeStruct((targets, parts.shape[2]), jnp.bfloat16),
+            jax.ShapeDtypeStruct((1, 1, 128), jnp.int32),
+        ),
         in_specs=[vmem, vmem],
-        out_specs=vmem,
+        out_specs=(vmem, vmem),
         scratch_shapes=[pltpu.VMEM((targets, parts.shape[2]), jnp.float32)],
         compiler_params=pltpu.CompilerParams(vmem_limit_bytes=32 * 2**20),
         name="relay_sums",
@@ -320,7 +369,7 @@
     )(pieces)
 
 
-def coarse_kernel(cols, slots, masks, places, a_hbm, p_hbm, halo_hbm, out_ref, a_v, ext_v, g_v, acc, items, sems):
+def coarse_kernel(cols, slots, masks, places, a_hbm, p_hbm, halo_hbm, out_ref, a_v, ext_v, g_v, pt_v, acc, items, sems):
     rows, width, span = a_v.shape
     ka = span // width
     kp = ext_v.shape[2] // width
@@ -353,8 +402,8 @@
         items[count + u] = nslots * kc
     for copy in copies:
         copy.wait()
-    all_products(cols, a_v, ext_v, g_v)
-    add_items(count, items, ext_v, g_v, acc, width, ka)
+    all_products(cols, a_v, ext_v, g_v, pt_v)
+    add_items(count, items, pt_v, g_v, acc, width, ka, kp)
     lower = lax.broadcasted_iota(jnp.int32, (width, pair), 1) < width
 
     def finish(t, unused):
@@ -385,6 +434,7 @@
             pltpu.VMEM((rows, width, span), jnp.bfloat16),
             pltpu.VMEM((extended, width, kp * width), jnp.bfloat16),
             pltpu.VMEM((rows * ka * (kp // 2), width, 2 * width), jnp.bfloat16),
+            pltpu.VMEM((rows * kp, width, width), jnp.bfloat16),
             pltpu.VMEM(((nslots * kc + 1) * width, 2 * width), jnp.float32),
             pltpu.SMEM((rows * kp * ka * kp + UNROLL,), jnp.int32),
             pltpu.SemaphoreType.DMA((3,)),
@@ -450,25 +500,23 @@
     lists = halo_rows[0]
     sent_blocks = p_blocks[lists]
     sent_ids = coarse_ids[lists]
-    routes = (
-        (1, "slab", [(i, i + 1) for i in range(nslab - 1)]),
-        (0, "slab", [(i + 1, i) for i in range(nslab - 1)]),
-        (3, "row", [(i, i + 1) for i in range(nrow - 1)]),
-        (2, "row", [(i + 1, i) for i in range(nrow - 1)]),
-    )
-    halo_ids = jnp.concatenate([lax.ppermute(sent_ids[n], axis, way) for n, axis, way in routes], 0)
-    halo = jnp.concatenate([lax.ppermute(sent_blocks[n], axis, way) for n, axis, way in routes], 0)
+    depth = lists.shape[1]
+    kp = p_slots.shape[1]
+    row_at = lax.axis_index("row")
+    ids_out = jnp.pad(sent_ids.reshape(4, 1, depth * kp), ((0, 0), (0, 0), (0, 128 - depth * kp)))
+    halo, halo_ids = exchange_halo(sent_blocks, ids_out)
+    outside = jnp.stack([slab_at == 0, slab_at == nslab - 1, row_at == 0, row_at == nrow - 1])
+    halo_ids = jnp.where(outside[:, None], -1, halo_ids[:, 0, : depth * kp]).reshape(4 * depth, kp)
+    halo = halo.reshape((4 * depth,) + halo.shape[2:])
     ext_ids = jnp.concatenate([coarse_ids, halo_ids], 0)
     places, masks = find_matches(ext_ids, a_cols, p_slots, patterns)
     width = a_blocks.shape[1]
     lists_in = (a_cols.reshape(-1), p_slots.reshape(-1), masks.reshape(-1), places.reshape(-1))
     bases = (jnp.arange(slots, dtype=jnp.int32) // cap * NC + table) * kc
-    packed, ids, blocks = packed_partials(*lists_in, bases, a_blocks, p_blocks, halo, kc)
-    most = lax.pmax(blocks[0], ("slab", "row"))
-    parts, part_ids = exchange((packed, ids.reshape(1, 1, IDS)), nrow, 0)
-    sums = relay_sums(part_ids, parts, nrow * NC * kc)
-    (pieces,) = exchange((sums.reshape(nrow, NC * kc, 2 * width),), nrow, 1)
-    result = assemble(pieces, width, kc)
+    packed, ids = packed_partials(*lists_in, bases, a_blocks, p_blocks, halo, kc)
+    parts, part_ids = exchange((packed, ids.reshape(1, 1, IDS)), ("row", "row"), 0)
+    sums, most = relay_sums(part_ids, parts, nrow * NC * kc)
+    pieces, counts = exchange((sums.reshape(nrow, NC * kc, 2 * width), most), ("row", "slab"), 1)
 
     def whole(unused):
         partial = coarse_partials(*lists_in, a_blocks, p_blocks, halo, slots, kc)
@@ -476,7 +524,7 @@
         owners = lax.all_to_all(touched[0], "row", 0, 0)
         return sum_parts(owners.reshape(-1), parts.reshape(slots, width, kc * width))
 
-    return lax.cond(most > BLOCKS, whole, lambda x: x, result)
+    return lax.cond(jnp.max(counts) > BLOCKS, whole, lambda unused: assemble(pieces, width, kc), 0)
 
 
 def solution(mesh):

time: 257 us -> 142 us (0.55)
  blocking collectives: 78.5 us -> 0 us
  starting transfers between devices: 22.9 us -> 0 us
  Pallas kernels: 129 us -> 120 us
  waiting for transfers between devices: 4.75 us -> 0 us
    pmax x1 -> x0, blocking collectives: 78.5 us -> none  [per_device(): most = lax.pmax(blocks[0], ('slab', 'row'))]
    ppermute x8 -> x0, starting transfers between devices: 22.9 us -> none  [the longest x4 12.2 us: per_device(): lax.ppermute(sent_blocks[n], axis, way)]
    pallas_call x1, Pallas kernels: 48 us -> 35.2 us  [packed_partials(): pl.pallas_call(packed_kernel, out_shape=(jax.ShapeDtypeStruct((width // 2...]
    pallas_call x3 -> x4, Pallas kernels: 78.3 us -> 83.7 us  [the longest x2 57.7 us: exchange(): pl.pallas_call(functools.partial(exchange_kernel, axes), out_shape=tuple(...]
    ppermute x8 -> x0, waiting for transfers between devices: 4.75 us -> none  [the longest x4 4.74 us: per_device(): lax.ppermute(sent_blocks[n], axis, way)]
    unnamed x25 -> x24, local copies, waits for them, and re-layouts: 7.99 us -> 6.55 us
  transfers between devices with their start and end apart: 8 -> 0, of which waited for: 2 -> 0; matrix products, arithmetic and copies ran while one was open for 3% -> 0% of each run, Pallas kernels for 0% -> 0%
where the time goes in v3:
time: 142 us; the launch traced here: 140 us
  Pallas kernels  120 us (85%)
  local copies, waits for them, and re-layouts  13.6 us (10%)
  other arithmetic  5.4 us (4%)
    pallas_call x2, Pallas kernels, exchange(): pl.pallas_call(functools.partial(exchange_kernel, axes), out_shape=tuple(...  57.7 us
    pallas_call x1, Pallas kernels, packed_partials(): pl.pallas_call(packed_kernel, out_shape=(jax.ShapeDtypeStruct((width // 2...  35.2 us
    pallas_call x1, Pallas kernels, exchange_halo(): pl.pallas_call(halo_kernel, out_shape=(jax.ShapeDtypeStruct(blocks.shape,...  16.3 us
    pallas_call x1, Pallas kernels, relay_sums(): pl.pallas_call(relay_kernel, out_shape=(jax.ShapeDtypeStruct((targets, pa...  9.68 us
    unnamed x24, local copies, waits for them, and re-layouts  6.55 us
    gather x1, local copies, waits for them, and re-layouts, per_device(): sent_blocks = p_blocks[lists]  3.34 us

profile of v3, /device:TPU:16, one launch (start us, length us, event | category | flops | bytes accessed | tf_op | source)
XLA Modules:
  0.0 139.9 jit_solution(1842514402896335313)
XLA Ops:
  0.0 0.0 copy-start.8
  0.0 0.8 copy.116
  0.8 0.3 slice_reduce_fusion
  1.1 0.8 copy.111
  1.9 0.1 reshape.86
  2.0 1.5 %select_reduce_fusion.13 = (s32[64,4]{0,1:T(4,128)S(1)}, s32[64,4]{0,1:T(4,128)S(1)}, s32[64,4]{0,1:T(4,128)S(1)}, s32[64,4]{0,1:T(4,128)S(1)}, s32[64,4]{0,1:T(...) fusion(s32[64]{0:T(128)S(1)} %reshape.86, ...), kind=kLoop, calls=%fused_computation.16 | loop fusion | flops 308992 | bytes 12544 | tf_op jit(solution)/shard_map/reduce_sum | solution.py:475
  3.5 0.7 fusion.3
  4.2 0.1 copy.112
  4.3 0.7 compare_select_fusion
  4.9 0.1 reshape.95
  5.0 0.6 gather_fusion.1
  5.6 0.1 reshape.87
  5.7 0.6 pad.4.ids
  6.3 0.0 copy-start.7
  6.3 0.0 copy-start.6
  6.3 3.3 %gather_fusion = bf16[32,64,256]{2,1,0:T(8,128)(2,1)} fusion(bf16[64,64,256]{2,1,0:T(8,128)(2,1)} %p_hbm.1, s32[1024]{0:T(1024)S(1)} %pad_clamp_fusion), kind=kCustom, calls=%fused_computation | custom fusion | bytes 2097280 | tf_op jit(solution)/shard_map/gather | solution.py:501
  9.6 16.3 %exchange_halo.1 = (bf16[4,8,64,256]{3,2,1,0:T(8,128)(2,1)S(1)}, s32[4,1,128]{2,1,0:T(1,128)}) custom-call(bf16[4,8,64,256]{3,2,1,0:T(8,128)(2,1)} %bitcast.58, s32[4,1,128]{2,1,0:T(1,128)} %pad.4.ids), custom_call_target="tpu_custom_call" | custom-call | tf_op jit(solution)/shard_map/exchange_halo/pallas_call | solution.py:298
  25.9 0.7 slice_reduce_fusion.8
  26.6 0.1 squeeze.44
  26.7 0.1 pad_add_fusion.2
  26.8 0.1 broadcast_in_dim.127
  26.9 0.1 broadcast_in_dim.128
  26.9 0.1 broadcast_select_fusion
  27.0 0.1 copy.114
  27.1 0.1 pad_add_fusion.1
  27.2 0.0 copy-done.8
  27.2 0.7 select_reduce_fusion.4
  27.9 0.2 select_reduce_fusion
  28.2 0.1 broadcast_add_fusion
  28.3 0.1 copy.126
  28.4 0.2 sub.20.places
  28.6 0.1 copy.125
  28.7 0.1 reshape.89.masks
  28.8 0.1 copy.109
  28.9 0.1 reshape.84.cols
  29.0 0.0 copy-done.7
  29.0 0.1 copy.110
  29.1 0.1 reshape.85.slots
  29.2 0.0 copy-done.6
  29.2 35.2 %packed_partials.1 = (bf16[32,144,128]{2,1,0:T(8,128)(2,1)S(1)}, s32[1,256]{1,0:T(1,128)S(1)}) custom-call(s32[448]{0:T(512)S(1)} %reshape.84.cols, s32[256]{0:T(256)S(1)} %reshape.85.slots, s32[256]{0:T(256)S(1)} %reshape.89.masks, s32[7168]{0:T(1024)S(1)} %sub.20.places, s32[64]{0:T(128)S(1)} %fusion.7.bases, bf16[64,64,448]{2,1,0:T(8,128)(2,1)} %a_hbm.1, ...), custom_call_target="tpu_custom_call" | custom-call | tf_op jit(solution)/shard_map/packed_partials/pallas_call | solution.py:160
  64.5 0.0 copy-start.1
  64.5 1.0 copy-done.1
  65.5 0.0 copy-start.4
  65.5 0.6 copy-done.4
  66.0 0.0 copy-start.9
  66.0 42.8 %exchange.2 = (bf16[32,144,128]{2,1,0:T(8,128)(2,1)}, s32[32,1,256]{2,1,0:T(1,128)}) custom-call(bf16[32,144,128]{2,1,0:T(8,128)(2,1)} %copy-done.1, s32[1,1,256]{2,1,0:T(1,128)} %bitcast.56), custom_call_target="tpu_custom_call" | custom-call | tf_op jit(solution)/shard_map/exchange/pallas_call | solution.py:254
  108.9 0.0 copy-start
  108.9 1.3 copy-done
  110.1 0.0 copy-start.3
  110.1 0.8 copy-done.3
  110.9 9.7 %relay_sums.1 = (bf16[1024,128]{1,0:T(8,128)(2,1)S(1)}, s32[1,1,128]{2,1,0:T(1,128)S(1)}) custom-call(s32[32,1,256]{2,1,0:T(1,128)S(1)} %copy-done.3, bf16[32,144,128]{2,1,0:T(8,128)(2,1)S(1)} %copy-done), custom_call_target="tpu_custom_call" | custom-call | tf_op jit(solution)/shard_map/relay_sums/pallas_call | solution.py:329
  120.6 0.0 copy-start.2
  120.6 0.7 copy-done.2
  121.3 0.0 copy-start.5
  121.3 0.5 copy-done.5
  121.8 14.9 %exchange.3 = (bf16[32,32,128]{2,1,0:T(8,128)(2,1)S(1)}, s32[8,1,128]{2,1,0:T(1,128)}) custom-call(bf16[32,32,128]{2,1,0:T(8,128)(2,1)} %bitcast.55, s32[1,1,128]{2,1,0:T(1,128)} %copy-done.5), custom_call_target="tpu_custom_call" | custom-call | tf_op jit(solution)/shard_map/exchange/pallas_call | solution.py:254
  136.7 1.3 reduce_max.9
  138.7 0.0 copy-done.9
  138.7 1.2 conditional.1
  138.7 1.2 assemble.1
  (9 shorter events, 0.1 us)
Async XLA Ops:
  0.0 27.2 %copy-start.8 = (s32[64,7]{0,1:T(8,128)S(1)}, s32[64,7]{0,1:T(8,128)}, u32[]{:S(2)}) copy-start(s32[64,7]{0,1:T(8,128)} %param.11) | copy-start | bytes 5380
  6.3 22.7 %copy-start.7 = (s32[64,4]{0,1:T(4,128)S(1)}, s32[64,4]{0,1:T(4,128)}, u32[]{:S(2)}) copy-start(s32[64,4]{0,1:T(4,128)} %param.12) | copy-start | bytes 3076
  6.3 22.9 %copy-start.6 = (bf16[64,64,256]{2,1,0:T(8,128)(2,1)S(1)}, bf16[64,64,256]{2,1,0:T(8,128)(2,1)}, u32[]{:S(2)}) copy-start(bf16[64,64,256]{2,1,0:T(8,128)(2,1)} %p_hbm.1) | copy-start | bytes 6291460
  64.5 1.0 copy-start.1
  65.5 0.6 copy-start.4
  66.0 72.6 %copy-start.9 = (s32[1,32,2]{1,2,0:T(2,128)S(1)}, s32[1,32,2]{1,2,0:T(2,128)}, u32[]{:S(2)}) copy-start(s32[1,32,2]{1,2,0:T(2,128)} %param.13) | copy-start | bytes 772
  108.9 1.3 copy-start
  110.1 0.8 copy-start.3
  120.6 0.7 copy-start.2
  121.3 0.5 copy-start.5

commit v4 on v3

--- a/solution.py
+++ b/solution.py
@@ -180,92 +180,6 @@
     )(cols, slots, masks, places, bases, a_blocks, p_blocks, halo)
 
 
-def exchange_kernel(axes, *refs):
-    count = len(axes)
-    sends, takes = refs[:count], refs[count : 2 * count]
-    here_sem, send_sem, take_sem = refs[2 * count :]
-    me = {axis: lax.axis_index(axis) for axis in axes}
-    size = {axis: lax.axis_size(axis) for axis in axes}
-    barrier = pltpu.get_barrier_semaphore()
-    for axis in me:
-
-        def greet(o, unused, axis=axis):
-            to = lax.rem(me[axis] + o, size[axis])
-            pl.semaphore_signal(barrier, inc=1, device_id={axis: to}, device_id_type=pl.DeviceIdType.MESH)
-            return unused
-
-        lax.fori_loop(1, size[axis], greet, 0)
-    pl.semaphore_wait(barrier, sum(n - 1 for n in size.values()))
-
-    def source(x, to):
-        return sends[x].at[to] if sends[x].shape[0] > 1 else sends[x].at[0]
-
-    def remote(x, o):
-        axis = axes[x]
-        to = lax.rem(me[axis] + o, size[axis])
-        return pltpu.make_async_remote_copy(
-            src_ref=source(x, to),
-            dst_ref=takes[x].at[me[axis]],
-            send_sem=send_sem.at[x, o],
-            recv_sem=take_sem.at[x, o],
-            device_id={axis: to},
-            device_id_type=pl.DeviceIdType.MESH,
-        )
-
-    def arriving(x, o):
-        axis = axes[x]
-        came = lax.rem(me[axis] + size[axis] - o, size[axis])
-        return pltpu.make_async_remote_copy(
-            src_ref=source(x, came),
-            dst_ref=takes[x].at[came],
-            send_sem=send_sem.at[x, o],
-            recv_sem=take_sem.at[x, o],
-            device_id={axis: came},
-            device_id_type=pl.DeviceIdType.MESH,
-        )
-
-    def here(x):
-        at = me[axes[x]]
-        return pltpu.make_async_copy(source(x, at), takes[x].at[at], here_sem.at[x])
-
-    for x in range(count):
-
-        def begin(o, unused, x=x):
-            remote(x, o).start()
-            return unused
-
-        lax.fori_loop(1, size[axes[x]], begin, 0)
-        here(x).start()
-    for x in range(count):
-
-        def end(o, unused, x=x):
-            remote(x, o).wait_send()
-            arriving(x, o).wait_recv()
-            return unused
-
-        lax.fori_loop(1, size[axes[x]], end, 0)
-        here(x).wait()
-
-
-def exchange(arrays, axes, collective_id):
-    hbm = pl.BlockSpec(memory_space=pl.ANY)
-    count = len(arrays)
-    most = max(lax.axis_size(axis) for axis in axes)
-    return pl.pallas_call(
-        functools.partial(exchange_kernel, axes),
-        out_shape=tuple(jax.ShapeDtypeStruct((lax.axis_size(a),) + x.shape[1:], x.dtype) for x, a in zip(arrays, axes)),
-        in_specs=[hbm] * count,
-        out_specs=(hbm,) * count,
-        scratch_shapes=[
-            pltpu.SemaphoreType.DMA((count,)),
-            pltpu.SemaphoreType.DMA((count, most)),
-            pltpu.SemaphoreType.DMA((count, most)),
-        ],
-        compiler_params=pltpu.CompilerParams(collective_id=collective_id, has_side_effects=True),
-        name="exchange",
-    )(*arrays)
-
-
 def halo_kernel(blocks, ids, out_blocks, out_ids, send_sem, take_sem):
     barrier = pltpu.get_barrier_semaphore()
     routes = []
@@ -301,43 +215,152 @@
         in_specs=[hbm, hbm],
         out_specs=(hbm, hbm),
         scratch_shapes=[pltpu.SemaphoreType.DMA((2, 4)), pltpu.SemaphoreType.DMA((2, 4))],
-        compiler_params=pltpu.CompilerParams(collective_id=2, has_side_effects=True),
+        compiler_params=pltpu.CompilerParams(collective_id=1, has_side_effects=True),
         name="exchange_halo",
     )(blocks, ids)
 
 
-def relay_kernel(ids_ref, parts_ref, out_ref, most_ref, acc):
-    n, blocks, lanes = parts_ref.shape
-    targets = acc.shape[0]
-    acc[...] = jnp.zeros_like(acc)
+def reduce_kernel(
+    parts, ids, pieces, most_ref, came_parts, came_ids, sums, flag, came_flags, acc, send_sem, take_sem, flag_send, flag_take
+):
+    row, slab = lax.axis_index("row"), lax.axis_index("slab")
+    n, slabs = lax.axis_size("row"), lax.axis_size("slab")
+    blocks = parts.shape[1]
+    targets, lanes = acc.shape
+    share = targets // n
+    barrier = pltpu.get_barrier_semaphore()
+    mesh_id = pl.DeviceIdType.MESH
+
+    def greet_row(o, unused):
+        pl.semaphore_signal(barrier, inc=1, device_id={"row": lax.rem(row + o, n)}, device_id_type=mesh_id)
+        return unused
+
+    def greet_slab(o, unused):
+        pl.semaphore_signal(barrier, inc=1, device_id={"slab": lax.rem(slab + o, slabs)}, device_id_type=mesh_id)
+        return unused
+
+    lax.fori_loop(1, n, greet_row, 0)
+    lax.fori_loop(1, slabs, greet_slab, 0)
+    pl.semaphore_wait(barrier, n + slabs - 2)
+
+    def row_copy(x, o, src, dst, other):
+        return pltpu.make_async_remote_copy(
+            src_ref=src,
+            dst_ref=dst,
+            send_sem=send_sem.at[x, o],
+            recv_sem=take_sem.at[x, o],
+            device_id={"row": other},
+            device_id_type=mesh_id,
+        )
+
+    def to_of(o):
+        return lax.rem(row + o, n)
+
+    def from_of(o):
+        return lax.rem(row + n - o, n)
+
+    def begin(o, unused):
+        to = to_of(o)
+        row_copy(0, o, ids.at[0], came_ids.at[row], to).start()
+        row_copy(1, o, parts.at[to], came_parts.at[row], to).start()
+        return unused
+
+    lax.fori_loop(1, n, begin, 0)
     order = lax.broadcasted_iota(jnp.int32, (targets, blocks), 0)
 
-    def one(d, unused):
-        hot = jnp.where(order == ids_ref[d, :, :blocks], 1.0, 0.0).astype(jnp.bfloat16)
-        acc[...] += jnp.dot(hot, parts_ref[d], preferred_element_type=jnp.float32)
-        return unused
-
-    lax.fori_loop(0, n, one, 0)
-    out_ref[...] = acc[...].astype(jnp.bfloat16)
-    ids = ids_ref[...]
-    counts = jnp.where(lax.broadcasted_iota(jnp.int32, ids.shape, 2) == ids.shape[2] - 1, ids, 0)
-    most_ref[...] = jnp.full(most_ref.shape, jnp.max(counts), jnp.int32)
-
-
-def relay_sums(ids, parts, targets):
+    def spread(names, values):
+        hot = jnp.where(order == names[:, :blocks], 1.0, 0.0).astype(jnp.bfloat16)
+        return jnp.dot(hot, values, preferred_element_type=jnp.float32)
+
+    own = ids[0]
+    acc[...] = spread(own, parts[row])
+    last = lax.broadcasted_iota(jnp.int32, own.shape, 1) == own.shape[1] - 1
+
+    def add(o, most):
+        came = from_of(o)
+        row_copy(0, o, ids.at[0], came_ids.at[came], came).wait_recv()
+        row_copy(1, o, parts.at[came], came_parts.at[came], came).wait_recv()
+        names = came_ids[came]
+        acc[...] += spread(names, came_parts[came])
+        return jnp.maximum(most, names)
+
+    most = lax.fori_loop(1, n, add, own)
+    flag[...] = jnp.where(last, most, 0)
+
+    def flag_copy(o, at, other):
+        return pltpu.make_async_remote_copy(
+            src_ref=flag,
+            dst_ref=came_flags.at[at],
+            send_sem=flag_send.at[o],
+            recv_sem=flag_take.at[o],
+            device_id={"slab": other},
+            device_id_type=mesh_id,
+        )
+
+    def begin_flag(o, unused):
+        flag_copy(o, slab, lax.rem(slab + o, slabs)).start()
+        return unused
+
+    lax.fori_loop(1, slabs, begin_flag, 0)
+    for p in range(n):
+        sums[p] = acc[p * share : (p + 1) * share, :].astype(jnp.bfloat16)
+
+    def begin_sums(o, unused):
+        to = to_of(o)
+        row_copy(2, o, sums.at[to], pieces.at[row], to).start()
+        return unused
+
+    lax.fori_loop(1, n, begin_sums, 0)
+    pieces[row] = sums[row]
+
+    def end_flag(o, most):
+        came = lax.rem(slab + slabs - o, slabs)
+        flag_copy(o, slab, lax.rem(slab + o, slabs)).wait_send()
+        flag_copy(o, came, came).wait_recv()
+        return jnp.maximum(most, came_flags[came])
+
+    most_ref[...] = lax.fori_loop(1, slabs, end_flag, flag[...])
+
+    def end(o, unused):
+        to, came = to_of(o), from_of(o)
+        row_copy(0, o, ids.at[0], came_ids.at[row], to).wait_send()
+        row_copy(1, o, parts.at[to], came_parts.at[row], to).wait_send()
+        row_copy(2, o, sums.at[to], pieces.at[row], to).wait_send()
+        row_copy(2, o, sums.at[came], pieces.at[came], came).wait_recv()
+        return unused
+
+    lax.fori_loop(1, n, end, 0)
+
+
+def reduce_parts(parts, ids, share):
+    n, slabs = lax.axis_size("row"), lax.axis_size("slab")
+    _, blocks, lanes = parts.shape
     vmem = pl.BlockSpec(memory_space=pltpu.VMEM)
     return pl.pallas_call(
-        relay_kernel,
+        reduce_kernel,
         out_shape=(
-            jax.ShapeDtypeStruct((targets, parts.shape[2]), jnp.bfloat16),
-            jax.ShapeDtypeStruct((1, 1, 128), jnp.int32),
+            jax.ShapeDtypeStruct((n, share, lanes), jnp.bfloat16),
+            jax.ShapeDtypeStruct((1, IDS), jnp.int32),
         ),
         in_specs=[vmem, vmem],
         out_specs=(vmem, vmem),
-        scratch_shapes=[pltpu.VMEM((targets, parts.shape[2]), jnp.float32)],
-        compiler_params=pltpu.CompilerParams(vmem_limit_bytes=32 * 2**20),
-        name="relay_sums",
-    )(ids, parts)
+        scratch_shapes=[
+            pltpu.VMEM((n, blocks, lanes), jnp.bfloat16),
+            pltpu.VMEM((n, 1, IDS), jnp.int32),
+            pltpu.VMEM((n, share, lanes), jnp.bfloat16),
+            pltpu.VMEM((1, IDS), jnp.int32),
+            pltpu.VMEM((slabs, 1, IDS), jnp.int32),
+            pltpu.VMEM((n * share, lanes), jnp.float32),
+            pltpu.SemaphoreType.DMA((3, n)),
+            pltpu.SemaphoreType.DMA((3, n)),
+            pltpu.SemaphoreType.DMA((slabs,)),
+            pltpu.SemaphoreType.DMA((slabs,)),
+        ],
+        compiler_params=pltpu.CompilerParams(
+            collective_id=0, has_side_effects=True, vmem_limit_bytes=32 * 2**20
+        ),
+        name="reduce_parts",
+    )(parts, ids)
 
 
 def assemble_kernel(pieces_ref, out_ref, wide):
@@ -514,9 +537,7 @@
     lists_in = (a_cols.reshape(-1), p_slots.reshape(-1), masks.reshape(-1), places.reshape(-1))
     bases = (jnp.arange(slots, dtype=jnp.int32) // cap * NC + table) * kc
     packed, ids = packed_partials(*lists_in, bases, a_blocks, p_blocks, halo, kc)
-    parts, part_ids = exchange((packed, ids.reshape(1, 1, IDS)), ("row", "row"), 0)
-    sums, most = relay_sums(part_ids, parts, nrow * NC * kc)
-    pieces, counts = exchange((sums.reshape(nrow, NC * kc, 2 * width), most), ("row", "slab"), 1)
+    pieces, counts = reduce_parts(packed, ids.reshape(1, 1, IDS), NC * kc)
 
     def whole(unused):
         partial = coarse_partials(*lists_in, a_blocks, p_blocks, halo, slots, kc)
@@ -524,7 +545,7 @@
         owners = lax.all_to_all(touched[0], "row", 0, 0)
         return sum_parts(owners.reshape(-1), parts.reshape(slots, width, kc * width))
 
-    return lax.cond(jnp.max(counts) > BLOCKS, whole, lambda unused: assemble(pieces, width, kc), 0)
+    return lax.cond(counts[0, IDS - 1] > BLOCKS, whole, lambda unused: assemble(pieces, width, kc), 0)
 
 
 def solution(mesh):

time: 142 us -> 122 us (0.86)
  Pallas kernels: 120 us -> 106 us
  local copies, waits for them, and re-layouts: 13.6 us -> 9.35 us
    pallas_call x3 -> x1, Pallas kernels: 67.4 us -> 52.8 us  [reduce_parts(): pl.pallas_call(reduce_kernel, out_shape=(jax.ShapeDtypeStruct((n, share,...]
    unnamed x24 -> x12, local copies, waits for them, and re-layouts: 6.55 us -> 1.92 us
where the time goes in v4:
time: 122 us; the launch traced here: 121 us
  Pallas kernels  106 us (87%)
  local copies, waits for them, and re-layouts  9.35 us (8%)
  other arithmetic  4.76 us (4%)
    pallas_call x1, Pallas kernels, reduce_parts(): pl.pallas_call(reduce_kernel, out_shape=(jax.ShapeDtypeStruct((n, share,...  52.8 us
    pallas_call x1, Pallas kernels, packed_partials(): pl.pallas_call(packed_kernel, out_shape=(jax.ShapeDtypeStruct((width // 2...  35.4 us
    pallas_call x1, Pallas kernels, exchange_halo(): pl.pallas_call(halo_kernel, out_shape=(jax.ShapeDtypeStruct(blocks.shape,...  16.3 us
    gather x1, local copies, waits for them, and re-layouts, per_device(): sent_blocks = p_blocks[lists]  3.19 us
    reduce_sum x2, other arithmetic, lookup(): return jnp.sum(jnp.where(hot, table, 0), axis=-1)  2.81 us

profile of v4, /device:TPU:16, one launch (start us, length us, event | category | flops | bytes accessed | tf_op | source)
XLA Modules:
  0.0 120.6 jit_solution(12252498339875456611)
XLA Ops:
  0.0 0.0 copy-start.1
  0.0 0.0 copy-start
  0.0 0.0 copy-start.2
  0.0 0.9 copy.116
  1.0 0.3 slice_reduce_fusion
  1.3 0.8 copy.111
  2.1 0.1 reshape.87
  2.2 1.5 %select_reduce_fusion.13 = (s32[64,4]{0,1:T(4,128)S(1)}, s32[64,4]{0,1:T(4,128)S(1)}, s32[64,4]{0,1:T(4,128)S(1)}, s32[64,4]{0,1:T(4,128)S(1)}, s32[64,4]{0,1:T(...) fusion(s32[64]{0:T(128)S(1)} %reshape.87, ...), kind=kLoop, calls=%fused_computation.16 | loop fusion | flops 308992 | bytes 12544 | tf_op jit(solution)/shard_map/reduce_sum | solution.py:498
  3.6 0.7 fusion.3
  4.3 0.1 copy.112
  4.4 0.7 compare_select_fusion
  5.1 0.1 reshape.96
  5.2 0.6 gather_fusion.1
  5.8 0.1 reshape.88
  5.9 0.6 pad.4.ids
  6.4 3.2 %gather_fusion = bf16[32,64,256]{2,1,0:T(8,128)(2,1)} fusion(bf16[64,64,256]{2,1,0:T(8,128)(2,1)} %p_hbm.1, s32[1024]{0:T(1024)S(1)} %pad_clamp_fusion), kind=kCustom, calls=%fused_computation | custom fusion | bytes 2097280 | tf_op jit(solution)/shard_map/gather | solution.py:524
  9.6 16.3 %exchange_halo.1 = (bf16[4,8,64,256]{3,2,1,0:T(8,128)(2,1)S(1)}, s32[4,1,128]{2,1,0:T(1,128)}) custom-call(bf16[4,8,64,256]{3,2,1,0:T(8,128)(2,1)} %bitcast.57, s32[4,1,128]{2,1,0:T(1,128)} %pad.4.ids), custom_call_target="tpu_custom_call" | custom-call | tf_op jit(solution)/shard_map/exchange_halo/pallas_call | solution.py:212
  25.9 0.7 slice_reduce_fusion.8
  26.6 0.1 squeeze.45
  26.7 0.1 pad_add_fusion.2
  26.8 0.1 broadcast_in_dim.127
  26.9 0.1 broadcast_in_dim.128
  26.9 0.1 broadcast_select_fusion
  27.0 0.1 copy.114
  27.1 0.1 pad_add_fusion.1
  27.2 1.4 %select_reduce_fusion.4 = (s32[64,7]{0,1:T(8,128)S(1)}, s32[64,7]{0,1:T(8,128)S(1)}, s32[64,7]{0,1:T(8,128)S(1)}, s32[64,7]{0,1:T(8,128)S(1)}) fusion(s32[96]{0:T(128)S(1)} %get-tuple-element.72, s32[64,7]{0,1:T(8,128)} %param.11, s32[96]{0:T(128)S(1)} %get-tuple-element.70, s32[96]{0:T(128)S(1)} %get-tuple-element.71, s32[96]{0:T(128)S(1)} %get-tuple-element.69), kind=kLoop, calls=%fused_computation.6 | loop fusion | flops 385280 | bytes 10496 | tf_op jit(solution)/shard_map/reduce_sum | solution.py:498
  28.6 0.2 select_reduce_fusion
  28.9 0.1 broadcast_add_fusion
  29.0 0.1 copy.126
  29.1 0.2 sub.20.places
  29.2 0.1 copy.125
  29.3 0.1 reshape.90.masks
  29.5 0.0 copy-done.2
  29.5 0.1 copy.109
  29.6 0.1 reshape.85.cols
  29.7 0.0 copy-done.1
  29.7 0.1 copy.110
  29.8 0.1 reshape.86.slots
  29.9 0.0 copy-done
  29.9 0.0 copy-start.3
  29.9 35.4 %packed_partials.1 = (bf16[32,144,128]{2,1,0:T(8,128)(2,1)S(1)}, s32[1,256]{1,0:T(1,128)S(1)}) custom-call(s32[448]{0:T(512)S(1)} %reshape.85.cols, s32[256]{0:T(256)S(1)} %reshape.86.slots, s32[256]{0:T(256)S(1)} %reshape.90.masks, s32[7168]{0:T(1024)S(1)} %sub.20.places, s32[64]{0:T(128)S(1)} %fusion.7.bases, bf16[64,64,448]{2,1,0:T(8,128)(2,1)} %a_hbm.1, ...), custom_call_target="tpu_custom_call" | custom-call | tf_op jit(solution)/shard_map/packed_partials/pallas_call | solution.py:160
  65.3 52.8 %reduce_parts.1 = (bf16[32,32,128]{2,1,0:T(8,128)(2,1)S(1)}, s32[1,256]{1,0:T(1,128)S(1)}) custom-call(bf16[32,144,128]{2,1,0:T(8,128)(2,1)S(1)} %get-tuple-element.41.parts, s32[1,1,256]{2,1,0:T(1,128)S(1)} %bitcast.55), custom_call_target="tpu_custom_call" | custom-call | tf_op jit(solution)/shard_map/reduce_parts/pallas_call | solution.py:339
  118.1 0.6 slice.55
  119.3 0.0 copy-done.3
  119.3 1.2 %conditional.1 = (f32[4,64,512]{2,1,0:T(8,128)}) conditional(s32[]{:T(128)} %bitcast.37, bf16[32,32,128]{2,1,0:T(8,128)(2,1)S(1)} %get-tuple-element.44, (s32[1,32,2]{1,2,0:T(2,128)S(1)}, s32[448]{0:T(512)S(1)}, s32[256]{0:T(256)S(1)}, s32[256]{0:T(256)S(1)}, s32[7168]{0:T(1024)S(1)}, /*index=5*/bf16[64,64,448]{2,1,0:T(8,128)(2,1)}, ...), branch_computations={%region_15.16_spmd, %region_16.17_spmd} | conditional | bytes 12617556 | solution.py:548
  119.3 1.2 %assemble.1 = f32[4,64,512]{2,1,0:T(8,128)} custom-call(bf16[32,32,128]{2,1,0:T(8,128)(2,1)S(1)} %pieces_ref), custom_call_target="tpu_custom_call" | custom-call | tf_op jit(solution)/shard_map/cond/branch_0_fun/assemble/pallas_call | solution.py:385
  (9 shorter events, 0.1 us)
Async XLA Ops:
  0.0 29.7 %copy-start.1 = (s32[64,4]{0,1:T(4,128)S(1)}, s32[64,4]{0,1:T(4,128)}, u32[]{:S(2)}) copy-start(s32[64,4]{0,1:T(4,128)} %param.12) | copy-start | bytes 3076
  0.0 29.9 %copy-start = (bf16[64,64,256]{2,1,0:T(8,128)(2,1)S(1)}, bf16[64,64,256]{2,1,0:T(8,128)(2,1)}, u32[]{:S(2)}) copy-start(bf16[64,64,256]{2,1,0:T(8,128)(2,1)} %p_hbm.1) | copy-start | bytes 6291460
  0.0 29.4 %copy-start.2 = (s32[64,7]{0,1:T(8,128)S(1)}, s32[64,7]{0,1:T(8,128)}, u32[]{:S(2)}) copy-start(s32[64,7]{0,1:T(8,128)} %param.11) | copy-start | bytes 5380
  29.9 89.4 %copy-start.3 = (s32[1,32,2]{1,2,0:T(2,128)S(1)}, s32[1,32,2]{1,2,0:T(2,128)}, u32[]{:S(2)}) copy-start(s32[1,32,2]{1,2,0:T(2,128)} %param.13) | copy-start | bytes 772

commit v5 on v4

--- a/solution.py
+++ b/solution.py
@@ -8,8 +8,8 @@
 from jax.sharding import PartitionSpec as P
 
 NC = 4
-UNROLL = 16
-BLOCKS = 144
+UNROLL = 64
+BLOCKS = 128
 IDS = 256
 
 
@@ -42,7 +42,7 @@
                 g_v[(i * ka + k) * pairs + h] = value[:, h * pair : (h + 1) * pair]
         return unused
 
-    lax.fori_loop(0, rows, products, 0)
+    lax.fori_loop(0, rows, products, 0, unroll=8)
 
 
 def add_items(count, items, pt_v, g_v, acc, width, ka, kp):
@@ -67,28 +67,26 @@
     lax.fori_loop(0, lax.div(count + UNROLL - 1, UNROLL), batch, 0)
 
 
-def clear_rows(acc, step):
+def clear_rows(acc, step, first, last):
     def clear(n, unused):
         acc[pl.ds(pl.multiple_of(n * step, step), step), :] = jnp.zeros((step, acc.shape[1]), jnp.float32)
         return unused
 
-    lax.fori_loop(0, acc.shape[0] // step, clear, 0)
+    lax.fori_loop(first, last, clear, 0)
 
 
 def packed_kernel(
-    cols, slots, masks, places, bases, a_hbm, p_hbm, halo_hbm, out_ref, ids_ref, a_v, ext_v, g_v, pt_v, acc, items, index, sems
+    cols, words, bases, a_hbm, p_hbm, halo_hbm, out_ref, ids_ref, a_v, ext_v, g_v, pt_v, acc, items, index, sems
 ):
     rows, width, span = a_v.shape
     ka = span // width
     kp = ext_v.shape[2] // width
-    kq = ka * kp
     pair = 2 * width
     half = width // 2
     kc = index.shape[0] // bases.shape[0]
     copies = load_operands(a_hbm, p_hbm, halo_hbm, a_v, ext_v, sems)
     for copy in copies:
         copy.start()
-    clear_rows(acc, 16 * width)
 
     def unset(n, unused):
         for u in range(8):
@@ -104,33 +102,31 @@
 
     lax.fori_loop(0, ids_ref.shape[1] // 8, no_id, 0)
 
-    def gather_items(im, state):
-        slot = slots[im]
-        base = bases[slot]
-        head = im * 32
-
-        def more(state):
-            return state[0] != 0
-
-        def take(state):
-            mask, at, blocks = state
-            bit = 31 - lax.clz(mask)
-            place = places[im * kq + bit]
-            old = index[slot * kc + place]
-            fresh = old < 0
-            block = jnp.where(fresh, blocks, old)
-            index[slot * kc + place] = block
-            kept = jnp.minimum(block, BLOCKS)
-            ids_ref[0, kept] = base + place
-            items[at] = (head + bit) * 1024 + kept
-            return (mask - lax.shift_left(1, bit), at + 1, blocks + fresh.astype(jnp.int32))
-
-        return lax.while_loop(more, take, (masks[im],) + state)[1:]
-
-    count, blocks = lax.fori_loop(0, rows * kp, gather_items, (0, 0))
+    last = words.shape[0] - 1
+
+    def more(state):
+        return state[0] != last
+
+    def take(state):
+        at, count, blocks = state
+        word = words[at]
+        place = word & 511
+        old = index[place]
+        fresh = old < 0
+        block = jnp.where(fresh, blocks, old)
+        index[place] = block
+        kept = jnp.minimum(block, BLOCKS)
+        ids_ref[0, kept] = bases[lax.shift_right_logical(place, 3)] + (place & 7)
+        items[count] = at * 1024 + kept
+        return (lax.shift_right_logical(word, 9), count + 1, blocks + fresh.astype(jnp.int32))
+
+    _, count, blocks = lax.while_loop(more, take, (lax.shift_right_logical(words[last], 9), 0, 0))
     for u in range(UNROLL):
         items[count + u] = BLOCKS
     ids_ref[0, IDS - 1] = blocks
+    full = jnp.minimum(lax.div(blocks + 15, 16), BLOCKS // 16)
+    clear_rows(acc, 16 * width, 0, full)
+    clear_rows(acc, 16 * width, BLOCKS // 16, BLOCKS // 16 + 1)
     for copy in copies:
         copy.wait()
     all_products(cols, a_v, ext_v, g_v, pt_v)
@@ -146,10 +142,16 @@
             out_ref[r, pl.ds(pl.multiple_of(n * 16, 16), 16), :] = jnp.where(lower, one, two).astype(jnp.bfloat16)
         return unused
 
-    lax.fori_loop(0, BLOCKS // 16, finish, 0)
-
-
-def packed_partials(cols, slots, masks, places, bases, a_blocks, p_blocks, halo, kc):
+    def empty(n, unused):
+        for r in range(half):
+            out_ref[r, pl.ds(pl.multiple_of(n * 16, 16), 16), :] = jnp.zeros((16, pair), jnp.bfloat16)
+        return unused
+
+    lax.fori_loop(0, full, finish, 0)
+    lax.fori_loop(full, BLOCKS // 16, empty, 0)
+
+
+def packed_partials(cols, words, bases, a_blocks, p_blocks, halo, kc):
     rows, width, span = a_blocks.shape
     kp = p_blocks.shape[2] // width
     ka = span // width
@@ -163,7 +165,7 @@
             jax.ShapeDtypeStruct((width // 2, BLOCKS, 2 * width), jnp.bfloat16),
             jax.ShapeDtypeStruct((1, IDS), jnp.int32),
         ),
-        in_specs=[smem, smem, smem, smem, smem, hbm, hbm, hbm],
+        in_specs=[smem, smem, smem, hbm, hbm, hbm],
         out_specs=(vmem, smem),
         scratch_shapes=[
             pltpu.VMEM((rows, width, span), jnp.bfloat16),
@@ -177,7 +179,7 @@
         ],
         compiler_params=pltpu.CompilerParams(vmem_limit_bytes=48 * 2**20),
         name="packed_partials",
-    )(cols, slots, masks, places, bases, a_blocks, p_blocks, halo)
+    )(cols, words, bases, a_blocks, p_blocks, halo)
 
 
 def halo_kernel(blocks, ids, out_blocks, out_ids, send_sem, take_sem):
@@ -392,35 +394,30 @@
     )(pieces)
 
 
-def coarse_kernel(cols, slots, masks, places, a_hbm, p_hbm, halo_hbm, out_ref, a_v, ext_v, g_v, pt_v, acc, items, sems):
+def coarse_kernel(cols, words, a_hbm, p_hbm, halo_hbm, out_ref, a_v, ext_v, g_v, pt_v, acc, items, sems):
     rows, width, span = a_v.shape
     ka = span // width
     kp = ext_v.shape[2] // width
-    kq = ka * kp
     nslots, _, outspan = out_ref.shape
     kc = outspan // width
     pair = 2 * width
     copies = load_operands(a_hbm, p_hbm, halo_hbm, a_v, ext_v, sems)
     for copy in copies:
         copy.start()
-    clear_rows(acc, width)
-
-    def gather_items(im, count):
-        slot = slots[im]
-        head = im * 32
-
-        def more(state):
-            return state[0] != 0
-
-        def take(state):
-            mask, at = state
-            bit = 31 - lax.clz(mask)
-            items[at] = (head + bit) * 1024 + slot * kc + places[im * kq + bit]
-            return (mask - lax.shift_left(1, bit), at + 1)
-
-        return lax.while_loop(more, take, (masks[im], count))[1]
-
-    count = lax.fori_loop(0, rows * kp, gather_items, 0)
+    clear_rows(acc, width, 0, acc.shape[0] // width)
+
+    last = words.shape[0] - 1
+
+    def more(state):
+        return state[0] != last
+
+    def take(state):
+        at, count = state
+        word = words[at]
+        items[count] = at * 1024 + (word & 511)
+        return (lax.shift_right_logical(word, 9), count + 1)
+
+    _, count = lax.while_loop(more, take, (lax.shift_right_logical(words[last], 9), 0))
     for u in range(UNROLL):
         items[count + u] = nslots * kc
     for copy in copies:
@@ -441,7 +438,7 @@
     lax.fori_loop(0, nslots, finish, 0)
 
 
-def coarse_partials(cols, slots, masks, places, a_blocks, p_blocks, halo, nslots, kc):
+def coarse_partials(cols, words, a_blocks, p_blocks, halo, nslots, kc):
     rows, width, span = a_blocks.shape
     kp = p_blocks.shape[2] // width
     ka = span // width
@@ -451,7 +448,7 @@
     return pl.pallas_call(
         coarse_kernel,
         out_shape=jax.ShapeDtypeStruct((nslots, width, kc * width), jnp.bfloat16),
-        in_specs=[smem, smem, smem, smem, hbm, hbm, hbm],
+        in_specs=[smem, smem, hbm, hbm, hbm],
         out_specs=pl.BlockSpec(memory_space=pltpu.VMEM),
         scratch_shapes=[
             pltpu.VMEM((rows, width, span), jnp.bfloat16),
@@ -464,7 +461,7 @@
         ],
         compiler_params=pltpu.CompilerParams(vmem_limit_bytes=56 * 2**20),
         name="coarse_partials",
-    )(cols, slots, masks, places, a_blocks, p_blocks, halo)
+    )(cols, words, a_blocks, p_blocks, halo)
 
 
 def sum_kernel(ids, parts, out_ref):
@@ -505,9 +502,19 @@
     wanted = jnp.stack([lookup(patterns[:, j], p_slots) for j in range(patterns.shape[1])], 0)
     order = jnp.arange(1, patterns.shape[1] + 1, dtype=jnp.int32)[:, None, None, None]
     places = jnp.sum(jnp.where(reached[None, :, None, :] == wanted[..., None], order, 0), 0)
-    bits = lax.shift_left(1, jnp.arange(reached.shape[1], dtype=jnp.int32))
-    masks = jnp.sum(jnp.where(places > 0, bits, 0), -1)
-    return places - 1, masks
+    kq = reached.shape[1]
+    heads = jnp.arange(rows * kp, dtype=jnp.int32)
+    bits = jnp.arange(kq, dtype=jnp.int32)
+    end = rows * kp * 32 - 1
+    at = jnp.where(places > 0, heads.reshape(rows, kp, 1) * 32 + bits, end)
+    first = jnp.min(at, -1)
+    flat = first.reshape(-1)
+    beyond = jnp.min(jnp.where(heads[None, :] > heads[:, None], flat[None, :], end), -1)
+    follow = jnp.min(jnp.where(bits[None, :] > bits[:, None], at[:, :, None, :], end), -1)
+    follow = jnp.minimum(follow, beyond.reshape(rows, kp, 1))
+    words = follow * 512 + p_slots[..., None] * patterns.shape[1] + places - 1
+    words = jnp.pad(words, ((0, 0), (0, 0), (0, 32 - kq))).reshape(-1)
+    return jnp.where(jnp.arange(end + 1, dtype=jnp.int32) == end, jnp.min(flat) * 512, words)
 
 
 def per_device(a_blocks, p_blocks, a_cols, p_slots, touched, touch_cols, halo_rows):
@@ -532,9 +539,9 @@
     halo_ids = jnp.where(outside[:, None], -1, halo_ids[:, 0, : depth * kp]).reshape(4 * depth, kp)
     halo = halo.reshape((4 * depth,) + halo.shape[2:])
     ext_ids = jnp.concatenate([coarse_ids, halo_ids], 0)
-    places, masks = find_matches(ext_ids, a_cols, p_slots, patterns)
+    words = find_matches(ext_ids, a_cols, p_slots, patterns)
     width = a_blocks.shape[1]
-    lists_in = (a_cols.reshape(-1), p_slots.reshape(-1), masks.reshape(-1), places.reshape(-1))
+    lists_in = (a_cols.reshape(-1), words)
     bases = (jnp.arange(slots, dtype=jnp.int32) // cap * NC + table) * kc
     packed, ids = packed_partials(*lists_in, bases, a_blocks, p_blocks, halo, kc)
     pieces, counts = reduce_parts(packed, ids.reshape(1, 1, IDS), NC * kc)

time: 122 us -> 101 us (0.83)
  Pallas kernels: 106 us -> 83.2 us
  other arithmetic: 4.76 us -> 5.98 us
    pallas_call x1, Pallas kernels: 35.4 us -> 20.6 us  [packed_partials(): pl.pallas_call(packed_kernel, out_shape=(jax.ShapeDtypeStruct((width // 2...]
    pallas_call x1, Pallas kernels: 52.8 us -> 45.1 us  [reduce_parts(): pl.pallas_call(reduce_kernel, out_shape=(jax.ShapeDtypeStruct((n, share,...]
    reduce_min x0 -> x3, other arithmetic: none -> 1.95 us  [the longest x1 1.18 us: find_matches(): jnp.min(jnp.where(bits[None, :] > bits[:, None], at[:, :, None, :], end),...]
where the time goes in v5:
time: 101 us; the launch traced here: 100 us
  Pallas kernels  83.2 us (82%)
  local copies, waits for them, and re-layouts  9.35 us (9%)
  other arithmetic  5.98 us (6%)
  between operations  1.49 us (1%)
    pallas_call x1, Pallas kernels, reduce_parts(): pl.pallas_call(reduce_kernel, out_shape=(jax.ShapeDtypeStruct((n, share,...  45.1 us
    pallas_call x1, Pallas kernels, packed_partials(): pl.pallas_call(packed_kernel, out_shape=(jax.ShapeDtypeStruct((width // 2...  20.6 us
    pallas_call x1, Pallas kernels, exchange_halo(): pl.pallas_call(halo_kernel, out_shape=(jax.ShapeDtypeStruct(blocks.shape,...  16.3 us
    gather x1, local copies, waits for them, and re-layouts, per_device(): sent_blocks = p_blocks[lists]  3.34 us
    reduce_sum x2, other arithmetic, lookup(): return jnp.sum(jnp.where(hot, table, 0), axis=-1)  2.12 us

profile of v5, /device:TPU:16, one launch (start us, length us, event | category | flops | bytes accessed | tf_op | source)
XLA Modules:
  0.0 100.0 jit_solution(3017408276643499981)
XLA Ops:
  0.0 0.0 copy-start.1
  0.0 0.8 copy.122
  0.8 0.3 slice_reduce_fusion
  1.1 0.8 copy.117
  1.9 0.1 reshape.109
  2.0 1.5 %select_reduce_fusion.15 = (s32[64,4]{0,1:T(4,128)S(1)}, s32[64,4]{0,1:T(4,128)S(1)}, s32[64,4]{0,1:T(4,128)S(1)}, s32[64,4]{0,1:T(4,128)S(1)}, s32[64,4]{0,1:T(...) fusion(s32[64]{0:T(128)S(1)} %reshape.109, ...), kind=kLoop, calls=%fused_computation.19 | loop fusion | flops 308992 | bytes 12544 | tf_op jit(solution)/shard_map/reduce_sum | solution.py:495
  3.5 0.7 broadcast_multiply_fusion
  4.2 0.1 copy.118
  4.3 0.7 compare_select_fusion
  4.9 0.1 reshape.120
  5.0 0.6 gather_fusion.1
  5.6 0.1 reshape.110
  5.7 0.6 pad.8.ids
  6.3 0.0 copy-start
  6.3 3.3 %gather_fusion = bf16[32,64,256]{2,1,0:T(8,128)(2,1)} fusion(bf16[64,64,256]{2,1,0:T(8,128)(2,1)} %p_hbm.1, s32[1024]{0:T(1024)S(1)} %pad_clamp_fusion), kind=kCustom, calls=%fused_computation | custom fusion | bytes 2097280 | tf_op jit(solution)/shard_map/gather | solution.py:531
  9.6 16.3 %exchange_halo.1 = (bf16[4,8,64,256]{3,2,1,0:T(8,128)(2,1)S(1)}, s32[4,1,128]{2,1,0:T(1,128)}) custom-call(bf16[4,8,64,256]{3,2,1,0:T(8,128)(2,1)} %bitcast.57, s32[4,1,128]{2,1,0:T(1,128)} %pad.8.ids), custom_call_target="tpu_custom_call" | custom-call | tf_op jit(solution)/shard_map/exchange_halo/pallas_call | solution.py:214
  25.9 0.7 slice_reduce_fusion.8
  26.6 0.1 squeeze.45
  26.7 0.1 pad_add_fusion.2
  26.8 0.1 broadcast_in_dim.166
  26.9 0.1 broadcast_in_dim.167
  26.9 0.1 broadcast_select_fusion
  27.0 0.1 copy.120
  27.1 0.1 pad_add_fusion.1
  27.2 0.0 copy-done.1
  27.2 0.7 select_reduce_fusion.6
  27.9 0.2 select_reduce_fusion.1
  28.2 0.7 fusion.13
  28.9 1.2 %select_reduce_fusion = s32[64,4,28]{0,1,2:T(4,128)S(1)} fusion(s32[64,4,28]{0,1,2:T(4,128)S(1)} %copy.131, pred[28,28]{1,0:T(8,128)(4,1)S(1)} %iota_compare_fusion.4), kind=kLoop, calls=%fused_computation.2 | loop fusion | flops 394240 | bytes 58128 | tf_op jit(solution)/shard_map/reduce_min | solution.py:513
  30.1 0.1 copy.132
  30.2 0.1 broadcast_in_dim.190
  30.3 0.1 select_reduce_fusion.2
  30.4 0.1 min.10
  30.5 0.1 copy.133
  30.6 0.1 copy.136
  30.8 0.1 reshape.114
  31.6 0.1 copy.116
  31.7 0.1 reshape.108.cols
  31.8 0.0 copy-done
  31.8 0.0 copy-start.2
  31.8 20.6 %packed_partials.1 = (bf16[32,128,128]{2,1,0:T(8,128)(2,1)S(1)}, s32[1,256]{1,0:T(1,128)S(1)}) custom-call(s32[448]{0:T(512)S(1)} %reshape.108.cols, s32[8192]{0:T(1024)S(1)} %fusion.4.words, s32[64]{0:T(128)S(1)} %fusion.12.bases, bf16[64,64,448]{2,1,0:T(8,128)(2,1)} %a_hbm.1, bf16[64,64,256]{2,1,0:T(8,128)(2,1)S(1)} %copy-done, ...), custom_call_target="tpu_custom_call" | custom-call | tf_op jit(solution)/shard_map/packed_partials/pallas_call | solution.py:162
  52.4 45.1 %reduce_parts.1 = (bf16[32,32,128]{2,1,0:T(8,128)(2,1)S(1)}, s32[1,256]{1,0:T(1,128)S(1)}) custom-call(bf16[32,128,128]{2,1,0:T(8,128)(2,1)S(1)} %get-tuple-element.35.parts, s32[1,1,256]{2,1,0:T(1,128)S(1)} %bitcast.55), custom_call_target="tpu_custom_call" | custom-call | tf_op jit(solution)/shard_map/reduce_parts/pallas_call | solution.py:341
  97.5 0.6 slice.55
  98.8 0.0 copy-done.2
  98.8 1.2 %conditional.1 = (f32[4,64,512]{2,1,0:T(8,128)}) conditional(s32[]{:T(128)} %bitcast.37, bf16[32,32,128]{2,1,0:T(8,128)(2,1)S(1)} %get-tuple-element.38, (s32[1,32,2]{1,2,0:T(2,128)S(1)}, s32[448]{0:T(512)S(1)}, s32[8192]{0:T(1024)S(1)}, bf16[64,64,448]{2,1,0:T(8,128)(2,1)}, bf16[64,64,256]{2,1,0:T(8,128)(2,1)S(1)}, ...), branch_computations={%region_18.19_spmd, %region_19.20_spmd} | conditional | bytes 12617556 | solution.py:555
  98.8 1.2 %assemble.1 = f32[4,64,512]{2,1,0:T(8,128)} custom-call(bf16[32,32,128]{2,1,0:T(8,128)(2,1)S(1)} %pieces_ref), custom_call_target="tpu_custom_call" | custom-call | tf_op jit(solution)/shard_map/cond/branch_0_fun/assemble/pallas_call | solution.py:387
  (14 shorter events, 0.2 us)
Async XLA Ops:
  0.0 27.2 %copy-start.1 = (s32[64,7]{0,1:T(8,128)S(1)}, s32[64,7]{0,1:T(8,128)}, u32[]{:S(2)}) copy-start(s32[64,7]{0,1:T(8,128)} %param.11) | copy-start | bytes 5380
  6.3 25.5 %copy-start = (bf16[64,64,256]{2,1,0:T(8,128)(2,1)S(1)}, bf16[64,64,256]{2,1,0:T(8,128)(2,1)}, u32[]{:S(2)}) copy-start(bf16[64,64,256]{2,1,0:T(8,128)(2,1)} %p_hbm.1) | copy-start | bytes 6291460
  31.8 67.0 %copy-start.2 = (s32[1,32,2]{1,2,0:T(2,128)S(1)}, s32[1,32,2]{1,2,0:T(2,128)}, u32[]{:S(2)}) copy-start(s32[1,32,2]{1,2,0:T(2,128)} %param.13) | copy-start | bytes 772

commit v6 on v5

--- a/solution.py
+++ b/solution.py
@@ -182,44 +182,59 @@
     )(cols, words, bases, a_blocks, p_blocks, halo)
 
 
-def halo_kernel(blocks, ids, out_blocks, out_ids, send_sem, take_sem):
+def halo_kernel(rows, p_ref, ids, out_blocks, out_ids, blocks, send_sem, take_sem):
     barrier = pltpu.get_barrier_semaphore()
     routes = []
-    for axis, way, chosen in (("slab", 1, 1), ("slab", -1, 0), ("row", 1, 3), ("row", -1, 2)):
+    for x, axis, way, chosen in ((2, "row", 1, 3), (3, "row", -1, 2), (0, "slab", 1, 1), (1, "slab", -1, 0)):
         n = lax.axis_size(axis)
-        routes.append(({axis: lax.rem(lax.axis_index(axis) + way + n, n)}, chosen))
-    for to, chosen in routes:
+        routes.append((x, {axis: lax.rem(lax.axis_index(axis) + way + n, n)}, chosen))
+    for _, to, _ in routes:
         pl.semaphore_signal(barrier, inc=1, device_id=to, device_id_type=pl.DeviceIdType.MESH)
-    pl.semaphore_wait(barrier, len(routes))
-    copies = []
-    for x, (to, chosen) in enumerate(routes):
-        for y, (src, dst) in enumerate(((ids, out_ids), (blocks, out_blocks))):
-            copies.append(
-                pltpu.make_async_remote_copy(
-                    src_ref=src.at[chosen],
-                    dst_ref=dst.at[x],
-                    send_sem=send_sem.at[y, x],
-                    recv_sem=take_sem.at[y, x],
-                    device_id=to,
-                    device_id_type=pl.DeviceIdType.MESH,
-                )
-            )
-            copies[-1].start()
-    for copy in copies:
-        copy.wait()
-
-
-def exchange_halo(blocks, ids):
+    depth = blocks.shape[1]
+    for y, x in enumerate((3, 2, 1, 0)):
+        for h in range(depth):
+            blocks[x, h] = p_ref[rows[0, x, h]]
+        if y == 0:
+            pl.semaphore_wait(barrier, len(routes))
+        slot, to, chosen = routes[y]
+        for z, (src, dst) in enumerate(((ids, out_ids), (blocks, out_blocks))):
+            pltpu.make_async_remote_copy(
+                src_ref=src.at[chosen],
+                dst_ref=dst.at[slot],
+                send_sem=send_sem.at[z, slot],
+                recv_sem=take_sem.at[z, slot],
+                device_id=to,
+                device_id_type=pl.DeviceIdType.MESH,
+            ).start()
+    for slot, to, chosen in routes:
+        for z, (src, dst) in enumerate(((ids, out_ids), (blocks, out_blocks))):
+            pltpu.make_async_remote_copy(
+                src_ref=src.at[chosen],
+                dst_ref=dst.at[slot],
+                send_sem=send_sem.at[z, slot],
+                recv_sem=take_sem.at[z, slot],
+                device_id=to,
+                device_id_type=pl.DeviceIdType.MESH,
+            ).wait()
+
+
+def exchange_halo(rows, p_blocks, ids):
+    vmem = pl.BlockSpec(memory_space=pltpu.VMEM)
     hbm = pl.BlockSpec(memory_space=pl.ANY)
+    shape = rows.shape[1:] + p_blocks.shape[1:]
     return pl.pallas_call(
         halo_kernel,
-        out_shape=(jax.ShapeDtypeStruct(blocks.shape, blocks.dtype), jax.ShapeDtypeStruct(ids.shape, ids.dtype)),
-        in_specs=[hbm, hbm],
+        out_shape=(jax.ShapeDtypeStruct(shape, p_blocks.dtype), jax.ShapeDtypeStruct(ids.shape, ids.dtype)),
+        in_specs=[pl.BlockSpec(memory_space=pltpu.SMEM), vmem, hbm],
         out_specs=(hbm, hbm),
-        scratch_shapes=[pltpu.SemaphoreType.DMA((2, 4)), pltpu.SemaphoreType.DMA((2, 4))],
-        compiler_params=pltpu.CompilerParams(collective_id=1, has_side_effects=True),
+        scratch_shapes=[
+            pltpu.VMEM(shape, p_blocks.dtype),
+            pltpu.SemaphoreType.DMA((2, 4)),
+            pltpu.SemaphoreType.DMA((2, 4)),
+        ],
+        compiler_params=pltpu.CompilerParams(collective_id=1, has_side_effects=True, vmem_limit_bytes=32 * 2**20),
         name="exchange_halo",
-    )(blocks, ids)
+    )(rows, p_blocks, ids)
 
 
 def reduce_kernel(
@@ -321,7 +336,7 @@
         flag_copy(o, came, came).wait_recv()
         return jnp.maximum(most, came_flags[came])
 
-    most_ref[...] = lax.fori_loop(1, slabs, end_flag, flag[...])
+    most_ref[0, 0] = jnp.max(lax.fori_loop(1, slabs, end_flag, flag[...]))
 
     def end(o, unused):
         to, came = to_of(o), from_of(o)
@@ -342,10 +357,10 @@
         reduce_kernel,
         out_shape=(
             jax.ShapeDtypeStruct((n, share, lanes), jnp.bfloat16),
-            jax.ShapeDtypeStruct((1, IDS), jnp.int32),
+            jax.ShapeDtypeStruct((1, 1), jnp.int32),
         ),
         in_specs=[vmem, vmem],
-        out_specs=(vmem, vmem),
+        out_specs=(vmem, pl.BlockSpec(memory_space=pltpu.SMEM)),
         scratch_shapes=[
             pltpu.VMEM((n, blocks, lanes), jnp.bfloat16),
             pltpu.VMEM((n, 1, IDS), jnp.int32),
@@ -528,13 +543,12 @@
     kc = patterns.shape[1]
     coarse_ids = (slab_at * nrow + p_slots // cap) * NC + lookup(table, p_slots)
     lists = halo_rows[0]
-    sent_blocks = p_blocks[lists]
     sent_ids = coarse_ids[lists]
     depth = lists.shape[1]
     kp = p_slots.shape[1]
     row_at = lax.axis_index("row")
     ids_out = jnp.pad(sent_ids.reshape(4, 1, depth * kp), ((0, 0), (0, 0), (0, 128 - depth * kp)))
-    halo, halo_ids = exchange_halo(sent_blocks, ids_out)
+    halo, halo_ids = exchange_halo(halo_rows, p_blocks, ids_out)
     outside = jnp.stack([slab_at == 0, slab_at == nslab - 1, row_at == 0, row_at == nrow - 1])
     halo_ids = jnp.where(outside[:, None], -1, halo_ids[:, 0, : depth * kp]).reshape(4 * depth, kp)
     halo = halo.reshape((4 * depth,) + halo.shape[2:])
@@ -552,7 +566,7 @@
         owners = lax.all_to_all(touched[0], "row", 0, 0)
         return sum_parts(owners.reshape(-1), parts.reshape(slots, width, kc * width))
 
-    return lax.cond(counts[0, IDS - 1] > BLOCKS, whole, lambda unused: assemble(pieces, width, kc), 0)
+    return lax.cond(counts[0, 0] > BLOCKS, whole, lambda unused: assemble(pieces, width, kc), 0)
 
 
 def solution(mesh):

time: 101 us -> 101 us (level)
  Pallas kernels: 83.2 us -> 88.3 us
  local copies, waits for them, and re-layouts: 9.35 us -> 4.85 us
    pallas_call x1, Pallas kernels: 20.6 us -> 24.1 us  [packed_partials(): pl.pallas_call(packed_kernel, out_shape=(jax.ShapeDtypeStruct((width // 2...]
    gather x1 -> x0, local copies, waits for them, and re-layouts: 3.34 us -> none  [per_device(): sent_blocks = p_blocks[lists]]
    pallas_call x1, Pallas kernels: 16.3 us -> 17.9 us  [exchange_halo(): pl.pallas_call(halo_kernel, out_shape=(jax.ShapeDtypeStruct(shape, p_bloc...]
    unnamed x10 -> x12, local copies, waits for them, and re-layouts: 1.79 us -> 2.47 us
where the time goes in v6:
time: 101 us
  Pallas kernels  88.3 us (87%)
  other arithmetic  5.98 us (6%)
  local copies, waits for them, and re-layouts  4.85 us (5%)
  between operations  1.54 us (2%)
    pallas_call x1, Pallas kernels, reduce_parts(): pl.pallas_call(reduce_kernel, out_shape=(jax.ShapeDtypeStruct((n, share,...  45.1 us
    pallas_call x1, Pallas kernels, packed_partials(): pl.pallas_call(packed_kernel, out_shape=(jax.ShapeDtypeStruct((width // 2...  24.1 us
    pallas_call x1, Pallas kernels, exchange_halo(): pl.pallas_call(halo_kernel, out_shape=(jax.ShapeDtypeStruct(shape, p_bloc...  17.9 us
    unnamed x12, local copies, waits for them, and re-layouts  2.47 us
    reduce_sum x2, other arithmetic, lookup(): return jnp.sum(jnp.where(hot, table, 0), axis=-1)  2.12 us

profile of v6, /device:TPU:16, one launch (start us, length us, event | category | flops | bytes accessed | tf_op | source)
XLA Modules:
  0.0 100.6 jit_solution(2685049202476289970)
XLA Ops:
  0.0 0.0 copy-start.2
  0.0 0.8 copy.122
  0.8 0.3 slice_reduce_fusion
  1.1 0.8 copy.117
  1.9 0.1 reshape.109
  2.0 1.5 %select_reduce_fusion.15 = (s32[64,4]{0,1:T(4,128)S(1)}, s32[64,4]{0,1:T(4,128)S(1)}, s32[64,4]{0,1:T(4,128)S(1)}, s32[64,4]{0,1:T(4,128)S(1)}, s32[64,4]{0,1:T(...) fusion(s32[64]{0:T(128)S(1)} %reshape.109, ...), kind=kLoop, calls=%fused_computation.18 | loop fusion | flops 308992 | bytes 12544 | tf_op jit(solution)/shard_map/reduce_sum | solution.py:510
  3.5 0.7 broadcast_multiply_fusion
  4.2 0.1 copy.118
  4.3 0.7 compare_select_fusion
  4.9 0.1 reshape.120
  5.0 0.6 gather_fusion
  5.6 0.1 reshape.110
  5.7 0.0 copy-start
  5.7 0.7 copy-done
  6.4 0.0 copy-start.1
  6.4 17.9 %exchange_halo.1 = (bf16[4,8,64,256]{3,2,1,0:T(8,128)(2,1)S(1)}, s32[4,1,128]{2,1,0:T(1,128)S(1)}) custom-call(s32[1,4,8]{2,1,0:T(4,128)S(1)} %copy-done, bf16[64,64,256]{2,1,0:T(8,128)(2,1)} %p_hbm.1, s32[4,1,128]{2,1,0:T(1,128)S(1)} %pad.8.ids), custom_call_target="tpu_custom_call" | custom-call | tf_op jit(solution)/shard_map/exchange_halo/pallas_call | solution.py:225
  24.3 0.1 squeeze.45
  24.4 0.1 pad_add_fusion.2
  24.5 0.1 broadcast_in_dim.165
  24.5 0.1 broadcast_in_dim.166
  24.6 0.1 broadcast_select_fusion
  24.7 0.1 copy.120
  24.8 0.1 pad_add_fusion.1
  24.9 0.0 copy-done.2
  24.9 0.7 select_reduce_fusion.6
  25.6 0.2 select_reduce_fusion.1
  25.9 0.7 fusion.13
  26.6 1.2 %select_reduce_fusion = s32[64,4,28]{0,1,2:T(4,128)S(1)} fusion(s32[64,4,28]{0,1,2:T(4,128)S(1)} %copy.131, pred[28,28]{1,0:T(8,128)(4,1)S(1)} %iota_compare_fusion.4), kind=kLoop, calls=%fused_computation.1 | loop fusion | flops 394240 | bytes 58128 | tf_op jit(solution)/shard_map/reduce_min | solution.py:528
  27.8 0.1 copy.132
  27.9 0.1 broadcast_in_dim.189
  28.0 0.1 select_reduce_fusion.2
  28.1 0.1 min.10
  28.2 0.1 copy.133
  28.3 0.1 copy.136
  28.5 0.1 reshape.114
  29.3 0.1 copy.116
  29.4 0.1 reshape.108.cols
  29.5 0.0 copy-done.1
  29.5 0.0 copy-start.3
  29.5 24.1 %packed_partials.1 = (bf16[32,128,128]{2,1,0:T(8,128)(2,1)S(1)}, s32[1,256]{1,0:T(1,128)S(1)}) custom-call(s32[448]{0:T(512)S(1)} %reshape.108.cols, s32[8192]{0:T(1024)S(1)} %fusion.4.words, s32[64]{0:T(128)S(1)} %fusion.12.bases, bf16[64,64,448]{2,1,0:T(8,128)(2,1)} %a_hbm.1, bf16[64,64,256]{2,1,0:T(8,128)(2,1)S(1)} %copy-done.1, ...), custom_call_target="tpu_custom_call" | custom-call | tf_op jit(solution)/shard_map/packed_partials/pallas_call | solution.py:162
  53.6 45.1 %reduce_parts.1 = (bf16[32,32,128]{2,1,0:T(8,128)(2,1)S(1)}, s32[1,1]{1,0:T(1,128)}) custom-call(bf16[32,128,128]{2,1,0:T(8,128)(2,1)S(1)} %get-tuple-element.35.parts, s32[1,1,256]{2,1,0:T(1,128)S(1)} %bitcast.54), custom_call_target="tpu_custom_call" | custom-call | tf_op jit(solution)/shard_map/reduce_parts/pallas_call | solution.py:356
  99.4 0.0 copy-done.3
  99.4 1.2 %conditional.1 = (f32[4,64,512]{2,1,0:T(8,128)}) conditional(s32[]{:T(128)} %bitcast.36, bf16[32,32,128]{2,1,0:T(8,128)(2,1)S(1)} %get-tuple-element.38, (s32[1,32,2]{1,2,0:T(2,128)S(1)}, s32[448]{0:T(512)S(1)}, s32[8192]{0:T(1024)S(1)}, bf16[64,64,448]{2,1,0:T(8,128)(2,1)}, bf16[64,64,256]{2,1,0:T(8,128)(2,1)S(1)}, ...), branch_computations={%region_18.19_spmd, %region_19.20_spmd} | conditional | bytes 12617556 | solution.py:569
  99.4 1.2 %assemble.1 = f32[4,64,512]{2,1,0:T(8,128)} custom-call(bf16[32,32,128]{2,1,0:T(8,128)(2,1)S(1)} %pieces_ref), custom_call_target="tpu_custom_call" | custom-call | tf_op jit(solution)/shard_map/cond/branch_0_fun/assemble/pallas_call | solution.py:402
  (16 shorter events, 0.2 us)
Async XLA Ops:
  0.0 24.9 %copy-start.2 = (s32[64,7]{0,1:T(8,128)S(1)}, s32[64,7]{0,1:T(8,128)}, u32[]{:S(2)}) copy-start(s32[64,7]{0,1:T(8,128)} %param.11) | copy-start | bytes 5380
  5.7 0.7 copy-start
  6.4 23.1 %copy-start.1 = (bf16[64,64,256]{2,1,0:T(8,128)(2,1)S(1)}, bf16[64,64,256]{2,1,0:T(8,128)(2,1)}, u32[]{:S(2)}) copy-start(bf16[64,64,256]{2,1,0:T(8,128)(2,1)} %p_hbm.1) | copy-start | bytes 6291460
  29.5 69.9 %copy-start.3 = (s32[1,32,2]{1,2,0:T(2,128)S(1)}, s32[1,32,2]{1,2,0:T(2,128)}, u32[]{:S(2)}) copy-start(s32[1,32,2]{1,2,0:T(2,128)} %param.13) | copy-start | bytes 772

commit v7 on v6

--- a/solution.py
+++ b/solution.py
@@ -34,7 +34,7 @@
         for m in range(2 * pairs):
             pt_v[i * 2 * pairs + m] = turned[m * width : (m + 1) * width, :]
         for k in range(ka):
-            right = ext_v[cols[i * ka + k]]
+            right = ext_v[cols[k, i]]
             value = jnp.dot(row[:, k * width : (k + 1) * width], right, preferred_element_type=jnp.float32).astype(
                 jnp.bfloat16
             )
@@ -54,11 +54,9 @@
         for u in range(UNROLL):
             word = items[b * UNROLL + u]
             target = word & 1023
-            bit = lax.shift_right_logical(word, 10) & 31
-            im = lax.shift_right_logical(word, 15)
-            g = g_v[lax.shift_right_logical(im, kp.bit_length() - 1) * (ka * kp // 2) + lax.shift_right_logical(bit, 1)]
-            g = jnp.where(upper == (bit & 1), g, jnp.zeros_like(g))
-            z = jnp.dot(pt_v[im], g, preferred_element_type=jnp.float32)
+            g = g_v[lax.shift_right_logical(word, 11) & 1023]
+            g = jnp.where(upper == (lax.shift_right_logical(word, 10) & 1), g, jnp.zeros_like(g))
+            z = jnp.dot(pt_v[lax.shift_right_logical(word, 21)], g, preferred_element_type=jnp.float32)
             found.append((pl.ds(pl.multiple_of(target * width, width), width), z))
         for where, z in found:
             acc[where, :] = acc[where, :] + z
@@ -73,6 +71,65 @@
         return unused
 
     lax.fori_loop(first, last, clear, 0)
+
+
+def link_matches(cols_v, slots_v, own_ids, halo_ids, edges, patterns, at_v, follow_v, place_v):
+    ka, rows = cols_v.shape
+    kp = slots_v.shape[0]
+    nslots, kc = patterns.shape
+    sides, depth = halo_ids.shape[0], rows // 8
+    end = at_v.shape[0] * 128 - 1
+    cols = cols_v[...]
+    reached = [jnp.full((ka, rows), -2, jnp.int32)] * kp
+    for c in range(rows):
+        hit = cols == c
+        reached = [jnp.where(hit, own_ids[q, c], reached[q]) for q in range(kp)]
+    for x in range(sides):
+        for d in range(depth):
+            hit = cols == rows + x * depth + d
+            reached = [
+                jnp.where(hit, jnp.where(edges[x], -1, halo_ids[x, 0, d * kp + q]), reached[q]) for q in range(kp)
+            ]
+    slots = slots_v[...]
+    wanted = [jnp.full((kp, rows), -3, jnp.int32)] * kc
+    for t in range(nslots):
+        hit = slots == t
+        wanted = [jnp.where(hit, patterns[t, j], wanted[j]) for j in range(kc)]
+    at_v[...] = jnp.full(at_v.shape, end, jnp.int32)
+    follow_v[...] = jnp.full(follow_v.shape, end, jnp.int32)
+    place_v[...] = jnp.zeros(place_v.shape, jnp.int32)
+    which = lax.broadcasted_iota(jnp.int32, (ka, rows), 0) * 128 + lax.broadcasted_iota(jnp.int32, (ka, rows), 1)
+    for m in range(kp):
+        for q in range(kp):
+            place = jnp.full((ka, rows), -1, jnp.int32)
+            for j in range(kc):
+                place = jnp.where(reached[q] == wanted[j][m : m + 1, :], j, place)
+            row = (m * kp + q) * 8
+            at_v[row : row + ka, :rows] = jnp.where(place >= 0, which + row * 128, end)
+            place_v[row : row + ka, :rows] = slots[m : m + 1, :] * kc + place
+    run = jnp.full((1, 128), end, jnp.int32)
+    for row in reversed(range(kp * kp * 8)):
+        if row % 8 < ka:
+            now = at_v[row : row + 1, :]
+            follow_v[row : row + 1, :] = run
+            run = jnp.minimum(run, now)
+    lane = lax.broadcasted_iota(jnp.int32, (8, 128), 1)
+    key = jnp.where(run == end, 128 * (end + 1) + end, lane * (end + 1) + run)
+    beyond = pltpu.roll(key, 127, 1)
+    for step in (1, 2, 4, 8, 16, 32):
+        beyond = jnp.minimum(beyond, pltpu.roll(beyond, 128 - step, 1))
+    beyond = (beyond & end)[:1, :]
+    follow = follow_v[...]
+    kinds = lax.broadcasted_iota(jnp.int32, at_v.shape, 0)
+    spots = lax.broadcasted_iota(jnp.int32, at_v.shape, 1) - rows
+    k = kinds & 7
+    q = lax.shift_right_logical(kinds, 3) & (kp - 1)
+    m = lax.shift_right_logical(kinds, 2 + kp.bit_length())
+    info = ((spots * kp + m) * 1024 + (spots * ka + k) * (kp // 2) + lax.shift_right_logical(q, 1)) * 2 + (q & 1)
+    links = jnp.where(follow == end, beyond, follow) * 512 + place_v[...]
+    at_v[...] = jnp.where(spots < 0, links, info * 1024)
+    start = jnp.min(key[:1], axis=1, keepdims=True) & end
+    at_v[at_v.shape[0] - 1 :, :] = jnp.broadcast_to(start, (1, 128))
 
 
 def packed_kernel(
@@ -102,14 +159,15 @@
 
     lax.fori_loop(0, ids_ref.shape[1] // 8, no_id, 0)
 
-    last = words.shape[0] - 1
+    last = words.shape[0] * 128 - 1
+    first = words[words.shape[0] - 1, 0]
 
     def more(state):
         return state[0] != last
 
     def take(state):
         at, count, blocks = state
-        word = words[at]
+        word = words[lax.shift_right_logical(at, 7), at & 127]
         place = word & 511
         old = index[place]
         fresh = old < 0
@@ -117,10 +175,10 @@
         index[place] = block
         kept = jnp.minimum(block, BLOCKS)
         ids_ref[0, kept] = bases[lax.shift_right_logical(place, 3)] + (place & 7)
-        items[count] = at * 1024 + kept
+        items[count] = words[lax.shift_right_logical(at, 7), (at & 127) + rows] + kept
         return (lax.shift_right_logical(word, 9), count + 1, blocks + fresh.astype(jnp.int32))
 
-    _, count, blocks = lax.while_loop(more, take, (lax.shift_right_logical(words[last], 9), 0, 0))
+    _, count, blocks = lax.while_loop(more, take, (first, 0, 0))
     for u in range(UNROLL):
         items[count + u] = BLOCKS
     ids_ref[0, IDS - 1] = blocks
@@ -182,59 +240,73 @@
     )(cols, words, bases, a_blocks, p_blocks, halo)
 
 
-def halo_kernel(rows, p_ref, ids, out_blocks, out_ids, blocks, send_sem, take_sem):
+def halo_kernel(
+    rows, own_ids, patterns, cols_v, slots_v, p_ref, ids, out_blocks, words, blocks, came_ids, halo_ids, follow_v, place_v,
+    here_sem, send_sem, take_sem
+):
     barrier = pltpu.get_barrier_semaphore()
     routes = []
+    edges = [None] * 4
     for x, axis, way, chosen in ((2, "row", 1, 3), (3, "row", -1, 2), (0, "slab", 1, 1), (1, "slab", -1, 0)):
-        n = lax.axis_size(axis)
-        routes.append((x, {axis: lax.rem(lax.axis_index(axis) + way + n, n)}, chosen))
+        n, at = lax.axis_size(axis), lax.axis_index(axis)
+        routes.append((x, {axis: lax.rem(at + way + n, n)}, chosen))
+        edges[x] = at == (0 if way == 1 else n - 1)
     for _, to, _ in routes:
         pl.semaphore_signal(barrier, inc=1, device_id=to, device_id_type=pl.DeviceIdType.MESH)
-    depth = blocks.shape[1]
-    for y, x in enumerate((3, 2, 1, 0)):
-        for h in range(depth):
+    for x in (3, 2, 1, 0):
+        for h in range(blocks.shape[1]):
             blocks[x, h] = p_ref[rows[0, x, h]]
-        if y == 0:
-            pl.semaphore_wait(barrier, len(routes))
-        slot, to, chosen = routes[y]
-        for z, (src, dst) in enumerate(((ids, out_ids), (blocks, out_blocks))):
-            pltpu.make_async_remote_copy(
-                src_ref=src.at[chosen],
-                dst_ref=dst.at[slot],
-                send_sem=send_sem.at[z, slot],
-                recv_sem=take_sem.at[z, slot],
-                device_id=to,
-                device_id_type=pl.DeviceIdType.MESH,
-            ).start()
+    pl.semaphore_wait(barrier, len(routes))
+
+    def send(z, slot, to, chosen):
+        src, dst = ((ids, came_ids), (blocks, out_blocks))[z]
+        return pltpu.make_async_remote_copy(
+            src_ref=src.at[chosen],
+            dst_ref=dst.at[slot],
+            send_sem=send_sem.at[z, slot],
+            recv_sem=take_sem.at[z, slot],
+            device_id=to,
+            device_id_type=pl.DeviceIdType.MESH,
+        )
+
+    for z in range(2):
+        for slot, to, chosen in routes:
+            send(z, slot, to, chosen).start()
     for slot, to, chosen in routes:
-        for z, (src, dst) in enumerate(((ids, out_ids), (blocks, out_blocks))):
-            pltpu.make_async_remote_copy(
-                src_ref=src.at[chosen],
-                dst_ref=dst.at[slot],
-                send_sem=send_sem.at[z, slot],
-                recv_sem=take_sem.at[z, slot],
-                device_id=to,
-                device_id_type=pl.DeviceIdType.MESH,
-            ).wait()
-
-
-def exchange_halo(rows, p_blocks, ids):
+        send(0, slot, to, chosen).wait()
+    here = pltpu.make_async_copy(came_ids, halo_ids, here_sem.at[0])
+    here.start()
+    here.wait()
+    link_matches(cols_v, slots_v, own_ids, halo_ids, edges, patterns, words, follow_v, place_v)
+    for slot, to, chosen in routes:
+        send(1, slot, to, chosen).wait()
+
+
+def exchange_halo(rows, own_ids, patterns, cols, slots, p_blocks, ids):
     vmem = pl.BlockSpec(memory_space=pltpu.VMEM)
+    smem = pl.BlockSpec(memory_space=pltpu.SMEM)
     hbm = pl.BlockSpec(memory_space=pl.ANY)
     shape = rows.shape[1:] + p_blocks.shape[1:]
+    kp = slots.shape[0]
+    linked = (kp * kp * 8, 128)
     return pl.pallas_call(
         halo_kernel,
-        out_shape=(jax.ShapeDtypeStruct(shape, p_blocks.dtype), jax.ShapeDtypeStruct(ids.shape, ids.dtype)),
-        in_specs=[pl.BlockSpec(memory_space=pltpu.SMEM), vmem, hbm],
-        out_specs=(hbm, hbm),
+        out_shape=(jax.ShapeDtypeStruct(shape, p_blocks.dtype), jax.ShapeDtypeStruct(linked, jnp.int32)),
+        in_specs=[smem, smem, smem, vmem, vmem, vmem, hbm],
+        out_specs=(hbm, vmem),
         scratch_shapes=[
             pltpu.VMEM(shape, p_blocks.dtype),
+            pltpu.VMEM(ids.shape, jnp.int32),
+            pltpu.SMEM(ids.shape, jnp.int32),
+            pltpu.VMEM(linked, jnp.int32),
+            pltpu.VMEM(linked, jnp.int32),
+            pltpu.SemaphoreType.DMA((1,)),
             pltpu.SemaphoreType.DMA((2, 4)),
             pltpu.SemaphoreType.DMA((2, 4)),
         ],
         compiler_params=pltpu.CompilerParams(collective_id=1, has_side_effects=True, vmem_limit_bytes=32 * 2**20),
         name="exchange_halo",
-    )(rows, p_blocks, ids)
+    )(rows, own_ids, patterns, cols, slots, p_blocks, ids)
 
 
 def reduce_kernel(
@@ -409,7 +481,9 @@
     )(pieces)
 
 
-def coarse_kernel(cols, words, a_hbm, p_hbm, halo_hbm, out_ref, a_v, ext_v, g_v, pt_v, acc, items, sems):
+def coarse_kernel(
+    cols, words, a_hbm, p_hbm, halo_hbm, out_ref, a_v, ext_v, g_v, pt_v, acc, items, sems
+):
     rows, width, span = a_v.shape
     ka = span // width
     kp = ext_v.shape[2] // width
@@ -421,18 +495,19 @@
         copy.start()
     clear_rows(acc, width, 0, acc.shape[0] // width)
 
-    last = words.shape[0] - 1
+    last = words.shape[0] * 128 - 1
+    first = words[words.shape[0] - 1, 0]
 
     def more(state):
         return state[0] != last
 
     def take(state):
         at, count = state
-        word = words[at]
-        items[count] = at * 1024 + (word & 511)
+        word = words[lax.shift_right_logical(at, 7), at & 127]
+        items[count] = words[lax.shift_right_logical(at, 7), (at & 127) + rows] + (word & 511)
         return (lax.shift_right_logical(word, 9), count + 1)
 
-    _, count = lax.while_loop(more, take, (lax.shift_right_logical(words[last], 9), 0))
+    _, count = lax.while_loop(more, take, (first, 0))
     for u in range(UNROLL):
         items[count + u] = nslots * kc
     for copy in copies:
@@ -460,6 +535,7 @@
     extended = rows + halo.shape[0]
     smem = pl.BlockSpec(memory_space=pltpu.SMEM)
     hbm = pl.BlockSpec(memory_space=pl.ANY)
+    vmem = pl.BlockSpec(memory_space=pltpu.VMEM)
     return pl.pallas_call(
         coarse_kernel,
         out_shape=jax.ShapeDtypeStruct((nslots, width, kc * width), jnp.bfloat16),
@@ -510,31 +586,8 @@
     return jnp.sum(jnp.where(hot, table, 0), axis=-1)
 
 
-def find_matches(ext_ids, a_cols, p_slots, patterns):
-    rows = a_cols.shape[0]
-    kp = p_slots.shape[1]
-    reached = jnp.stack([lookup(ext_ids[:, q], a_cols) for q in range(kp)], -1).reshape(rows, -1)
-    wanted = jnp.stack([lookup(patterns[:, j], p_slots) for j in range(patterns.shape[1])], 0)
-    order = jnp.arange(1, patterns.shape[1] + 1, dtype=jnp.int32)[:, None, None, None]
-    places = jnp.sum(jnp.where(reached[None, :, None, :] == wanted[..., None], order, 0), 0)
-    kq = reached.shape[1]
-    heads = jnp.arange(rows * kp, dtype=jnp.int32)
-    bits = jnp.arange(kq, dtype=jnp.int32)
-    end = rows * kp * 32 - 1
-    at = jnp.where(places > 0, heads.reshape(rows, kp, 1) * 32 + bits, end)
-    first = jnp.min(at, -1)
-    flat = first.reshape(-1)
-    beyond = jnp.min(jnp.where(heads[None, :] > heads[:, None], flat[None, :], end), -1)
-    follow = jnp.min(jnp.where(bits[None, :] > bits[:, None], at[:, :, None, :], end), -1)
-    follow = jnp.minimum(follow, beyond.reshape(rows, kp, 1))
-    words = follow * 512 + p_slots[..., None] * patterns.shape[1] + places - 1
-    words = jnp.pad(words, ((0, 0), (0, 0), (0, 32 - kq))).reshape(-1)
-    return jnp.where(jnp.arange(end + 1, dtype=jnp.int32) == end, jnp.min(flat) * 512, words)
-
-
 def per_device(a_blocks, p_blocks, a_cols, p_slots, touched, touch_cols, halo_rows):
     nrow = lax.axis_size("row")
-    nslab = lax.axis_size("slab")
     slab_at = lax.axis_index("slab")
     cap = touched.shape[2]
     slots = touched.shape[1] * cap
@@ -546,22 +599,17 @@
     sent_ids = coarse_ids[lists]
     depth = lists.shape[1]
     kp = p_slots.shape[1]
-    row_at = lax.axis_index("row")
     ids_out = jnp.pad(sent_ids.reshape(4, 1, depth * kp), ((0, 0), (0, 0), (0, 128 - depth * kp)))
-    halo, halo_ids = exchange_halo(halo_rows, p_blocks, ids_out)
-    outside = jnp.stack([slab_at == 0, slab_at == nslab - 1, row_at == 0, row_at == nrow - 1])
-    halo_ids = jnp.where(outside[:, None], -1, halo_ids[:, 0, : depth * kp]).reshape(4 * depth, kp)
+    columns = a_cols.T
+    halo, words = exchange_halo(halo_rows, coarse_ids.T, patterns, columns, p_slots.T, p_blocks, ids_out)
     halo = halo.reshape((4 * depth,) + halo.shape[2:])
-    ext_ids = jnp.concatenate([coarse_ids, halo_ids], 0)
-    words = find_matches(ext_ids, a_cols, p_slots, patterns)
     width = a_blocks.shape[1]
-    lists_in = (a_cols.reshape(-1), words)
     bases = (jnp.arange(slots, dtype=jnp.int32) // cap * NC + table) * kc
-    packed, ids = packed_partials(*lists_in, bases, a_blocks, p_blocks, halo, kc)
+    packed, ids = packed_partials(columns, words, bases, a_blocks, p_blocks, halo, kc)
     pieces, counts = reduce_parts(packed, ids.reshape(1, 1, IDS), NC * kc)
 
     def whole(unused):
-        partial = coarse_partials(*lists_in, a_blocks, p_blocks, halo, slots, kc)
+        partial = coarse_partials(columns, words, a_blocks, p_blocks, halo, slots, kc)
         parts = lax.all_to_all(partial.reshape(nrow, cap * width, kc * width), "row", 0, 0)
         owners = lax.all_to_all(touched[0], "row", 0, 0)
         return sum_parts(owners.reshape(-1), parts.reshape(slots, width, kc * width))

time: 101 us -> 96.3 us (0.953)
  the two profiles are of different devices: /device:TPU:16 before, /device:TPU:2 now
where the time goes in v7:
time: 96.3 us; the launch traced here: 96 us
  Pallas kernels  89 us (92%)
  local copies, waits for them, and re-layouts  3.87 us (4%)
  other arithmetic  2.3 us (2%)
    pallas_call x1, Pallas kernels, reduce_parts(): pl.pallas_call(reduce_kernel, out_shape=(jax.ShapeDtypeStruct((n, share,...  44 us
    pallas_call x1, Pallas kernels, packed_partials(): pl.pallas_call(packed_kernel, out_shape=(jax.ShapeDtypeStruct((width // 2...  27.9 us
    pallas_call x1, Pallas kernels, exchange_halo(): pl.pallas_call(halo_kernel, out_shape=(jax.ShapeDtypeStruct(shape, p_bloc...  15.8 us
    unnamed x12, local copies, waits for them, and re-layouts  2.92 us

profile of v7, /device:TPU:2, one launch (start us, length us, event | category | flops | bytes accessed | tf_op | source)
XLA Modules:
  0.0 96.0 jit_solution(15231495219272922194)
XLA Ops:
  0.0 0.8 copy.29
  0.8 0.1 reshape.61
  0.9 0.9 select_reduce_fusion
  1.8 0.7 fusion.3
  2.5 0.1 copy.31
  2.6 0.7 compare_select_fusion
  3.3 0.1 reshape.69
  3.4 0.6 gather_fusion
  3.9 0.1 reshape.63
  4.0 0.8 copy.30
  4.8 0.0 copy-start
  4.8 0.7 copy-done
  5.5 0.0 copy-start.1
  5.5 0.7 copy-done.1
  6.2 15.8 %exchange_halo.1 = (bf16[4,8,64,256]{3,2,1,0:T(8,128)(2,1)S(1)}, s32[128,128]{1,0:T(8,128)S(1)}) custom-call(s32[1,4,8]{2,1,0:T(4,128)S(1)} %copy-done.1, s32[4,64]{1,0:T(4,128)S(1)} %bitcast.16, s32[64,8]{1,0:T(8,128)S(1)} %bitcast.15, s32[7,64]{1,0:T(8,128)} %bitcast.22, s32[4,64]{1,0:T(4,128)S(1)} %bitcast.17, bf16[64,64,256]{2,1,0:T(8,128)(2,1)} %p_hbm.1, ...), custom_call_target="tpu_custom_call" | custom-call | tf_op jit(solution)/shard_map/exchange_halo/pallas_call | solution.py:292
  22.0 0.0 copy-start.2
  22.0 0.0 copy-start.3
  22.0 0.0 copy-start.4
  22.0 27.9 %packed_partials.1 = (bf16[32,128,128]{2,1,0:T(8,128)(2,1)S(1)}, s32[1,256]{1,0:T(1,128)S(1)}) custom-call(s32[7,64]{1,0:T(8,128)} %bitcast.23, s32[128,128]{1,0:T(8,128)S(1)} %get-tuple-element.33.words, s32[64]{0:T(128)S(1)} %fusion.7.bases, bf16[64,64,448]{2,1,0:T(8,128)(2,1)} %a_hbm.1, bf16[64,64,256]{2,1,0:T(8,128)(2,1)} %p_hbm.1, ...), custom_call_target="tpu_custom_call" | custom-call | tf_op jit(solution)/shard_map/packed_partials/pallas_call | solution.py:220
  50.0 44.0 %reduce_parts.1 = (bf16[32,32,128]{2,1,0:T(8,128)(2,1)S(1)}, s32[1,1]{1,0:T(1,128)}) custom-call(bf16[32,128,128]{2,1,0:T(8,128)(2,1)S(1)} %get-tuple-element.35.parts, s32[1,1,256]{2,1,0:T(1,128)S(1)} %bitcast.18), custom_call_target="tpu_custom_call" | custom-call | tf_op jit(solution)/shard_map/reduce_parts/pallas_call | solution.py:428
  94.7 0.0 copy-done.2
  94.7 0.0 copy-done.3
  94.7 0.0 copy-done.4
  94.7 1.2 %conditional.1 = (f32[4,64,512]{2,1,0:T(8,128)}) conditional(s32[]{:T(128)} %bitcast.11, bf16[32,32,128]{2,1,0:T(8,128)(2,1)S(1)} %get-tuple-element.38, (s32[1,32,2]{1,2,0:T(2,128)S(1)}, s32[7,64]{1,0:T(8,128)S(1)}, s32[128,128]{1,0:T(8,128)S(1)}, bf16[64,64,448]{2,1,0:T(8,128)(2,1)}, bf16[64,64,256]{2,1,0:T(8,128)(2,1)S(1)}, ...), branch_computations={%region_1.2_spmd, %region_2.3_spmd} | conditional | bytes 12617556 | solution.py:617
  94.7 1.2 %assemble.1 = f32[4,64,512]{2,1,0:T(8,128)} custom-call(bf16[32,32,128]{2,1,0:T(8,128)(2,1)S(1)} %pieces_ref), custom_call_target="tpu_custom_call" | custom-call | tf_op jit(solution)/shard_map/cond/branch_0_fun/assemble/pallas_call | solution.py:474
  (3 shorter events, 0.0 us)
Async XLA Ops:
  4.8 0.7 copy-start
  5.5 0.7 copy-start.1
  22.0 72.7 %copy-start.2 = (bf16[64,64,256]{2,1,0:T(8,128)(2,1)S(1)}, bf16[64,64,256]{2,1,0:T(8,128)(2,1)}, u32[]{:S(2)}) copy-start(bf16[64,64,256]{2,1,0:T(8,128)(2,1)} %p_hbm.1) | copy-start | bytes 6291460
  22.0 72.7 %copy-start.3 = (s32[64,7]{0,1:T(8,128)S(1)}, s32[64,7]{0,1:T(8,128)}, u32[]{:S(2)}) copy-start(s32[64,7]{0,1:T(8,128)} %param.11) | copy-start | bytes 5380
  22.0 72.7 %copy-start.4 = (s32[1,32,2]{1,2,0:T(2,128)S(1)}, s32[1,32,2]{1,2,0:T(2,128)}, u32[]{:S(2)}) copy-start(s32[1,32,2]{1,2,0:T(2,128)} %param.13) | copy-start | bytes 772

commit v8 on v7

--- a/solution.py
+++ b/solution.py
@@ -76,7 +76,7 @@
 def link_matches(cols_v, slots_v, own_ids, halo_ids, edges, patterns, at_v, follow_v, place_v):
     ka, rows = cols_v.shape
     kp = slots_v.shape[0]
-    nslots, kc = patterns.shape
+    _, cap, kc, owners = patterns.shape
     sides, depth = halo_ids.shape[0], rows // 8
     end = at_v.shape[0] * 128 - 1
     cols = cols_v[...]
@@ -92,9 +92,10 @@
             ]
     slots = slots_v[...]
     wanted = [jnp.full((kp, rows), -3, jnp.int32)] * kc
-    for t in range(nslots):
-        hit = slots == t
-        wanted = [jnp.where(hit, patterns[t, j], wanted[j]) for j in range(kc)]
+    for p in range(owners):
+        for c in range(cap):
+            hit = slots == p * cap + c
+            wanted = [jnp.where(hit, patterns[0, c, j, p], wanted[j]) for j in range(kc)]
     at_v[...] = jnp.full(at_v.shape, end, jnp.int32)
     follow_v[...] = jnp.full(follow_v.shape, end, jnp.int32)
     place_v[...] = jnp.zeros(place_v.shape, jnp.int32)
@@ -133,7 +134,7 @@
 
 
 def packed_kernel(
-    cols, words, bases, a_hbm, p_hbm, halo_hbm, out_ref, ids_ref, a_v, ext_v, g_v, pt_v, acc, items, index, sems
+    cols, words, table, a_hbm, p_hbm, halo_hbm, out_ref, ids_ref, a_v, ext_v, g_v, pt_v, acc, items, index, bases, sems
 ):
     rows, width, span = a_v.shape
     ka = span // width
@@ -144,6 +145,10 @@
     copies = load_operands(a_hbm, p_hbm, halo_hbm, a_v, ext_v, sems)
     for copy in copies:
         copy.start()
+
+    for p in range(table.shape[2]):
+        for c in range(table.shape[1]):
+            bases[p * table.shape[1] + c] = (p * NC + table[0, c, p]) * kc
 
     def unset(n, unused):
         for u in range(8):
@@ -209,11 +214,12 @@
     lax.fori_loop(full, BLOCKS // 16, empty, 0)
 
 
-def packed_partials(cols, words, bases, a_blocks, p_blocks, halo, kc):
+def packed_partials(cols, words, table, a_blocks, p_blocks, halo, kc):
     rows, width, span = a_blocks.shape
     kp = p_blocks.shape[2] // width
     ka = span // width
     extended = rows + halo.shape[0]
+    nslots = table.shape[1] * table.shape[2]
     smem = pl.BlockSpec(memory_space=pltpu.SMEM)
     vmem = pl.BlockSpec(memory_space=pltpu.VMEM)
     hbm = pl.BlockSpec(memory_space=pl.ANY)
@@ -232,17 +238,18 @@
             pltpu.VMEM((rows * kp, width, width), jnp.bfloat16),
             pltpu.VMEM(((BLOCKS + 16) * width, 2 * width), jnp.float32),
             pltpu.SMEM((rows * kp * ka * kp + UNROLL,), jnp.int32),
-            pltpu.SMEM((bases.shape[0] * kc,), jnp.int32),
+            pltpu.SMEM((nslots * kc,), jnp.int32),
+            pltpu.SMEM((nslots,), jnp.int32),
             pltpu.SemaphoreType.DMA((3,)),
         ],
         compiler_params=pltpu.CompilerParams(vmem_limit_bytes=48 * 2**20),
         name="packed_partials",
-    )(cols, words, bases, a_blocks, p_blocks, halo)
+    )(cols, words, table, a_blocks, p_blocks, halo)
 
 
 def halo_kernel(
-    rows, own_ids, patterns, cols_v, slots_v, p_ref, ids, out_blocks, words, blocks, came_ids, halo_ids, follow_v, place_v,
-    here_sem, send_sem, take_sem
+    rows, table, patterns, cols_v, slots_v, p_ref, out_blocks, words, blocks, own_v, own_ids, ids, came_ids, halo_ids,
+    follow_v, place_v, here_sem, send_sem, take_sem
 ):
     barrier = pltpu.get_barrier_semaphore()
     routes = []
@@ -269,9 +276,30 @@
             device_id_type=pl.DeviceIdType.MESH,
         )
 
-    for z in range(2):
-        for slot, to, chosen in routes:
-            send(z, slot, to, chosen).start()
+    for slot, to, chosen in routes:
+        send(1, slot, to, chosen).start()
+    slots = slots_v[...]
+    kp, cap = slots.shape[0], table.shape[1]
+    local = jnp.zeros_like(slots)
+    for p in range(table.shape[2]):
+        for c in range(cap):
+            local = jnp.where(slots == p * cap + c, table[0, c, p], local)
+    owner = lax.axis_index("slab") * lax.axis_size("row") + lax.div(slots, cap)
+    own_v[...] = jnp.zeros(own_v.shape, jnp.int32)
+    own_v[:kp, : slots.shape[1]] = owner * NC + local
+    here = pltpu.make_async_copy(own_v, own_ids, here_sem.at[1])
+    here.start()
+    here.wait()
+    lane = lax.broadcasted_iota(jnp.int32, (1, 128), 1)
+    for x in range(rows.shape[1]):
+        listed = jnp.zeros((1, 128), jnp.int32)
+        for d in range(rows.shape[2]):
+            at = rows[0, x, d]
+            for m in range(kp):
+                listed = jnp.where(lane == d * kp + m, own_ids[m, at], listed)
+        ids[x] = listed
+    for slot, to, chosen in routes:
+        send(0, slot, to, chosen).start()
     for slot, to, chosen in routes:
         send(0, slot, to, chosen).wait()
     here = pltpu.make_async_copy(came_ids, halo_ids, here_sem.at[0])
@@ -282,7 +310,7 @@
         send(1, slot, to, chosen).wait()
 
 
-def exchange_halo(rows, own_ids, patterns, cols, slots, p_blocks, ids):
+def exchange_halo(rows, table, patterns, cols, slots, p_blocks):
     vmem = pl.BlockSpec(memory_space=pltpu.VMEM)
     smem = pl.BlockSpec(memory_space=pltpu.SMEM)
     hbm = pl.BlockSpec(memory_space=pl.ANY)
@@ -292,21 +320,24 @@
     return pl.pallas_call(
         halo_kernel,
         out_shape=(jax.ShapeDtypeStruct(shape, p_blocks.dtype), jax.ShapeDtypeStruct(linked, jnp.int32)),
-        in_specs=[smem, smem, smem, vmem, vmem, vmem, hbm],
+        in_specs=[smem, smem, smem, vmem, vmem, vmem],
         out_specs=(hbm, vmem),
         scratch_shapes=[
             pltpu.VMEM(shape, p_blocks.dtype),
-            pltpu.VMEM(ids.shape, jnp.int32),
-            pltpu.SMEM(ids.shape, jnp.int32),
+            pltpu.VMEM((8, 128), jnp.int32),
+            pltpu.SMEM((8, 128), jnp.int32),
+            pltpu.VMEM((4, 1, 128), jnp.int32),
+            pltpu.VMEM((4, 1, 128), jnp.int32),
+            pltpu.SMEM((4, 1, 128), jnp.int32),
             pltpu.VMEM(linked, jnp.int32),
             pltpu.VMEM(linked, jnp.int32),
-            pltpu.SemaphoreType.DMA((1,)),
+            pltpu.SemaphoreType.DMA((2,)),
             pltpu.SemaphoreType.DMA((2, 4)),
             pltpu.SemaphoreType.DMA((2, 4)),
         ],
         compiler_params=pltpu.CompilerParams(collective_id=1, has_side_effects=True, vmem_limit_bytes=32 * 2**20),
         name="exchange_halo",
-    )(rows, own_ids, patterns, cols, slots, p_blocks, ids)
+    )(rows, table, patterns, cols, slots, p_blocks)
 
 
 def reduce_kernel(
@@ -581,31 +612,18 @@
     )(ids, parts)
 
 
-def lookup(table, index):
-    hot = index[..., None] == jnp.arange(table.shape[0], dtype=jnp.int32)
-    return jnp.sum(jnp.where(hot, table, 0), axis=-1)
-
-
 def per_device(a_blocks, p_blocks, a_cols, p_slots, touched, touch_cols, halo_rows):
     nrow = lax.axis_size("row")
-    slab_at = lax.axis_index("slab")
     cap = touched.shape[2]
     slots = touched.shape[1] * cap
-    table = touched.reshape(slots)
-    patterns = touch_cols.reshape(slots, touch_cols.shape[3])
-    kc = patterns.shape[1]
-    coarse_ids = (slab_at * nrow + p_slots // cap) * NC + lookup(table, p_slots)
-    lists = halo_rows[0]
-    sent_ids = coarse_ids[lists]
-    depth = lists.shape[1]
-    kp = p_slots.shape[1]
-    ids_out = jnp.pad(sent_ids.reshape(4, 1, depth * kp), ((0, 0), (0, 0), (0, 128 - depth * kp)))
+    kc = touch_cols.shape[3]
+    table = touched.transpose(0, 2, 1)
+    patterns = touch_cols.transpose(0, 2, 3, 1)
     columns = a_cols.T
-    halo, words = exchange_halo(halo_rows, coarse_ids.T, patterns, columns, p_slots.T, p_blocks, ids_out)
-    halo = halo.reshape((4 * depth,) + halo.shape[2:])
+    halo, words = exchange_halo(halo_rows, table, patterns, columns, p_slots.T, p_blocks)
+    halo = halo.reshape((-1,) + halo.shape[2:])
     width = a_blocks.shape[1]
-    bases = (jnp.arange(slots, dtype=jnp.int32) // cap * NC + table) * kc
-    packed, ids = packed_partials(columns, words, bases, a_blocks, p_blocks, halo, kc)
+    packed, ids = packed_partials(columns, words, table, a_blocks, p_blocks, halo, kc)
     pieces, counts = reduce_parts(packed, ids.reshape(1, 1, IDS), NC * kc)
 
     def whole(unused):

time: 96.3 us -> 93.8 us (0.974)
  the two profiles are of different devices: /device:TPU:2 before, /device:TPU:8 now
where the time goes in v8:
time: 93.8 us; the launch traced here: 93.6 us
  Pallas kernels  90.8 us (97%)
  local copies, waits for them, and re-layouts  2.08 us (2%)
    pallas_call x1, Pallas kernels, reduce_parts(): pl.pallas_call(reduce_kernel, out_shape=(jax.ShapeDtypeStruct((n, share,...  48.4 us
    pallas_call x1, Pallas kernels, packed_partials(): pl.pallas_call(packed_kernel, out_shape=(jax.ShapeDtypeStruct((width // 2...  21.5 us
    pallas_call x1, Pallas kernels, exchange_halo(): pl.pallas_call(halo_kernel, out_shape=(jax.ShapeDtypeStruct(shape, p_bloc...  19.6 us
    unnamed x12, local copies, waits for them, and re-layouts  2.08 us

profile of v8, /device:TPU:8, one launch (start us, length us, event | category | flops | bytes accessed | tf_op | source)
XLA Modules:
  0.0 93.6 jit_solution(11398681998336611246)
XLA Ops:
  0.0 0.0 copy-start
  0.0 0.7 copy-done
  0.7 0.0 copy-start.1
  0.7 0.7 copy-done.1
  1.4 0.0 copy-start.2
  1.4 0.7 copy-done.2
  2.1 19.6 %exchange_halo.1 = (bf16[4,8,64,256]{3,2,1,0:T(8,128)(2,1)S(1)}, s32[128,128]{1,0:T(8,128)S(1)}) custom-call(s32[1,4,8]{2,1,0:T(4,128)S(1)} %copy-done.1, s32[1,2,32]{2,1,0:T(2,128)} %bitcast.19, s32[1,2,8,32]{3,2,1,0:T(8,128)S(1)} %bitcast.10, s32[7,64]{1,0:T(8,128)} %bitcast.16, s32[4,64]{1,0:T(4,128)S(1)} %bitcast.11, bf16[64,64,256]{2,1,0:T(8,128)(2,1)} %p_hbm.1), custom_call_target="tpu_custom_call" | custom-call | tf_op jit(solution)/shard_map/exchange_halo/pallas_call | solution.py:320
  21.7 0.0 copy-start.3
  21.7 0.0 copy-start.4
  21.7 0.0 copy-start.5
  21.7 21.5 %packed_partials.1 = (bf16[32,128,128]{2,1,0:T(8,128)(2,1)S(1)}, s32[1,256]{1,0:T(1,128)S(1)}) custom-call(s32[7,64]{1,0:T(8,128)} %bitcast.17, s32[128,128]{1,0:T(8,128)S(1)} %get-tuple-element.33.words, s32[1,2,32]{2,1,0:T(2,128)} %bitcast.20, bf16[64,64,448]{2,1,0:T(8,128)(2,1)} %a_hbm.1, bf16[64,64,256]{2,1,0:T(8,128)(2,1)} %p_hbm.1, ...), custom_call_target="tpu_custom_call" | custom-call | tf_op jit(solution)/shard_map/packed_partials/pallas_call | solution.py:226
  43.2 48.4 %reduce_parts.1 = (bf16[32,32,128]{2,1,0:T(8,128)(2,1)S(1)}, s32[1,1]{1,0:T(1,128)}) custom-call(bf16[32,128,128]{2,1,0:T(8,128)(2,1)S(1)} %get-tuple-element.35.parts, s32[1,1,256]{2,1,0:T(1,128)S(1)} %bitcast.12), custom_call_target="tpu_custom_call" | custom-call | tf_op jit(solution)/shard_map/reduce_parts/pallas_call | solution.py:459
  92.3 0.0 copy-done.3
  92.3 0.0 copy-done.4
  92.3 0.0 copy-done.5
  92.3 1.2 %conditional.1 = (f32[4,64,512]{2,1,0:T(8,128)}) conditional(s32[]{:T(128)} %bitcast.9, bf16[32,32,128]{2,1,0:T(8,128)(2,1)S(1)} %get-tuple-element.38, (s32[1,32,2]{1,2,0:T(2,128)S(1)}, s32[7,64]{1,0:T(8,128)S(1)}, s32[128,128]{1,0:T(8,128)S(1)}, bf16[64,64,448]{2,1,0:T(8,128)(2,1)}, bf16[64,64,256]{2,1,0:T(8,128)(2,1)S(1)}, ...), branch_computations={%region_0.0_spmd, %region_1.0_spmd} | conditional | bytes 12617556 | solution.py:635
  92.3 1.2 %assemble.1 = f32[4,64,512]{2,1,0:T(8,128)} custom-call(bf16[32,32,128]{2,1,0:T(8,128)(2,1)S(1)} %pieces_ref), custom_call_target="tpu_custom_call" | custom-call | tf_op jit(solution)/shard_map/cond/branch_0_fun/assemble/pallas_call | solution.py:505
Async XLA Ops:
  0.0 0.7 copy-start
  0.7 0.7 copy-start.1
  1.4 0.7 copy-start.2
  21.7 70.6 %copy-start.3 = (bf16[64,64,256]{2,1,0:T(8,128)(2,1)S(1)}, bf16[64,64,256]{2,1,0:T(8,128)(2,1)}, u32[]{:S(2)}) copy-start(bf16[64,64,256]{2,1,0:T(8,128)(2,1)} %p_hbm.1) | copy-start | bytes 6291460
  21.7 70.6 %copy-start.4 = (s32[64,7]{0,1:T(8,128)S(1)}, s32[64,7]{0,1:T(8,128)}, u32[]{:S(2)}) copy-start(s32[64,7]{0,1:T(8,128)} %param.11) | copy-start | bytes 5380
  21.7 70.6 %copy-start.5 = (s32[1,32,2]{1,2,0:T(2,128)S(1)}, s32[1,32,2]{1,2,0:T(2,128)}, u32[]{:S(2)}) copy-start(s32[1,32,2]{1,2,0:T(2,128)} %param.13) | copy-start | bytes 772

commit v9 on v8

--- a/solution.py
+++ b/solution.py
@@ -164,15 +164,15 @@
 
     lax.fori_loop(0, ids_ref.shape[1] // 8, no_id, 0)
 
-    last = words.shape[0] * 128 - 1
-    first = words[words.shape[0] - 1, 0]
+    last = words.shape[0] - 1
+    first = words[words.shape[0] - 128]
 
     def more(state):
         return state[0] != last
 
     def take(state):
         at, count, blocks = state
-        word = words[lax.shift_right_logical(at, 7), at & 127]
+        word = words[at]
         place = word & 511
         old = index[place]
         fresh = old < 0
@@ -180,7 +180,7 @@
         index[place] = block
         kept = jnp.minimum(block, BLOCKS)
         ids_ref[0, kept] = bases[lax.shift_right_logical(place, 3)] + (place & 7)
-        items[count] = words[lax.shift_right_logical(at, 7), (at & 127) + rows] + kept
+        items[count] = words[at + rows] + kept
         return (lax.shift_right_logical(word, 9), count + 1, blocks + fresh.astype(jnp.int32))
 
     _, count, blocks = lax.while_loop(more, take, (first, 0, 0))
@@ -335,7 +335,7 @@
             pltpu.SemaphoreType.DMA((2, 4)),
             pltpu.SemaphoreType.DMA((2, 4)),
         ],
-        compiler_params=pltpu.CompilerParams(collective_id=1, has_side_effects=True, vmem_limit_bytes=32 * 2**20),
+        compiler_params=pltpu.CompilerParams(collective_id=1, has_side_effects=True, vmem_limit_bytes=60 * 2**20),
         name="exchange_halo",
     )(rows, table, patterns, cols, slots, p_blocks)
 
@@ -526,16 +526,16 @@
         copy.start()
     clear_rows(acc, width, 0, acc.shape[0] // width)
 
-    last = words.shape[0] * 128 - 1
-    first = words[words.shape[0] - 1, 0]
+    last = words.shape[0] - 1
+    first = words[words.shape[0] - 128]
 
     def more(state):
         return state[0] != last
 
     def take(state):
         at, count = state
-        word = words[lax.shift_right_logical(at, 7), at & 127]
-        items[count] = words[lax.shift_right_logical(at, 7), (at & 127) + rows] + (word & 511)
+        word = words[at]
+        items[count] = words[at + rows] + (word & 511)
         return (lax.shift_right_logical(word, 9), count + 1)
 
     _, count = lax.while_loop(more, take, (first, 0))
@@ -622,6 +622,7 @@
     columns = a_cols.T
     halo, words = exchange_halo(halo_rows, table, patterns, columns, p_slots.T, p_blocks)
     halo = halo.reshape((-1,) + halo.shape[2:])
+    words = words.reshape(-1)
     width = a_blocks.shape[1]
     packed, ids = packed_partials(columns, words, table, a_blocks, p_blocks, halo, kc)
     pieces, counts = reduce_parts(packed, ids.reshape(1, 1, IDS), NC * kc)

time: 93.8 us -> 91.9 us (0.980)
  the two profiles are of different devices: /device:TPU:8 before, /device:TPU:16 now
where the time goes in v9:
time: 91.9 us; the launch traced here: 90.8 us
  Pallas kernels  90 us (98%)
    pallas_call x1, Pallas kernels, reduce_parts(): pl.pallas_call(reduce_kernel, out_shape=(jax.ShapeDtypeStruct((n, share,...  49.7 us
    pallas_call x1, Pallas kernels, packed_partials(): pl.pallas_call(packed_kernel, out_shape=(jax.ShapeDtypeStruct((width // 2...  19.7 us
    pallas_call x1, Pallas kernels, exchange_halo(): pl.pallas_call(halo_kernel, out_shape=(jax.ShapeDtypeStruct(shape, p_bloc...  19.4 us

profile of v9, /device:TPU:16, one launch (start us, length us, event | category | flops | bytes accessed | tf_op | source)
XLA Modules:
  0.0 90.8 jit_solution(524432853071960045)
XLA Ops:
  0.0 19.4 %exchange_halo.1 = (bf16[4,8,64,256]{3,2,1,0:T(8,128)(2,1)S(1)}, s32[128,128]{1,0:T(8,128)S(1)}) custom-call(s32[1,4,8]{2,1,0:T(4,128)} %rows.1, s32[1,2,32]{2,1,0:T(2,128)} %bitcast.20, s32[1,2,8,32]{3,2,1,0:T(8,128)} %bitcast.23, s32[7,64]{1,0:T(8,128)} %bitcast.17, s32[4,64]{1,0:T(4,128)} %bitcast.24, bf16[64,64,256]{2,1,0:T(8,128)(2,1)} %p_hbm.1), custom_call_target="tpu_custom_call" | custom-call | tf_op jit(solution)/shard_map/exchange_halo/pallas_call | solution.py:320
  19.4 0.0 copy-start
  19.4 0.0 copy-start.1
  19.4 0.0 copy-start.2
  19.4 19.7 %packed_partials.1 = (bf16[32,128,128]{2,1,0:T(8,128)(2,1)S(1)}, s32[1,256]{1,0:T(1,128)S(1)}) custom-call(s32[7,64]{1,0:T(8,128)} %bitcast.18, s32[16384]{0:T(1024)S(1)} %bitcast.15, s32[1,2,32]{2,1,0:T(2,128)} %bitcast.21, bf16[64,64,448]{2,1,0:T(8,128)(2,1)} %a_hbm.1, bf16[64,64,256]{2,1,0:T(8,128)(2,1)} %p_hbm.1, bf16[32,64,256]{2,1,0:T(8,128)(2,1)S(1)} %bitcast.13), custom_call_target="tpu_custom_call" | custom-call | tf_op jit(solution)/shard_map/packed_partials/pallas_call | solution.py:226
  39.2 49.7 %reduce_parts.1 = (bf16[32,32,128]{2,1,0:T(8,128)(2,1)S(1)}, s32[1,1]{1,0:T(1,128)}) custom-call(bf16[32,128,128]{2,1,0:T(8,128)(2,1)S(1)} %get-tuple-element.35.parts, s32[1,1,256]{2,1,0:T(1,128)S(1)} %bitcast.11), custom_call_target="tpu_custom_call" | custom-call | tf_op jit(solution)/shard_map/reduce_parts/pallas_call | solution.py:459
  89.5 0.0 copy-done
  89.5 0.0 copy-done.1
  89.5 0.0 copy-done.2
  89.5 1.2 %conditional.1 = (f32[4,64,512]{2,1,0:T(8,128)}) conditional(s32[]{:T(128)} %bitcast.10, bf16[32,32,128]{2,1,0:T(8,128)(2,1)S(1)} %get-tuple-element.38, (s32[1,32,2]{1,2,0:T(2,128)S(1)}, s32[7,64]{1,0:T(8,128)S(1)}, s32[16384]{0:T(1024)S(1)}, bf16[64,64,448]{2,1,0:T(8,128)(2,1)}, bf16[64,64,256]{2,1,0:T(8,128)(2,1)S(1)}, ...), branch_computations={%region_0.0_spmd, %region_1.0_spmd} | conditional | bytes 12617556 | solution.py:636
  89.5 1.2 %assemble.1 = f32[4,64,512]{2,1,0:T(8,128)} custom-call(bf16[32,32,128]{2,1,0:T(8,128)(2,1)S(1)} %pieces_ref), custom_call_target="tpu_custom_call" | custom-call | tf_op jit(solution)/shard_map/cond/branch_0_fun/assemble/pallas_call | solution.py:505
Async XLA Ops:
  19.4 70.1 %copy-start = (bf16[64,64,256]{2,1,0:T(8,128)(2,1)S(1)}, bf16[64,64,256]{2,1,0:T(8,128)(2,1)}, u32[]{:S(2)}) copy-start(bf16[64,64,256]{2,1,0:T(8,128)(2,1)} %p_hbm.1) | copy-start | bytes 6291460
  19.4 70.1 %copy-start.1 = (s32[64,7]{0,1:T(8,128)S(1)}, s32[64,7]{0,1:T(8,128)}, u32[]{:S(2)}) copy-start(s32[64,7]{0,1:T(8,128)} %param.11) | copy-start | bytes 5380
  19.4 70.1 %copy-start.2 = (s32[1,32,2]{1,2,0:T(2,128)S(1)}, s32[1,32,2]{1,2,0:T(2,128)}, u32[]{:S(2)}) copy-start(s32[1,32,2]{1,2,0:T(2,128)} %param.13) | copy-start | bytes 772

commit v10 on v9

--- a/solution.py
+++ b/solution.py
@@ -42,7 +42,7 @@
                 g_v[(i * ka + k) * pairs + h] = value[:, h * pair : (h + 1) * pair]
         return unused
 
-    lax.fori_loop(0, rows, products, 0, unroll=8)
+    lax.fori_loop(0, rows, products, 0, unroll=16)
 
 
 def add_items(count, items, pt_v, g_v, acc, width, ka, kp):

time: 91.9 us -> 91.3 us (level)
    pallas_call x1, Pallas kernels: 49.7 us -> 45.8 us  [reduce_parts(): pl.pallas_call(reduce_kernel, out_shape=(jax.ShapeDtypeStruct((n, share,...]
    pallas_call x1, Pallas kernels: 19.7 us -> 22.8 us  [packed_partials(): pl.pallas_call(packed_kernel, out_shape=(jax.ShapeDtypeStruct((width // 2...]
where the time goes in v10:
time: 91.3 us; the launch traced here: 89.9 us
  Pallas kernels  89.1 us (98%)
    pallas_call x1, Pallas kernels, reduce_parts(): pl.pallas_call(reduce_kernel, out_shape=(jax.ShapeDtypeStruct((n, share,...  45.8 us
    pallas_call x1, Pallas kernels, packed_partials(): pl.pallas_call(packed_kernel, out_shape=(jax.ShapeDtypeStruct((width // 2...  22.8 us
    pallas_call x1, Pallas kernels, exchange_halo(): pl.pallas_call(halo_kernel, out_shape=(jax.ShapeDtypeStruct(shape, p_bloc...  19.4 us

profile of v10, /device:TPU:16, one launch (start us, length us, event | category | flops | bytes accessed | tf_op | source)
XLA Modules:
  0.0 89.9 jit_solution(4501519678194657352)
XLA Ops:
  0.0 19.4 %exchange_halo.1 = (bf16[4,8,64,256]{3,2,1,0:T(8,128)(2,1)S(1)}, s32[128,128]{1,0:T(8,128)S(1)}) custom-call(s32[1,4,8]{2,1,0:T(4,128)} %rows.1, s32[1,2,32]{2,1,0:T(2,128)} %bitcast.20, s32[1,2,8,32]{3,2,1,0:T(8,128)} %bitcast.23, s32[7,64]{1,0:T(8,128)} %bitcast.17, s32[4,64]{1,0:T(4,128)} %bitcast.24, bf16[64,64,256]{2,1,0:T(8,128)(2,1)} %p_hbm.1), custom_call_target="tpu_custom_call" | custom-call | tf_op jit(solution)/shard_map/exchange_halo/pallas_call | solution.py:320
  19.4 0.0 copy-start
  19.4 0.0 copy-start.1
  19.4 0.0 copy-start.2
  19.4 22.8 %packed_partials.1 = (bf16[32,128,128]{2,1,0:T(8,128)(2,1)S(1)}, s32[1,256]{1,0:T(1,128)S(1)}) custom-call(s32[7,64]{1,0:T(8,128)} %bitcast.18, s32[16384]{0:T(1024)S(1)} %bitcast.15, s32[1,2,32]{2,1,0:T(2,128)} %bitcast.21, bf16[64,64,448]{2,1,0:T(8,128)(2,1)} %a_hbm.1, bf16[64,64,256]{2,1,0:T(8,128)(2,1)} %p_hbm.1, bf16[32,64,256]{2,1,0:T(8,128)(2,1)S(1)} %bitcast.13), custom_call_target="tpu_custom_call" | custom-call | tf_op jit(solution)/shard_map/packed_partials/pallas_call | solution.py:226
  42.2 45.8 %reduce_parts.1 = (bf16[32,32,128]{2,1,0:T(8,128)(2,1)S(1)}, s32[1,1]{1,0:T(1,128)}) custom-call(bf16[32,128,128]{2,1,0:T(8,128)(2,1)S(1)} %get-tuple-element.35.parts, s32[1,1,256]{2,1,0:T(1,128)S(1)} %bitcast.11), custom_call_target="tpu_custom_call" | custom-call | tf_op jit(solution)/shard_map/reduce_parts/pallas_call | solution.py:459
  88.6 0.0 copy-done
  88.6 0.0 copy-done.1
  88.6 0.0 copy-done.2
  88.6 1.2 %conditional.1 = (f32[4,64,512]{2,1,0:T(8,128)}) conditional(s32[]{:T(128)} %bitcast.10, bf16[32,32,128]{2,1,0:T(8,128)(2,1)S(1)} %get-tuple-element.38, (s32[1,32,2]{1,2,0:T(2,128)S(1)}, s32[7,64]{1,0:T(8,128)S(1)}, s32[16384]{0:T(1024)S(1)}, bf16[64,64,448]{2,1,0:T(8,128)(2,1)}, bf16[64,64,256]{2,1,0:T(8,128)(2,1)S(1)}, ...), branch_computations={%region_0.0_spmd, %region_1.0_spmd} | conditional | bytes 12617556 | solution.py:636
  88.6 1.2 %assemble.1 = f32[4,64,512]{2,1,0:T(8,128)} custom-call(bf16[32,32,128]{2,1,0:T(8,128)(2,1)S(1)} %pieces_ref), custom_call_target="tpu_custom_call" | custom-call | tf_op jit(solution)/shard_map/cond/branch_0_fun/assemble/pallas_call | solution.py:505
Async XLA Ops:
  19.4 69.2 %copy-start = (bf16[64,64,256]{2,1,0:T(8,128)(2,1)S(1)}, bf16[64,64,256]{2,1,0:T(8,128)(2,1)}, u32[]{:S(2)}) copy-start(bf16[64,64,256]{2,1,0:T(8,128)(2,1)} %p_hbm.1) | copy-start | bytes 6291460
  19.4 69.2 %copy-start.1 = (s32[64,7]{0,1:T(8,128)S(1)}, s32[64,7]{0,1:T(8,128)}, u32[]{:S(2)}) copy-start(s32[64,7]{0,1:T(8,128)} %param.11) | copy-start | bytes 5380
  19.4 69.2 %copy-start.2 = (s32[1,32,2]{1,2,0:T(2,128)S(1)}, s32[1,32,2]{1,2,0:T(2,128)}, u32[]{:S(2)}) copy-start(s32[1,32,2]{1,2,0:T(2,128)} %param.13) | copy-start | bytes 772
